TPU v7x, 32 devices: a whole 2x2x4 slice. The times are simulated.
32 devices in a mesh: row: 4 (over y, x), col: 8 (over z, core).
Axes of the slice: x: 2, y: 2, z: 4, core: 2. Of those that a mesh axis runs over, the one named last changes fastest.
Arguments:
- tokens: bfloat16 [64, 12288], P('col', 'row'), may hold values from -6 to 6
- cotangent: bfloat16 [64, 12288], P('col', 'row'), may hold values from -6 to 6
- w1_mask: int32 [96, 384], P('row', 'col'), may hold values from 0 to 1, as said below
- w1_blocks: bfloat16 [4, 8, 288, 128, 128], P('row', 'col'), may hold values from -0.109375 to 0.109375
- bias: bfloat16 [49152], P('col'), may hold values from -4 to 4
- w2_mask: int32 [384, 96], P('col', 'row'), may hold values from 0 to 1, as said below
- w2_blocks: bfloat16 [4, 8, 288, 128, 128], P('row', 'col'), may hold values from -0.0546875 to 0.0546875
Outputs:
- out: bfloat16 [64, 12288], P('col', 'row')
- tokens_grad: bfloat16 [64, 12288], P('col', 'row')
- w1_grad: float32 [4, 8, 288, 128, 128], P('row', 'col')
- w2_grad: float32 [4, 8, 288, 128, 128], P('row', 'col')
- bias_grad: float32 [49152], P('col')
Inputs may be any that keep to these rules, and one draw needn't show every extreme that they name: `w1_mask`: in every block row, each aligned group of 8 blocks along the columns holds exactly two ones. One device's tile of 24 x 48 blocks holds at most 288 ones, and in every draw some device's tile holds exactly 288. `w2_mask`: in every block row, each aligned group of 8 blocks along the columns holds exactly two ones. One device's tile of 48 x 24 blocks holds at most 288 ones, and in every draw some device's tile holds exactly 288.
All inputs are finite; a program needn't handle non-finite values.
Results may differ from a plain program's by a relative error of at most 0.005.
Values may be sent and summed in bfloat16 or wider, within the bound.
No kernel may reach another device: no remote copies, remote signals or barrier semaphores. Data moves between devices by JAX's collectives and lax.ppermute only.
A program may use at most 128 MiB of HBM per device.

v0:
```python
import math

import jax
import jax.numpy as jnp
from jax import lax
from jax.sharding import PartitionSpec as P

BLK = 128


slope_const = math.sqrt(2.0 / math.pi)


def gelu_value(values):
    inner = slope_const * (values + 0.044715 * values * values * values)
    return 0.5 * values * (1.0 + jnp.tanh(inner))


def gelu_slope(values):
    inner = slope_const * (values + 0.044715 * values * values * values)
    tangent = jnp.tanh(inner)
    return 0.5 * (1.0 + tangent) + 0.5 * values * (1.0 - tangent * tangent) * slope_const * (
        1.0 + 3.0 * 0.044715 * values * values
    )


def slot_layout(mask_tile, capacity):
    col_count = mask_tile.shape[1]
    flat = mask_tile.reshape(-1)
    order = jnp.argsort(1 - flat, stable=True)[:capacity]
    live_slot = jnp.arange(capacity, dtype=jnp.int32) < jnp.sum(flat)
    return (order // col_count, order % col_count, live_slot)


def sparse_apply(inputs, blocks, source, target, live_slot, outputs, flipped):
    row_count = inputs.shape[0]
    block_width = blocks.shape[1]
    pieces = inputs.reshape(row_count, -1, block_width)
    picked = jnp.take(pieces, source, axis=1)
    pattern = "tkb,kcb->ktc" if flipped else "tkb,kbc->ktc"
    products = jnp.einsum(pattern, picked, blocks, preferred_element_type=jnp.float32)
    placement_table = (
        (target[:, None] == jnp.arange(outputs, dtype=jnp.int32)[None, :]) & live_slot[:, None]
    ).astype(jnp.float32)
    summed = jnp.einsum(
        "ktc,ko->toc",
        products,
        placement_table,
        precision=lax.Precision.HIGHEST,
        preferred_element_type=jnp.float32,
    )
    return summed.reshape(row_count, outputs * block_width)


def block_grads(left, right, left_index, right_index, live_slot):
    row_count = left.shape[0]
    block_width = BLK
    left_picked = jnp.take(left.reshape(row_count, -1, block_width), left_index, axis=1)
    right_picked = jnp.take(right.reshape(row_count, -1, block_width), right_index, axis=1)
    grads = jnp.einsum(
        "tkb,tkc->kbc", left_picked, right_picked, preferred_element_type=jnp.float32
    )
    return grads * live_slot[:, None, None].astype(jnp.float32)


def local(tokens, cotangent, w1_mask, w1_blocks, bias, w2_mask, w2_blocks):
    full_tokens, full_cotangent = (
        lax.all_gather(tokens, "col", axis=0, tiled=True),
        lax.all_gather(cotangent, "col", axis=0, tiled=True),
    )
    first_blocks = w1_blocks[0, 0]
    second_blocks = w2_blocks[0, 0]
    w1_rows, w1_cols, w1_live = slot_layout(w1_mask, first_blocks.shape[0])
    w2_rows, w2_cols, w2_live = slot_layout(w2_mask, second_blocks.shape[0])
    model_blocks = w1_mask.shape[0]
    hidden_blocks = w1_mask.shape[1]
    bias_wide = bias.astype(jnp.float32)
    rows_part = full_tokens
    hidden = (
        lax.psum_scatter(
            sparse_apply(rows_part, first_blocks, w1_rows, w1_cols, w1_live, hidden_blocks, False),
            "row",
            scatter_dimension=0,
            tiled=True,
        )
        + bias_wide
    )
    activated = lax.all_gather(gelu_value(hidden).astype(jnp.bfloat16), "row", axis=0, tiled=True)
    out_terms = sparse_apply(
        activated, second_blocks, w2_rows, w2_cols, w2_live, model_blocks, False
    )
    rows_part = full_cotangent
    grad_act = lax.psum_scatter(
        sparse_apply(rows_part, second_blocks, w2_cols, w2_rows, w2_live, hidden_blocks, True),
        "row",
        scatter_dimension=0,
        tiled=True,
    )
    grad_hidden = lax.all_gather(
        (grad_act * gelu_slope(hidden)).astype(jnp.bfloat16), "row", axis=0, tiled=True
    )
    w2_grad = block_grads(activated, full_cotangent, w2_rows, w2_cols, w2_live)
    w1_grad = block_grads(full_tokens, grad_hidden, w1_rows, w1_cols, w1_live)
    bias_grad = jnp.sum(grad_hidden, axis=0, dtype=jnp.float32)
    grad_terms = sparse_apply(
        grad_hidden, first_blocks, w1_cols, w1_rows, w1_live, model_blocks, True
    )
    mixed, input_grad = (
        lax.psum_scatter(out_terms, "col", scatter_dimension=0, tiled=True),
        lax.psum_scatter(grad_terms, "col", scatter_dimension=0, tiled=True),
    )
    return (
        mixed.astype(jnp.bfloat16),
        input_grad.astype(jnp.bfloat16),
        w1_grad[None, None],
        w2_grad[None, None],
        bias_grad,
    )


def solution(mesh):
    return jax.shard_map(
        local,
        mesh=mesh,
        in_specs=(
            P("col", "row"),
            P("col", "row"),
            P("row", "col"),
            P("row", "col", None, None, None),
            P("col"),
            P("col", "row"),
            P("row", "col", None, None, None),
        ),
        out_specs=(
            P("col", "row"),
            P("col", "row"),
            P("row", "col", None, None, None),
            P("row", "col", None, None, None),
            P("col"),
        ),
        check_vma=False,
    )
```

profile of v0, /device:TPU:0, one launch (start us, length us, event | category | flops | bytes accessed | tf_op | source)
XLA Modules:
  0.0 297.6 jit_solution(8188155198489613293)
XLA Ops:
  7.2 0.0 reduce-scatter.5.cloned.1.call-start
  7.2 1.3 fusion.62
  8.6 0.1 sub.28
  8.6 5.0 %sort.32 = (s32[1152]{0:T(1024)}, s32[1152]{0:T(1024)S(1)}) sort(s32[1152]{0:T(1024)S(1)} %sub.28, s32[1152]{0:T(1024)S(1)} %iota.33), dimensions={0}, to_apply=%region_2.3 | sort | flops 12672 | bytes 18432 | tf_op jit(solution)/shard_map/jit(argsort)/sort | solution.py:30
  13.7 0.7 iota_compare_fusion.4
  14.4 16.4 %all_gather.12 = bf16[64,3072]{1,0:T(8,128)(2,1)S(1)} all-gather(bf16[8,3072]{1,0:T(8,128)(2,1)} %param.11), channel_id=1, replica_groups=mesh['row'=4,'col'=8] {'col'}, dimensions={0}, use_global_device_ids=true | all-gather | bytes 442368 | tf_op jit(solution)/shard_map/all_gather | solution.py:68
  30.8 0.1 copy_bitcast_fusion.7
  30.9 13.3 %gather_fusion = bf16[288,64,128]{2,1,0:T(8,128)(2,1)} fusion(bf16[64,24,128]{2,0,1:T(8,128)(2,1)S(1)} %copy_bitcast_fusion.7, s32[1024]{0:T(1024)S(1)} %pad_clamp_fusion.3), kind=kCustom, calls=%fused_computation.clone | custom fusion | bytes 9438336 | tf_op jit(solution)/shard_map/jit(_take)/gather | solution.py:39
  44.3 6.7 %fusion.6 = f32[288,64,128]{2,1,0:T(8,128)S(1)} fusion(bf16[1,1,288,128,128]{4,3,2,1,0:T(8,128)(2,1)} %param.14, bf16[288,64,128]{2,1,0:T(8,128)(2,1)} %gather_fusion, pred[288]{0:T(512)(128)(4,1)S(1)} %get-tuple-element.27), kind=kOutput, calls=%fused_computation.12 | convolution fusion | flops 606339072 | bytes 23593248 | tf_op jit(solution)/shard_map/tkb,kbc->ktc/dot_general | solution.py:41
  51.0 9.4 %fusion.14 = f32[48,64,128]{2,0,1:T(8,128)S(1)} fusion(f32[288,64,128]{2,1,0:T(8,128)S(1)} %fusion.6, s32[288]{0:T(512)S(1)} %get-tuple-element.12, pred[288]{0:T(512)(128)(4,1)S(1)} %iota_compare_fusion.4), kind=kOutput, calls=%fused_computation.20 | convolution fusion | flops 1358982144 | bytes 11011488 | tf_op jit(solution)/shard_map/ktc,ko->toc/dot_general | solution.py:45
  60.5 0.0 copy-start.1
  60.5 0.0 copy-start
  60.5 1.6 copy.47
  62.1 0.0 reduce-scatter.5.cloned.1.call-update
  62.1 0.0 reduce-scatter.9.cloned.1.call-start
  62.2 0.0 copy-done.1
  62.2 0.6 fusion.61
  62.8 0.1 copy.13
  62.9 0.1 sub.26
  63.0 5.0 %sort.31 = (s32[1152]{0:T(1024)}, s32[1152]{0:T(1024)S(1)}) sort(s32[1152]{0:T(1024)S(1)} %sub.26, s32[1152]{0:T(1024)S(1)} %iota.31), dimensions={0}, to_apply=%region_0.0 | sort | flops 12672 | bytes 18432 | tf_op jit(solution)/shard_map/jit(argsort)/sort | solution.py:30
  68.1 0.0 copy-done
  68.1 14.4 %all_gather.14 = bf16[64,3072]{1,0:T(8,128)(2,1)S(1)} all-gather(bf16[8,3072]{1,0:T(8,128)(2,1)S(1)} %copy-done), channel_id=1, replica_groups=mesh['row'=4,'col'=8] {'col'}, dimensions={0}, use_global_device_ids=true | all-gather | bytes 442368 | tf_op jit(solution)/shard_map/all_gather | solution.py:69
  82.6 0.1 copy_bitcast_fusion.6
  82.7 13.6 %gather_fusion.2 = bf16[288,64,128]{2,1,0:T(8,128)(2,1)} fusion(bf16[64,24,128]{2,0,1:T(8,128)(2,1)S(1)} %copy_bitcast_fusion.6, s32[1024]{0:T(1024)S(1)} %pad_clamp_fusion.1), kind=kCustom, calls=%fused_computation.2.clone | custom fusion | bytes 9438336 | tf_op jit(solution)/shard_map/jit(_take)/gather | solution.py:39
  96.2 0.7 iota_compare_fusion.5
  96.9 15.3 %fusion = f32[288,64,128]{2,1,0:T(8,128)} fusion(bf16[1,1,288,128,128]{4,3,2,1,0:T(8,128)(2,1)} %param.17, bf16[288,64,128]{2,1,0:T(8,128)(2,1)} %gather_fusion.2, pred[288]{0:T(512)(128)(4,1)S(1)} %get-tuple-element.13), kind=kOutput, calls=%fused_computation.6 | convolution fusion | flops 606339072 | bytes 23593248 | tf_op jit(solution)/shard_map/tkb,kcb->ktc/dot_general | solution.py:41
  112.2 13.2 %fusion.10 = f32[48,64,128]{2,0,1:T(8,128)S(1)} fusion(f32[288,64,128]{2,1,0:T(8,128)} %fusion, s32[288]{0:T(512)S(1)} %get-tuple-element.26, pred[288]{0:T(512)(128)(4,1)S(1)} %iota_compare_fusion.5), kind=kOutput, calls=%fused_computation.16 | convolution fusion | flops 1358982144 | bytes 11011488 | tf_op jit(solution)/shard_map/ktc,ko->toc/dot_general | solution.py:45
  125.3 0.0 copy-start.2
  125.4 1.6 copy.46
  127.0 0.0 reduce-scatter.9.cloned.1.call-update
  127.0 0.0 reduce-scatter.11.cloned.1.call-start
  127.0 0.0 copy-done.2
  127.1 0.7 fusion.60
  127.7 0.7 fusion.59
  128.4 0.0 reduce-scatter.5.cloned.1.call-done
  128.5 30.8 %reduce-scatter.9.cloned.1.call-done = f32[16,6144]{1,0:T(8,128)} async-done(((f32[64,6144]{1,0:T(8,128)}), f32[16,6144]{1,0:T(8,128)}) %reduce-scatter.9.cloned.1.call-update) | async-done | bytes 393232 | tf_op jit(solution)/shard_map/reduce_scatter | solution.py:93
  159.3 1.4 fusion.30
  160.7 11.1 %all_gather.15 = bf16[64,6144]{1,0:T(8,128)(2,1)S(1)} all-gather(bf16[16,6144]{1,0:T(8,128)(2,1)S(1)} %get-tuple-element.19), channel_id=1, replica_groups=mesh['row'=4,'col'=8] {'row'}, dimensions={0}, use_global_device_ids=true | all-gather | bytes 983040 | tf_op jit(solution)/shard_map/all_gather | solution.py:99
  171.8 0.2 copy_bitcast_fusion.4
  172.0 11.0 %all_gather.13 = bf16[64,6144]{1,0:T(8,128)(2,1)S(1)} all-gather(bf16[16,6144]{1,0:T(8,128)(2,1)S(1)} %get-tuple-element.20), channel_id=1, replica_groups=mesh['row'=4,'col'=8] {'row'}, dimensions={0}, use_global_device_ids=true | all-gather | bytes 983040 | tf_op jit(solution)/shard_map/all_gather | solution.py:88
  183.0 13.5 %gather_fusion.3 = bf16[288,64,128]{2,1,0:T(8,128)(2,1)} fusion(bf16[64,48,128]{2,0,1:T(8,128)(2,1)S(1)} %copy_bitcast_fusion.4, s32[1024]{0:T(1024)S(1)} %pad_clamp_fusion), kind=kCustom, calls=%fused_computation.3.clone | custom fusion | bytes 9438336 | tf_op jit(solution)/shard_map/jit(_take)/gather | solution.py:39
  196.5 15.3 %fusion.4 = f32[288,64,128]{2,1,0:T(8,128)} fusion(bf16[1,1,288,128,128]{4,3,2,1,0:T(8,128)(2,1)} %param.14, bf16[288,64,128]{2,1,0:T(8,128)(2,1)} %gather_fusion.3, pred[288]{0:T(512)(128)(4,1)S(1)} %get-tuple-element.11), kind=kOutput, calls=%fused_computation.10 | convolution fusion | flops 606339072 | bytes 23593248 | tf_op jit(solution)/shard_map/tkb,kcb->ktc/dot_general | solution.py:41
  211.8 12.3 %fusion.8 = f32[24,64,128]{2,0,1:T(8,128)S(1)} fusion(f32[288,64,128]{2,1,0:T(8,128)} %fusion.4, s32[288]{0:T(512)S(1)} %get-tuple-element.28, pred[288]{0:T(512)(128)(4,1)S(1)} %iota_compare_fusion.4), kind=kOutput, calls=%fused_computation.14 | convolution fusion | flops 679491072 | bytes 10225056 | tf_op jit(solution)/shard_map/ktc,ko->toc/dot_general | solution.py:45
  224.1 1.1 copy.48
  225.2 0.0 reduce-scatter.11.cloned.1.call-update
  225.2 0.0 reduce-scatter.7.cloned.1.call-start
  225.3 0.2 copy_bitcast_fusion.5
  225.5 13.3 %gather_fusion.1 = bf16[288,64,128]{2,1,0:T(8,128)(2,1)} fusion(bf16[64,48,128]{2,0,1:T(8,128)(2,1)S(1)} %copy_bitcast_fusion.5, s32[1024]{0:T(1024)S(1)} %pad_clamp_fusion.2), kind=kCustom, calls=%fused_computation.1.clone | custom fusion | bytes 9438336 | tf_op jit(solution)/shard_map/jit(_take)/gather | solution.py:39
  238.8 6.8 %fusion.2 = f32[288,64,128]{2,1,0:T(8,128)S(1)} fusion(bf16[1,1,288,128,128]{4,3,2,1,0:T(8,128)(2,1)} %param.17, bf16[288,64,128]{2,1,0:T(8,128)(2,1)} %gather_fusion.1, pred[288]{0:T(512)(128)(4,1)S(1)} %get-tuple-element.25), kind=kOutput, calls=%fused_computation.8 | convolution fusion | flops 606339072 | bytes 23593248 | tf_op jit(solution)/shard_map/tkb,kbc->ktc/dot_general | solution.py:41
  245.7 8.9 %fusion.12 = f32[24,64,128]{2,0,1:T(8,128)S(1)} fusion(f32[288,64,128]{2,1,0:T(8,128)S(1)} %fusion.2, s32[288]{0:T(512)S(1)} %get-tuple-element.14, pred[288]{0:T(512)(128)(4,1)S(1)} %iota_compare_fusion.5), kind=kOutput, calls=%fused_computation.18 | convolution fusion | flops 679491072 | bytes 10225056 | tf_op jit(solution)/shard_map/ktc,ko->toc/dot_general | solution.py:45
  254.5 0.0 slice-start
  254.5 1.0 copy.49
  255.5 0.8 convert_reduce_fusion
  256.3 0.0 reduce-scatter.7.cloned.1.call-update
  256.3 0.0 slice-start.1
  256.3 12.5 %multiply_bitcast_fusion.1 = f32[1,1,288,128,128]{4,3,2,1,0:T(8,128)} fusion(f32[288]{0:T(512)S(1)} %fusion.60, bf16[288,64,128]{2,1,0:T(8,128)(2,1)} %gather_fusion, pred[288]{0:T(512)(128)(4,1)S(1)} %get-tuple-element.27, bf16[288,64,128]{2,1,0:T(8,128)(2,1)} %gather_fusion.3, pred[288]{0:T(512)(128)(4,1)S(1)} %get-tuple-element.11), kind=kOutput, calls=%fused_computation.5 | convolution fusion | flops 613416960 | bytes 28313280 | tf_op jit(solution)/shard_map/tkb,tkc->kbc/dot_general | solution.py:60
  268.8 0.0 slice-done
  268.8 0.0 slice-done.1
  268.9 11.3 %multiply_bitcast_fusion = f32[1,1,288,128,128]{4,3,2,1,0:T(8,128)} fusion(f32[288]{0:T(512)S(1)} %fusion.59, bf16[288,64,128]{2,1,0:T(8,128)(2,1)} %gather_fusion.1, pred[288]{0:T(512)(128)(4,1)S(1)} %get-tuple-element.25, bf16[288,64,128]{2,1,0:T(8,128)(2,1)S(1)} %bitcast.87, pred[288]{0:T(512)(128)(4,1)S(1)} %get-tuple-element.13), kind=kOutput, calls=%fused_computation.4 | convolution fusion | flops 613416960 | bytes 28313280 | tf_op jit(solution)/shard_map/tkb,tkc->kbc/dot_general | solution.py:60
  280.2 0.0 reduce-scatter.11.cloned.1.call-done
  280.2 1.5 convert_element_type.42
  281.7 7.4 %reduce-scatter.7.cloned.1.call-done = f32[8,3072]{1,0:T(8,128)} async-done(((f32[64,3072]{1,0:T(8,128)}), f32[8,3072]{1,0:T(8,128)}) %reduce-scatter.7.cloned.1.call-update) | async-done | bytes 98320 | tf_op jit(solution)/shard_map/reduce_scatter | solution.py:109
  289.1 1.5 convert_element_type.40
  (14 shorter events, 0.1 us)
Async XLA Ops:
  7.2 121.3 %reduce-scatter.5.cloned.1.call-start = ((), (), s32[]{:S(2)}) async-start(), calls=%async_computation.4 | async-start | bytes 1966080 | tf_op jit(solution)/shard_map/reduce_scatter | solution.py:80
  60.5 1.7 copy-start.1
  60.5 7.6 %copy-start = (bf16[8,3072]{1,0:T(8,128)(2,1)S(1)}, bf16[8,3072]{1,0:T(8,128)(2,1)}, u32[]{:S(2)}) copy-start(bf16[8,3072]{1,0:T(8,128)(2,1)} %param.12) | copy-start | bytes 147460
  62.1 97.1 %reduce-scatter.9.cloned.1.call-start = ((), (), s32[]{:S(2)}) async-start(), calls=%async_computation.6 | async-start | bytes 1966080 | tf_op jit(solution)/shard_map/reduce_scatter | solution.py:93
  125.3 1.7 copy-start.2
  127.0 153.2 %reduce-scatter.11.cloned.1.call-start = ((), (), s32[]{:S(2)}) async-start(), calls=%async_computation.7 | async-start | bytes 884736 | tf_op jit(solution)/shard_map/reduce_scatter | solution.py:110
  225.2 63.9 %reduce-scatter.7.cloned.1.call-start = ((), (), s32[]{:S(2)}) async-start(), calls=%async_computation.5 | async-start | bytes 884736 | tf_op jit(solution)/shard_map/reduce_scatter | solution.py:109
  254.5 14.3 %slice-start = ((s8[4718592]{0:T(1024)(128)(4,1)}), s8[524288]{0:T(1024)(128)(4,1)S(1)}, s32[]{:S(2)}) async-start(s8[4718592]{0:T(1024)(128)(4,1)} %bitcast.86), calls=%async_computation.8 | async-start | bytes 1048576
  256.3 12.5 %slice-start.1 = ((s8[4718592]{0:T(1024)(128)(4,1)}), s8[4194304]{0:T(1024)(128)(4,1)S(1)}, s32[]{:S(2)}) async-start(s8[4718592]{0:T(1024)(128)(4,1)} %bitcast.86), calls=%async_computation.9 | async-start | bytes 8388608
Sparse Core Ops, SparseCore 0:
  62.3 32.0 reduce-scatter.4
  127.1 32.1 reduce-scatter.8
  225.3 31.6 reduce-scatter.10
  259.3 29.7 reduce-scatter.6
where the time goes:
time: 304 us; the launch traced here: 298 us
  matrix products  112 us (37%)
  local copies, waits for them, and re-layouts  60 us (20%)
  blocking collectives  53 us (17%)
  waiting for transfers between devices  38.3 us (13%)
  other arithmetic  19.9 us (7%)
  between operations  14.6 us (5%)
    gather x4, local copies, waits for them, and re-layouts, sparse_apply(): picked = jnp.take(pieces, source, axis=1)  53.8 us
    dot_general x4, matrix products, sparse_apply(): jnp.einsum(pattern, picked, blocks, preferred_element_type=jnp.float32)  44.1 us
    dot_general x4, matrix products, sparse_apply(): jnp.einsum('ktc,ko->toc', products, placement_table, precision=lax.Precis...  43.8 us
    reduce_scatter x1, waiting for transfers between devices, local(): lax.psum_scatter(sparse_apply(rows_part, second_blocks, w2_cols, w2_rows,...  30.8 us
    dot_general x2, matrix products, block_grads(): jnp.einsum('tkb,tkc->kbc', left_picked, right_picked, preferred_element_t...  23.8 us
    all_gather x1, blocking collectives, local(): lax.all_gather(tokens, 'col', axis=0, tiled=True)  16.4 us
    all_gather x1, blocking collectives, local(): lax.all_gather(cotangent, 'col', axis=0, tiled=True)  14.4 us
    all_gather x1, blocking collectives, local(): lax.all_gather((grad_act * gelu_slope(hidden)).astype(jnp.bfloat16), 'row...  11.1 us
  transfers between devices with their start and end apart: 4, of which 2 were waited for; matrix products, arithmetic and copies ran while one was open for 36% of the time, Pallas kernels for 0%

commit v1 on v0

v1 whole, which is shorter than its diff:
```python
import math

import jax
import jax.numpy as jnp
from jax import lax
from jax.experimental import pallas as pl
from jax.experimental.pallas import tpu as pltpu
from jax.sharding import PartitionSpec as P

BLK = 128
F32 = jnp.float32
BF16 = jnp.bfloat16
VMEM_LIMIT = 40 * 1024 * 1024

slope_const = math.sqrt(2.0 / math.pi)


def gelu_parts(values):
    inner = slope_const * (values + 0.044715 * values * values * values)
    tangent = jnp.tanh(inner)
    value = 0.5 * values * (1.0 + tangent)
    slope = 0.5 * (1.0 + tangent) + 0.5 * values * (1.0 - tangent * tangent) * slope_const * (
        1.0 + 3.0 * 0.044715 * values * values
    )
    return value, slope


def swap(array, axis, size, mask):
    return lax.ppermute(array, axis, [(place, place ^ mask) for place in range(size)])


def call(body, outs, in_specs, args, scratch=(), grid=None, out_specs=None, flops=0, moved=0):
    whole = pl.BlockSpec(memory_space=pltpu.VMEM)
    extra = {} if grid is None else {"grid": grid}
    return pl.pallas_call(
        body,
        out_shape=outs,
        in_specs=in_specs,
        out_specs=[whole] * len(outs) if out_specs is None else out_specs,
        scratch_shapes=list(scratch),
        compiler_params=pltpu.CompilerParams(vmem_limit_bytes=VMEM_LIMIT),
        cost_estimate=pl.CostEstimate(flops=flops, bytes_accessed=moved, transcendentals=0),
        **extra,
    )(*args)


VM = pl.BlockSpec(memory_space=pltpu.VMEM)
SM = pl.BlockSpec(memory_space=pltpu.SMEM)


def shape_of(shape, dtype):
    return jax.ShapeDtypeStruct(shape, dtype)


def dot(left, right, left_dim, right_dim):
    return lax.dot_general(
        left, right, (((left_dim,), (right_dim,)), ((), ())), preferred_element_type=F32
    )


class Slots:
    def __init__(self, mask_shape, capacity):
        self.rows, self.cols = mask_shape
        self.capacity = capacity
        self.even = self.cols % 8 == 0 and capacity == self.rows * (self.cols // 4)
        self.group = self.cols // 4 if self.even else 1
        self.groups = capacity // self.group
        self.spare = 0 if self.even else 1

    def index_args(self, mask):
        flat = mask.reshape(-1)
        count = flat.shape[0]
        places = jnp.arange(count, dtype=jnp.int32)
        lane = jnp.arange(self.cols, dtype=jnp.int32)
        within = jnp.sum(jnp.where(lane[None, :] <= lane[:, None], mask[:, None, :], 0), axis=2)
        row_sum = jnp.sum(mask, axis=1)
        line = jnp.arange(self.rows, dtype=jnp.int32)
        before = jnp.sum(jnp.where(line[None, :] < line[:, None], row_sum[None, :], 0), axis=1)
        rank = (within + before[:, None] - 1).reshape(-1)
        slot = jnp.arange(self.capacity, dtype=jnp.int32)
        hit = (rank[None, :] == slot[:, None]) & (flat[None, :] > 0)
        order = jnp.sum(jnp.where(hit, places[None, :], 0), axis=1)
        live = slot < jnp.sum(flat)
        row = jnp.where(live, order // self.cols, self.rows)
        col = jnp.where(live, order % self.cols, self.cols)
        return row, col


def index_kernel(layouts, *refs):
    count = len(layouts)
    for layout, mask_ref, out_ref in zip(layouts, refs[:count], refs[count:]):
        rows, cols, group = layout.rows, layout.cols, layout.group
        mask = mask_ref[...].astype(F32)
        lower = lax.broadcasted_iota(jnp.int32, (cols, cols), 0)
        upper = lax.broadcasted_iota(jnp.int32, (cols, cols), 1)
        ramp = jnp.where(lower <= upper, 1.0, 0.0).astype(BF16)
        rank = dot(mask.astype(BF16), ramp, 1, 0)
        place = lax.broadcasted_iota(jnp.int32, (rows, cols), 1).astype(F32)
        lane = lax.broadcasted_iota(jnp.int32, (rows, BLK), 1)
        found = jnp.zeros((rows, BLK), F32)
        for slot in range(group):
            hit = (rank == float(slot + 1)) & (mask > 0.0)
            column = jnp.sum(jnp.where(hit, place, 0.0), axis=1, keepdims=True)
            found = jnp.where(lane == slot, column, found)
        out_ref[...] = found.astype(jnp.int32)


def slot_indices(layouts, masks):
    if all(layout.even and layout.group <= BLK for layout in layouts):
        outs = call(
            lambda *refs: index_kernel(layouts, *refs),
            [shape_of((layout.rows, BLK), jnp.int32) for layout in layouts],
            [VM] * len(layouts),
            masks,
        )
        return [(out, out) for out in outs]
    return [layout.index_args(mask) for layout, mask in zip(layouts, masks)]


def read_slot(layout, row_ref, col_ref, group, member):
    if layout.even:
        return group, col_ref[group, member]
    return row_ref[group], col_ref[group]


def add_forward(layout, row_ref, col_ref, first, here, source, blocks, total):
    group = layout.group
    for near in range(here):
        if layout.even:
            left = source[first + near]
            width = 2 if group % 2 == 0 else 1
            for member in range(0, group, width):
                place = near * group + member
                right = [blocks[place + more] for more in range(width)]
                right = right[0] if width == 1 else jnp.concatenate(right, axis=1)
                product = dot(left, right, 1, 0)
                for more in range(width):
                    col = col_ref[first + near, member + more]
                    total[col] += product[:, more * BLK : (more + 1) * BLK]
        else:
            row, col = read_slot(layout, row_ref, col_ref, first + near, 0)
            total[col] += dot(source[row], blocks[near], 1, 0)


def add_backward(layout, row_ref, col_ref, first, here, source, blocks, total):
    group = layout.group
    for near in range(here):
        if layout.even:
            width = 2 if group % 2 == 0 else 1
            result = None
            for member in range(0, group, width):
                place = near * group + member
                cols = [col_ref[first + near, member + more] for more in range(width)]
                left = [source[col] for col in cols]
                right = [blocks[place + more] for more in range(width)]
                left = left[0] if width == 1 else jnp.concatenate(left, axis=1)
                right = right[0] if width == 1 else jnp.concatenate(right, axis=1)
                product = dot(left, right, 1, 1)
                result = product if result is None else result + product
            total[first + near] = result
        else:
            row, col = read_slot(layout, row_ref, col_ref, first + near, 0)
            total[row] += dot(source[col], blocks[near], 1, 1)


def block_products(layout, row_ref, col_ref, first, here, left, right, out):
    group = layout.group
    for near in range(here):
        if layout.even:
            turned = left[first + near].T
            width = 2 if group % 2 == 0 else 1
            for member in range(0, group, width):
                place = near * group + member
                cols = [col_ref[first + near, member + more] for more in range(width)]
                wide = [right[col] for col in cols]
                wide = wide[0] if width == 1 else jnp.concatenate(wide, axis=1)
                product = dot(turned, wide, 1, 0)
                for more in range(width):
                    out[place + more] = product[:, more * BLK : (more + 1) * BLK]
        else:
            row, col = read_slot(layout, row_ref, col_ref, first + near, 0)
            live = row < layout.rows
            product = dot(left[row].T, right[col], 1, 0)
            out[near] = jnp.where(live, product, 0.0)


def gather_model(me, shards, stage, full):
    piece = shards[0].shape[0]
    for mask, shard in enumerate(shards):
        start = pl.multiple_of((me ^ mask) * piece, piece)
        stage[pl.ds(start, piece), :] = shard[...].astype(F32)
    for block in range(shards[0].shape[1] // BLK):
        full[block] = stage[:, block * BLK : (block + 1) * BLK].astype(full.dtype)


def gather_hidden(me, shares, full):
    blocks, piece, _ = shares[0].shape
    for mask, share in enumerate(shares):
        start = pl.multiple_of((me ^ mask) * piece, piece)
        full[pl.ds(0, blocks), pl.ds(start, piece), :] = share[...]


def steps_for(layout):
    for steps in (6, 4, 3, 2):
        if layout.groups % steps == 0:
            return steps
    return 1


def weight_spec(layout, steps):
    slots = layout.capacity // steps
    return pl.BlockSpec((slots, BLK, BLK), lambda step: (step, 0, 0))


def whole_spec(shape):
    rank = len(shape)
    return pl.BlockSpec(shape, lambda step: (0,) * rank)


def apply_cost(layout, tokens):
    return 2 * layout.capacity * BLK * BLK * tokens, 2 * layout.capacity * BLK * BLK


def model_to_hidden(layout, rows_cols, shards, blocks, forward, hidden_blocks, n_row):
    steps = steps_for(layout)
    here = layout.groups // steps
    count = len(shards)
    tokens = shards[0].shape[0] * count
    model_blocks = shards[0].shape[1] // BLK
    piece = tokens // n_row
    spare = layout.spare

    def body(row_ref, col_ref, *refs):
        parts = refs[:count]
        weights = refs[count]
        own, *sends, whole = refs[count + 1 : count + 2 + n_row]
        stage, full, total = refs[count + 2 + n_row :]
        step = pl.program_id(0)

        @pl.when(step == 0)
        def _():
            gather_model(lax.axis_index("col"), parts, stage, full)
            if spare:
                full[model_blocks] = jnp.zeros((tokens, BLK), BF16)
            total[...] = jnp.zeros_like(total)

        work = add_forward if forward else add_backward
        work(layout, row_ref, col_ref, step * here, here, full, weights, total)

        @pl.when(step == steps - 1)
        def _():
            me = lax.axis_index("row")
            whole[...] = full[pl.ds(0, model_blocks)]
            for mask, out in enumerate([own] + sends):
                start = pl.multiple_of((me ^ mask) * piece, piece)
                out[...] = total[pl.ds(0, hidden_blocks), pl.ds(start, piece), :].astype(out.dtype)

    share = (hidden_blocks, piece, BLK)
    outs = [shape_of(share, F32)] + [shape_of(share, BF16)] * (n_row - 1)
    outs += [shape_of((model_blocks, tokens, BLK), BF16)]
    flops, moved = apply_cost(layout, tokens)
    own, *rest = call(
        body,
        outs,
        [SM, SM] + [whole_spec(shards[0].shape)] * count + [weight_spec(layout, steps)],
        [*rows_cols, *shards, blocks],
        scratch=[
            pltpu.VMEM((tokens, model_blocks * BLK), F32),
            pltpu.VMEM((model_blocks + spare, tokens, BLK), BF16),
            pltpu.VMEM((hidden_blocks + spare, tokens, BLK), F32),
        ],
        grid=(steps,),
        out_specs=[whole_spec(out.shape) for out in outs],
        flops=flops,
        moved=moved,
    )
    return own, rest[:-1], rest[-1]


def hidden_to_model(layout, rows_cols, shares, blocks, forward, model_blocks, n_col, other=None):
    steps = steps_for(layout)
    here = layout.groups // steps
    count = len(shares)
    hidden_blocks, part, _ = shares[0].shape
    tokens = part * count
    piece = tokens // n_col
    half = n_col // 2
    spare = layout.spare
    grads = other is not None

    def body(row_ref, col_ref, *refs):
        parts = refs[:count]
        refs = refs[count:]
        if grads:
            other_ref, refs = refs[0], refs[1:]
        weights, keep, send = refs[:3]
        refs = refs[3:]
        if grads:
            grad, full, other_full, total = refs
        else:
            whole, sums, full, total = refs
        step = pl.program_id(0)

        @pl.when(step == 0)
        def _():
            gather_hidden(lax.axis_index("row"), parts, full)
            if spare:
                full[hidden_blocks] = jnp.zeros((tokens, BLK), BF16)
            if grads:
                other_full[pl.ds(0, model_blocks)] = other_ref[...]
                if spare:
                    other_full[model_blocks] = jnp.zeros((tokens, BLK), BF16)
            total[...] = jnp.zeros_like(total)

        work = add_forward if forward else add_backward
        work(layout, row_ref, col_ref, step * here, here, full, weights, total)
        if grads:
            block_products(layout, row_ref, col_ref, step * here, here, full, other_full, grad)

        @pl.when(step == steps - 1)
        def _():
            me = lax.axis_index("col")
            for entry in range(half):
                mine = pl.multiple_of((me ^ (2 * entry)) * piece, piece)
                theirs = pl.multiple_of((me ^ (2 * entry + 1)) * piece, piece)
                for block in range(model_blocks):
                    lanes = pl.ds(block * BLK, BLK)
                    keep[entry, :, lanes] = total[block, pl.ds(mine, piece), :]
                    send[entry, :, lanes] = total[block, pl.ds(theirs, piece), :].astype(BF16)
            if not grads:
                whole[...] = full[pl.ds(0, hidden_blocks)]
                for block in range(hidden_blocks):
                    sums[pl.ds(block, 1), :] = jnp.sum(full[block].astype(F32), axis=0, keepdims=True)

    pair = (half, piece, model_blocks * BLK)
    outs = [shape_of(pair, F32), shape_of(pair, BF16)]
    out_specs = [whole_spec(pair), whole_spec(pair)]
    in_specs = [SM, SM] + [whole_spec(shares[0].shape)] * count
    args = [*rows_cols, *shares]
    scratch = [pltpu.VMEM((hidden_blocks + spare, tokens, BLK), BF16)]
    flops, moved = apply_cost(layout, tokens)
    if grads:
        in_specs += [whole_spec(other.shape)]
        args += [other]
        outs += [shape_of((layout.capacity, BLK, BLK), F32)]
        out_specs += [weight_spec(layout, steps)]
        scratch += [pltpu.VMEM((model_blocks + spare, tokens, BLK), BF16)]
        flops, moved = 2 * flops, 3 * moved
    else:
        outs += [shape_of((hidden_blocks, tokens, BLK), BF16), shape_of((hidden_blocks, BLK), F32)]
        out_specs += [whole_spec(out.shape) for out in outs[2:]]
    scratch += [pltpu.VMEM((model_blocks + spare, tokens, BLK), F32)]
    return call(
        body,
        outs,
        in_specs + [weight_spec(layout, steps)],
        args + [blocks],
        scratch=scratch,
        grid=(steps,),
        out_specs=out_specs,
        flops=flops,
        moved=moved,
    )


def weight_grad(layout, rows_cols, left, right):
    steps = steps_for(layout)
    here = layout.groups // steps
    spare = layout.spare

    def body(row_ref, col_ref, left_ref, right_ref, grad, *held):
        step = pl.program_id(0)
        if spare:

            @pl.when(step == 0)
            def _():
                for source, full in zip((left_ref, right_ref), held):
                    full[pl.ds(0, source.shape[0])] = source[...]
                    full[source.shape[0]] = jnp.zeros(source.shape[1:], BF16)

            left_ref, right_ref = held
        block_products(layout, row_ref, col_ref, step * here, here, left_ref, right_ref, grad)

    flops, moved = apply_cost(layout, left.shape[1])
    return call(
        body,
        [shape_of((layout.capacity, BLK, BLK), F32)],
        [SM, SM, whole_spec(left.shape), whole_spec(right.shape)],
        [*rows_cols, left, right],
        scratch=[pltpu.VMEM((a.shape[0] + 1, *a.shape[1:]), BF16) for a in (left, right)] if spare else [],
        grid=(steps,),
        out_specs=[weight_spec(layout, steps)],
        flops=flops,
        moved=2 * moved,
    )[0]


def add_up(own_ref, parts):
    total = own_ref[...]
    for part in parts:
        total = total + part[...].astype(F32)
    return total


def activate(own, parts, bias):
    def body(own_ref, bias_ref, *refs):
        parts, (value_ref, slope_ref) = refs[:-2], refs[-2:]
        hidden = add_up(own_ref, parts) + bias_ref[...][:, None, :]
        value, slope = gelu_parts(hidden)
        value_ref[...] = value.astype(BF16)
        slope_ref[...] = slope

    outs = [shape_of(own.shape, BF16), shape_of(own.shape, F32)]
    return call(body, outs, [VM] * (2 + len(parts)), [own, bias, *parts], moved=own.size * 20)


def scale_by_slope(own, parts, slope):
    def body(own_ref, slope_ref, *refs):
        parts, out_ref = refs[:-1], refs[-1]
        out_ref[...] = (add_up(own_ref, parts) * slope_ref[...]).astype(BF16)

    outs = [shape_of(own.shape, BF16)]
    return call(body, outs, [VM] * (2 + len(parts)), [own, slope, *parts], moved=own.size * 16)[0]


def pair_sum(keep, came):
    half, piece, width = keep.shape

    def body(keep_ref, came_ref, own_ref, *sends):
        own_ref[...] = keep_ref[0] + came_ref[0].astype(F32)
        for entry, send in enumerate(sends, 1):
            send[...] = (keep_ref[entry] + came_ref[entry].astype(F32)).astype(BF16)

    outs = [shape_of((piece, width), F32)] + [shape_of((piece, width), BF16)] * (half - 1)
    own, *sends = call(body, outs, [VM, VM], [keep, came], moved=keep.size * 8)
    return own, sends


def final_sum(own, parts):
    def body(own_ref, *refs):
        refs[-1][...] = add_up(own_ref, refs[:-1]).astype(BF16)

    outs = [shape_of(own.shape, BF16)]
    return call(body, outs, [VM] * (1 + len(parts)), [own, *parts], moved=own.size * 8)[0]


def gather_col(shard, n_col):
    shards = [None] * n_col
    shards[0] = shard
    for mask in range(2, n_col, 2):
        shards[mask] = swap(shard, "col", n_col, mask)
    for mask in range(0, n_col, 2):
        shards[mask + 1] = swap(shards[mask], "col", n_col, 1)
    return shards


def gather_row(share, n_row):
    return [share] + [swap(share, "row", n_row, mask) for mask in range(1, n_row)]


def send_row(sends, n_row):
    return [swap(send, "row", n_row, mask) for mask, send in enumerate(sends, 1)]


def reduce_col(keep, send, n_col):
    came = swap(send, "col", n_col, 1)
    own, sends = pair_sum(keep, came)
    return own, [swap(part, "col", n_col, 2 * entry) for entry, part in enumerate(sends, 1)]


def local(n_row, n_col, tokens, cotangent, w1_mask, w1_blocks, bias, w2_mask, w2_blocks):
    first_blocks = w1_blocks[0, 0]
    second_blocks = w2_blocks[0, 0]
    model_blocks, hidden_blocks = w1_mask.shape
    first = Slots(w1_mask.shape, first_blocks.shape[0])
    second = Slots(w2_mask.shape, second_blocks.shape[0])
    first_at, second_at = slot_indices([first, second], [w1_mask, w2_mask])
    bias_wide = bias.astype(F32).reshape(hidden_blocks, BLK)

    token_shards = gather_col(tokens, n_col)
    cotangent_shards = gather_col(cotangent, n_col)

    hidden_own, hidden_sends, full_tokens = model_to_hidden(
        first, first_at, token_shards, first_blocks, True, hidden_blocks, n_row
    )
    hidden_parts = send_row(hidden_sends, n_row)
    act_own, act_sends, full_cotangent = model_to_hidden(
        second, second_at, cotangent_shards, second_blocks, False, hidden_blocks, n_row
    )
    act_parts = send_row(act_sends, n_row)

    activated, slope = activate(hidden_own, hidden_parts, bias_wide)
    activated_shares = gather_row(activated, n_row)
    grad_hidden = scale_by_slope(act_own, act_parts, slope)
    grad_shares = gather_row(grad_hidden, n_row)

    out_keep, out_send, w2_grad = hidden_to_model(
        second, second_at, activated_shares, second_blocks, True, model_blocks, n_col, full_cotangent
    )
    out_own, out_parts = reduce_col(out_keep, out_send, n_col)
    in_keep, in_send, full_grad, bias_sum = hidden_to_model(
        first, first_at, grad_shares, first_blocks, False, model_blocks, n_col
    )
    in_own, in_parts = reduce_col(in_keep, in_send, n_col)
    w1_grad = weight_grad(first, first_at, full_tokens, full_grad)
    return (
        final_sum(out_own, out_parts),
        final_sum(in_own, in_parts),
        w1_grad[None, None],
        w2_grad[None, None],
        bias_sum.reshape(-1),
    )


def solution(mesh):
    n_row, n_col = mesh.shape["row"], mesh.shape["col"]
    return jax.shard_map(
        lambda *args: local(n_row, n_col, *args),
        mesh=mesh,
        in_specs=(
            P("col", "row"),
            P("col", "row"),
            P("row", "col"),
            P("row", "col", None, None, None),
            P("col"),
            P("col", "row"),
            P("row", "col", None, None, None),
        ),
        out_specs=(
            P("col", "row"),
            P("col", "row"),
            P("row", "col", None, None, None),
            P("row", "col", None, None, None),
            P("col"),
        ),
        check_vma=False,
    )
```

time: 304 us -> 118 us (0.39); the launches traced: 298 us -> 118 us
  matrix products: 112 us -> 0 us
  blocking collectives: 53 us -> 0 us
  local copies, waits for them, and re-layouts: 60 us -> 14.1 us
  Pallas kernels: 0 us -> 37 us
  starting transfers between devices: 0.16 us -> 35.3 us
  other arithmetic: 19.9 us -> 0.01 us
  between operations: 14.6 us -> 0.84 us
  waiting for transfers between devices: 38.3 us -> 30.5 us
    dot_general x10 -> x0, matrix products: 112 us -> none  [the longest x4 44.1 us: sparse_apply(): jnp.einsum(pattern, picked, blocks, preferred_element_type=jnp.float32)]
    gather x4 -> x0, local copies, waits for them, and re-layouts: 53.8 us -> none  [sparse_apply(): picked = jnp.take(pieces, source, axis=1)]
    all_gather x4 -> x0, blocking collectives: 53 us -> none  [the longest x1 16.4 us: local(): lax.all_gather(tokens, 'col', axis=0, tiled=True)]
    reduce_scatter x4 -> x0, waiting for transfers between devices: 38.2 us -> none  [the longest x1 30.8 us: local(): lax.psum_scatter(sparse_apply(rows_part, second_blocks, w2_cols, w2_rows,...]
    pallas_call x0 -> x12, Pallas kernels: none -> 37 us  [call(): pl.pallas_call(body, out_shape=outs, in_specs=in_specs, out_specs=[whole]...]
    ppermute x0 -> x34, starting transfers between devices: none -> 35.3 us  [swap(): lax.ppermute(array, axis, [(place, place ^ mask) for place in range(size)])]
    ppermute x0 -> x34, waiting for transfers between devices: none -> 30.5 us  [swap(): lax.ppermute(array, axis, [(place, place ^ mask) for place in range(size)])]
    sort x2 -> x0, other arithmetic: 10.1 us -> none  [slot_layout(): order = jnp.argsort(1 - flat, stable=True)[:capacity]]
  transfers between devices with their start and end apart: 4 -> 34, of which waited for: 2 -> 9; matrix products, arithmetic and copies ran while one was open for 36% -> 1% of each run, Pallas kernels for 0% -> 27%
where the time goes in v1:
time: 118 us
  Pallas kernels  37 us (31%)
  starting transfers between devices  35.3 us (30%)
  waiting for transfers between devices  30.5 us (26%)
  local copies, waits for them, and re-layouts  14.1 us (12%)
    pallas_call x12, Pallas kernels, call(): pl.pallas_call(body, out_shape=outs, in_specs=in_specs, out_specs=[whole]...  37 us
    ppermute x34, starting transfers between devices, swap(): lax.ppermute(array, axis, [(place, place ^ mask) for place in range(size)])  35.3 us
    ppermute x34, waiting for transfers between devices, swap(): lax.ppermute(array, axis, [(place, place ^ mask) for place in range(size)])  30.5 us
    unnamed x21, local copies, waits for them, and re-layouts  14.1 us
  transfers between devices with their start and end apart: 34, of which 9 were waited for; matrix products, arithmetic and copies ran while one was open for 1% of the time, Pallas kernels for 27%

profile of v1, /device:TPU:0, one launch (start us, length us, event | category | flops | bytes accessed | tf_op | source)
XLA Modules:
  0.0 117.8 jit_solution(14683517685148901505)
XLA Ops:
  0.6 4.1 %collective-permute-start.3 = (bf16[8,3072]{1,0:T(8,128)(2,1)}, bf16[8,3072]{1,0:T(8,128)(2,1)S(1)}, u32[]{:S(2)}, u32[]{:S(2)}) collective-permute-start(bf16[8,3072]{1,0:T(8,128)(2,1)} %refs_0_.4), channel_id=1, source_target_pairs={{0,4},{1,5},{2,6},{3,7},{4,0},{5,1},{6,2},{7,3},{8,12},{9,13},{10,... | collective-permute-start | bytes 147464 | tf_op jit(solution)/shard_map/ppermute | solution.py:29
  4.7 1.6 %collective-permute-start.1 = (bf16[8,3072]{1,0:T(8,128)(2,1)}, bf16[8,3072]{1,0:T(8,128)(2,1)S(1)}, u32[]{:S(2)}, u32[]{:S(2)}) collective-permute-start(bf16[8,3072]{1,0:T(8,128)(2,1)} %refs_0_.4), channel_id=1, source_target_pairs={{0,2},{1,3},{2,0},{3,1},{4,6},{5,7},{6,4},{7,5},{8,10},{9,11},{10,... | collective-permute-start | bytes 147464 | tf_op jit(solution)/shard_map/ppermute | solution.py:29
  6.3 0.0 collective-permute-start.5
  6.3 0.0 collective-permute-start
  6.3 1.3 %collective-permute-done.3.refs_4_ = bf16[8,3072]{1,0:T(8,128)(2,1)S(1)} collective-permute-done((bf16[8,3072]{1,0:T(8,128)(2,1)}, bf16[8,3072]{1,0:T(8,128)(2,1)S(1)}, u32[]{:S(2)}, u32[]{:S(2)}) %collective-permute-start.3) | collective-permute-done | bytes 49184 | tf_op jit(solution)/shard_map/ppermute | solution.py:29
  7.7 1.4 %collective-permute-done.1.refs_2_ = bf16[8,3072]{1,0:T(8,128)(2,1)S(1)} collective-permute-done((bf16[8,3072]{1,0:T(8,128)(2,1)}, bf16[8,3072]{1,0:T(8,128)(2,1)S(1)}, u32[]{:S(2)}, u32[]{:S(2)}) %collective-permute-start.1) | collective-permute-done | bytes 49184 | tf_op jit(solution)/shard_map/ppermute | solution.py:29
  9.0 3.4 %collective-permute-done.5.refs_6_ = bf16[8,3072]{1,0:T(8,128)(2,1)S(1)} collective-permute-done((bf16[8,3072]{1,0:T(8,128)(2,1)}, bf16[8,3072]{1,0:T(8,128)(2,1)S(1)}, u32[]{:S(2)}, u32[]{:S(2)}) %collective-permute-start.5) | collective-permute-done | bytes 49184 | tf_op jit(solution)/shard_map/ppermute | solution.py:29
  12.4 0.8 copy.12.refs_1_
  13.2 0.7 copy-done.5
  13.9 0.3 shard_map.110
  14.2 0.0 collective-permute-done.refs_1_
  14.2 0.0 collective-permute-done.2.refs_3_
  14.2 0.0 collective-permute-done.6.refs_7_
  14.2 0.0 copy-start
  14.2 3.7 %copy-done = bf16[1,1,288,128,128]{4,3,2,1,0:T(8,128)(2,1)S(1)} copy-done((bf16[1,1,288,128,128]{4,3,2,1,0:T(8,128)(2,1)S(1)}, bf16[1,1,288,128,128]{4,3,2,1,0:T(8,128)(2,1)}, u32[]{:S(2)}) %copy-start) | copy-done | bytes 9437208
  17.9 0.8 copy-done.3
  18.7 4.2 %shard_map.111 = (f32[48,16,128]{2,1,0:T(8,128)S(1)}, bf16[48,16,128]{2,1,0:T(8,128)(2,1)S(1)}, bf16[48,16,128]{2,1,0:T(8,128)(2,1)S(1)}, bf16[48,16,128]{2,1,0:T(8,128)(2,1)S(1)}, bf16[24,64,128]{2,1,0:T(8,128)(2,1)S(1)}) custom-call(s32[24,128]{1,0:T(8,128)S(1)} %get-tuple-element.35.row_ref.col_ref, s32[24,128]{1,0:T(8,128)S(1)} %get-tuple-element.35.row_ref.col_ref, ...), custom_call_target="tpu_custom_call" | custom-call | flops 603979776 | bytes 9437184 | tf_op jit(solution)/shard_map/pallas_call | solution.py:35
  22.9 1.6 %collective-permute-start.7 = (bf16[48,16,128]{2,1,0:T(8,128)(2,1)S(1)}, bf16[48,16,128]{2,1,0:T(8,128)(2,1)S(1)}, u32[]{:S(2)}, u32[]{:S(2)}) collective-permute-start(bf16[48,16,128]{2,1,0:T(8,128)(2,1)S(1)} %get-tuple-element.37), channel_id=1, source_target_pairs={{0,8},{8,0},{16,24},{24,16},{1,9},{9,1},{17,25},{25,17},{2,10},{10... | collective-permute-start | bytes 589832 | tf_op jit(solution)/shard_map/ppermute | solution.py:29
  24.5 0.1 collective-permute-start.16
  24.6 1.1 collective-permute-start.14
  25.7 3.2 %collective-permute-start.18 = (bf16[8,3072]{1,0:T(8,128)(2,1)}, bf16[8,3072]{1,0:T(8,128)(2,1)S(1)}, u32[]{:S(2)}, u32[]{:S(2)}) collective-permute-start(bf16[8,3072]{1,0:T(8,128)(2,1)} %refs_0_.5), channel_id=1, source_target_pairs={{0,6},{1,7},{2,4},{3,5},{4,2},{5,3},{6,0},{7,1},{8,14},{9,15},{10,... | collective-permute-start | bytes 147464 | tf_op jit(solution)/shard_map/ppermute | solution.py:29
  28.9 0.0 collective-permute-start.13
  28.9 1.1 collective-permute-done.16.refs_4_
  30.0 0.0 collective-permute-start.17
  30.0 0.0 collective-permute-done.14.refs_2_
  30.0 0.5 collective-permute-start.15
  30.5 1.3 %collective-permute-done.18.refs_6_ = bf16[8,3072]{1,0:T(8,128)(2,1)S(1)} collective-permute-done((bf16[8,3072]{1,0:T(8,128)(2,1)}, bf16[8,3072]{1,0:T(8,128)(2,1)S(1)}, u32[]{:S(2)}, u32[]{:S(2)}) %collective-permute-start.18) | collective-permute-done | bytes 49184 | tf_op jit(solution)/shard_map/ppermute | solution.py:29
  31.8 0.0 collective-permute-done.15.refs_3_
  31.8 1.2 %collective-permute-done.19.refs_7_ = bf16[8,3072]{1,0:T(8,128)(2,1)S(1)} collective-permute-done((bf16[8,3072]{1,0:T(8,128)(2,1)S(1)}, bf16[8,3072]{1,0:T(8,128)(2,1)S(1)}, u32[]{:S(2)}, u32[]{:S(2)}) %collective-permute-start.19) | collective-permute-done | bytes 49184 | tf_op jit(solution)/shard_map/ppermute | solution.py:29
  33.0 3.7 %copy-done.1 = bf16[1,1,288,128,128]{4,3,2,1,0:T(8,128)(2,1)S(1)} copy-done((bf16[1,1,288,128,128]{4,3,2,1,0:T(8,128)(2,1)S(1)}, bf16[1,1,288,128,128]{4,3,2,1,0:T(8,128)(2,1)}, u32[]{:S(2)}) %copy-start.1) | copy-done | bytes 9437208
  36.7 0.8 copy-done.4
  37.5 5.7 %shard_map.113 = (f32[48,16,128]{2,1,0:T(8,128)S(1)}, bf16[48,16,128]{2,1,0:T(8,128)(2,1)S(1)}, bf16[48,16,128]{2,1,0:T(8,128)(2,1)S(1)}, bf16[48,16,128]{2,1,0:T(8,128)(2,1)S(1)}, bf16[24,64,128]{2,1,0:T(8,128)(2,1)S(1)}) custom-call(s32[48,128]{1,0:T(8,128)S(1)} %get-tuple-element.34.row_ref.col_ref, s32[48,128]{1,0:T(8,128)S(1)} %get-tuple-element.34.row_ref.col_ref, ...), custom_call_target="tpu_custom_call" | custom-call | flops 603979776 | bytes 9437184 | tf_op jit(solution)/shard_map/pallas_call | solution.py:35
  43.2 0.6 collective-permute-start.24
  43.8 1.5 %collective-permute-start.25 = (bf16[48,16,128]{2,1,0:T(8,128)(2,1)S(1)}, bf16[48,16,128]{2,1,0:T(8,128)(2,1)S(1)}, u32[]{:S(2)}, u32[]{:S(2)}) collective-permute-start(bf16[48,16,128]{2,1,0:T(8,128)(2,1)S(1)} %get-tuple-element.51), channel_id=1, source_target_pairs={{0,16},{8,24},{16,0},{24,8},{1,17},{9,25},{17,1},{25,9},{2,18},{10... | collective-permute-start | bytes 589832 | tf_op jit(solution)/shard_map/ppermute | solution.py:29
  45.3 1.4 %collective-permute-start.26 = (bf16[48,16,128]{2,1,0:T(8,128)(2,1)S(1)}, bf16[48,16,128]{2,1,0:T(8,128)(2,1)S(1)}, u32[]{:S(2)}, u32[]{:S(2)}) collective-permute-start(bf16[48,16,128]{2,1,0:T(8,128)(2,1)S(1)} %get-tuple-element.52), channel_id=1, source_target_pairs={{0,24},{8,16},{16,8},{24,0},{1,25},{9,17},{17,9},{25,1},{2,26},{10... | collective-permute-start | bytes 589832 | tf_op jit(solution)/shard_map/ppermute | solution.py:29
  46.7 1.5 %collective-permute-start.8 = (bf16[48,16,128]{2,1,0:T(8,128)(2,1)S(1)}, bf16[48,16,128]{2,1,0:T(8,128)(2,1)S(1)}, u32[]{:S(2)}, u32[]{:S(2)}) collective-permute-start(bf16[48,16,128]{2,1,0:T(8,128)(2,1)S(1)} %get-tuple-element.38), channel_id=1, source_target_pairs={{0,16},{8,24},{16,0},{24,8},{1,17},{9,25},{17,1},{25,9},{2,18},{10... | collective-permute-start | bytes 589832 | tf_op jit(solution)/shard_map/ppermute | solution.py:29
  48.2 0.0 collective-permute-done.7.refs_0_
  48.2 0.5 collective-permute-start.9
  48.8 14.4 %collective-permute-done.8.refs_1_ = bf16[48,16,128]{2,1,0:T(8,128)(2,1)S(1)} collective-permute-done((bf16[48,16,128]{2,1,0:T(8,128)(2,1)S(1)}, bf16[48,16,128]{2,1,0:T(8,128)(2,1)S(1)}, u32[]{:S(2)}, u32[]{:S(2)}) %collective-permute-start.8) | collective-permute-done | bytes 196640 | tf_op jit(solution)/shard_map/ppermute | solution.py:29
  63.1 0.0 collective-permute-done.9.refs_2_
  63.1 0.4 shard_map.112
  63.6 0.1 shard_map.117.refs_0_
  63.7 2.5 %collective-permute-start.29 = (bf16[48,16,128]{2,1,0:T(8,128)(2,1)S(1)}, bf16[48,16,128]{2,1,0:T(8,128)(2,1)S(1)}, u32[]{:S(2)}, u32[]{:S(2)}) collective-permute-start(bf16[48,16,128]{2,1,0:T(8,128)(2,1)S(1)} %shard_map.117.refs_0_), channel_id=1, source_target_pairs={{0,24},{8,16},{16,8},{24,0},{1,25},{9,17},{17,9},{25,1},{2,26},{10... | collective-permute-start | bytes 589832 | tf_op jit(solution)/shard_map/ppermute | solution.py:29
  66.2 0.5 collective-permute-start.28
  66.7 0.6 collective-permute-start.27
  67.2 2.4 %collective-permute-start.12 = (bf16[48,16,128]{2,1,0:T(8,128)(2,1)S(1)}, bf16[48,16,128]{2,1,0:T(8,128)(2,1)S(1)}, u32[]{:S(2)}, u32[]{:S(2)}) collective-permute-start(bf16[48,16,128]{2,1,0:T(8,128)(2,1)S(1)} %get-tuple-element.40.refs_0_), channel_id=1, source_target_pairs={{0,24},{8,16},{16,8},{24,0},{1,25},{9,17},{17,9},{25,1},{2,26},{10... | collective-permute-start | bytes 589832 | tf_op jit(solution)/shard_map/ppermute | solution.py:29
  69.6 0.5 collective-permute-start.11
  70.2 2.1 %collective-permute-done.29.refs_3_ = bf16[48,16,128]{2,1,0:T(8,128)(2,1)S(1)} collective-permute-done((bf16[48,16,128]{2,1,0:T(8,128)(2,1)S(1)}, bf16[48,16,128]{2,1,0:T(8,128)(2,1)S(1)}, u32[]{:S(2)}, u32[]{:S(2)}) %collective-permute-start.29) | collective-permute-done | bytes 196640 | tf_op jit(solution)/shard_map/ppermute | solution.py:29
  72.2 1.7 %collective-permute-start.10 = (bf16[48,16,128]{2,1,0:T(8,128)(2,1)S(1)}, bf16[48,16,128]{2,1,0:T(8,128)(2,1)S(1)}, u32[]{:S(2)}, u32[]{:S(2)}) collective-permute-start(bf16[48,16,128]{2,1,0:T(8,128)(2,1)S(1)} %get-tuple-element.40.refs_0_), channel_id=1, source_target_pairs={{0,8},{8,0},{16,24},{24,16},{1,9},{9,1},{17,25},{25,17},{2,10},{10... | collective-permute-start | bytes 589832 | tf_op jit(solution)/shard_map/ppermute | solution.py:29
  74.0 4.3 %collective-permute-done.28.refs_2_ = bf16[48,16,128]{2,1,0:T(8,128)(2,1)S(1)} collective-permute-done((bf16[48,16,128]{2,1,0:T(8,128)(2,1)S(1)}, bf16[48,16,128]{2,1,0:T(8,128)(2,1)S(1)}, u32[]{:S(2)}, u32[]{:S(2)}) %collective-permute-start.28) | collective-permute-done | bytes 196640 | tf_op jit(solution)/shard_map/ppermute | solution.py:29
  78.3 6.0 %shard_map.118 = (f32[4,8,3072]{2,1,0:T(8,128)S(1)}, bf16[4,8,3072]{2,1,0:T(8,128)(2,1)S(1)}, bf16[48,64,128]{2,1,0:T(8,128)(2,1)S(1)}, f32[48,128]{1,0:T(8,128)}) custom-call(s32[24,128]{1,0:T(8,128)S(1)} %get-tuple-element.35.row_ref.col_ref, s32[24,128]{1,0:T(8,128)S(1)} %get-tuple-element.35.row_ref.col_ref, ...), custom_call_target="tpu_custom_call" | custom-call | flops 603979776 | bytes 9437184 | tf_op jit(solution)/shard_map/pallas_call | solution.py:35
  84.3 0.0 copy-start.2
  84.3 3.7 %copy-done.2 = bf16[1,1,288,128,128]{4,3,2,1,0:T(8,128)(2,1)S(1)} copy-done((bf16[1,1,288,128,128]{4,3,2,1,0:T(8,128)(2,1)S(1)}, bf16[1,1,288,128,128]{4,3,2,1,0:T(8,128)(2,1)}, u32[]{:S(2)}) %copy-start.2) | copy-done | bytes 9437208
  88.0 10.2 %shard_map.114 = (f32[4,8,3072]{2,1,0:T(8,128)S(1)}, bf16[4,8,3072]{2,1,0:T(8,128)(2,1)S(1)}, f32[288,128,128]{2,1,0:T(8,128)}) custom-call(s32[48,128]{1,0:T(8,128)S(1)} %get-tuple-element.34.row_ref.col_ref, s32[48,128]{1,0:T(8,128)S(1)} %get-tuple-element.34.row_ref.col_ref, bf16[48,16,128]{2,1,0:T(8,128)(2,1)S(1)} %get-tuple-element.40.refs_0_, ...), custom_call_target="tpu_custom_call" | custom-call | flops 1207959552 | bytes 28311552 | tf_op jit(solution)/shard_map/pallas_call | solution.py:35
  98.2 0.5 collective-permute-start.20
  98.8 0.1 collective-permute-start.31
  98.9 3.8 %collective-permute-start.32 = (bf16[8,3072]{1,0:T(8,128)(2,1)S(1)}, bf16[8,3072]{1,0:T(8,128)(2,1)S(1)}, u32[]{:S(2)}, u32[]{:S(2)}) collective-permute-start(bf16[8,3072]{1,0:T(8,128)(2,1)S(1)} %get-tuple-element.57), channel_id=1, source_target_pairs={{0,4},{1,5},{2,6},{3,7},{4,0},{5,1},{6,2},{7,3},{8,12},{9,13},{10,... | collective-permute-start | bytes 147464 | tf_op jit(solution)/shard_map/ppermute | solution.py:29
  102.7 0.6 collective-permute-start.33
  103.3 0.1 collective-permute-start.21
  103.4 3.8 %collective-permute-start.22 = (bf16[8,3072]{1,0:T(8,128)(2,1)S(1)}, bf16[8,3072]{1,0:T(8,128)(2,1)S(1)}, u32[]{:S(2)}, u32[]{:S(2)}) collective-permute-start(bf16[8,3072]{1,0:T(8,128)(2,1)S(1)} %get-tuple-element.46), channel_id=1, source_target_pairs={{0,4},{1,5},{2,6},{3,7},{4,0},{5,1},{6,2},{7,3},{8,12},{9,13},{10,... | collective-permute-start | bytes 147464 | tf_op jit(solution)/shard_map/ppermute | solution.py:29
  107.2 0.6 collective-permute-start.23
  107.7 8.8 %shard_map.121 = f32[288,128,128]{2,1,0:T(8,128)} custom-call(s32[24,128]{1,0:T(8,128)S(1)} %get-tuple-element.35.row_ref.col_ref, s32[24,128]{1,0:T(8,128)S(1)} %get-tuple-element.35.row_ref.col_ref, bf16[24,64,128]{2,1,0:T(8,128)(2,1)S(1)} %get-tuple-element.59.left_ref, bf16[48,64,128]{2,1,0:T(8,128)(2,1)S(1)} %get-tuple-element.60.right_ref), custom_call_target="tpu_custom_call" | custom-call | flops 603979776 | bytes 18874368 | tf_op jit(solution)/shard_map/pallas_call | solution.py:35
  116.5 0.7 shard_map.120
  117.2 0.6 shard_map.116
  (39 shorter events, 0.2 us)
Async XLA Ops:
  0.6 48.1 %copy-start.6 = (bf16[6144]{0:T(1024)(128)(2,1)S(1)}, bf16[6144]{0:T(1024)(128)(2,1)}, u32[]{:S(2)}) copy-start(bf16[6144]{0:T(1024)(128)(2,1)} %param.11) | copy-start | bytes 36868
  0.6 7.0 %collective-permute-start.3 = (bf16[8,3072]{1,0:T(8,128)(2,1)}, bf16[8,3072]{1,0:T(8,128)(2,1)S(1)}, u32[]{:S(2)}, u32[]{:S(2)}) collective-permute-start(bf16[8,3072]{1,0:T(8,128)(2,1)} %refs_0_.4), channel_id=1, source_target_pairs={{0,4},{1,5},{2,6},{3,7},{4,0},{5,1},{6,2},{7,3},{8,12},{9,13},{10,... | collective-permute-start | bytes 147464 | tf_op jit(solution)/shard_map/ppermute | solution.py:29
  4.7 4.3 %collective-permute-start.1 = (bf16[8,3072]{1,0:T(8,128)(2,1)}, bf16[8,3072]{1,0:T(8,128)(2,1)S(1)}, u32[]{:S(2)}, u32[]{:S(2)}) collective-permute-start(bf16[8,3072]{1,0:T(8,128)(2,1)} %refs_0_.4), channel_id=1, source_target_pairs={{0,2},{1,3},{2,0},{3,1},{4,6},{5,7},{6,4},{7,5},{8,10},{9,11},{10,... | collective-permute-start | bytes 147464 | tf_op jit(solution)/shard_map/ppermute | solution.py:29
  6.3 6.1 %collective-permute-start.5 = (bf16[8,3072]{1,0:T(8,128)(2,1)}, bf16[8,3072]{1,0:T(8,128)(2,1)S(1)}, u32[]{:S(2)}, u32[]{:S(2)}) collective-permute-start(bf16[8,3072]{1,0:T(8,128)(2,1)} %refs_0_.4), channel_id=1, source_target_pairs={{0,6},{1,7},{2,4},{3,5},{4,2},{5,3},{6,0},{7,1},{8,14},{9,15},{10,... | collective-permute-start | bytes 147464 | tf_op jit(solution)/shard_map/ppermute | solution.py:29
  6.3 7.9 %collective-permute-start = (bf16[8,3072]{1,0:T(8,128)(2,1)}, bf16[8,3072]{1,0:T(8,128)(2,1)S(1)}, u32[]{:S(2)}, u32[]{:S(2)}) collective-permute-start(bf16[8,3072]{1,0:T(8,128)(2,1)} %refs_0_.4), channel_id=1, source_target_pairs={{0,1},{1,0},{2,3},{3,2},{4,5},{5,4},{6,7},{7,6},{8,9},{9,8},{10,11... | collective-permute-start | bytes 147464 | tf_op jit(solution)/shard_map/ppermute | solution.py:29
  7.7 6.5 %collective-permute-start.4 = (bf16[8,3072]{1,0:T(8,128)(2,1)S(1)}, bf16[8,3072]{1,0:T(8,128)(2,1)S(1)}, u32[]{:S(2)}, u32[]{:S(2)}) collective-permute-start(bf16[8,3072]{1,0:T(8,128)(2,1)S(1)} %collective-permute-done.3.refs_4_), channel_id=1, source_target_pairs={{0,1},{1,0},{2,3},{3,2},{4,5},{5,4},{6,7},{7,6},{8,9},{9,8},{10,11... | collective-permute-start | bytes 147464 | tf_op jit(solution)/shard_map/ppermute | solution.py:29
  9.0 5.2 %collective-permute-start.2 = (bf16[8,3072]{1,0:T(8,128)(2,1)S(1)}, bf16[8,3072]{1,0:T(8,128)(2,1)S(1)}, u32[]{:S(2)}, u32[]{:S(2)}) collective-permute-start(bf16[8,3072]{1,0:T(8,128)(2,1)S(1)} %collective-permute-done.1.refs_2_), channel_id=1, source_target_pairs={{0,1},{1,0},{2,3},{3,2},{4,5},{5,4},{6,7},{7,6},{8,9},{9,8},{10,11... | collective-permute-start | bytes 147464 | tf_op jit(solution)/shard_map/ppermute | solution.py:29
  12.4 1.8 %collective-permute-start.6 = (bf16[8,3072]{1,0:T(8,128)(2,1)S(1)}, bf16[8,3072]{1,0:T(8,128)(2,1)S(1)}, u32[]{:S(2)}, u32[]{:S(2)}) collective-permute-start(bf16[8,3072]{1,0:T(8,128)(2,1)S(1)} %collective-permute-done.5.refs_6_), channel_id=1, source_target_pairs={{0,1},{1,0},{2,3},{3,2},{4,5},{5,4},{6,7},{7,6},{8,9},{9,8},{10,11... | collective-permute-start | bytes 147464 | tf_op jit(solution)/shard_map/ppermute | solution.py:29
  13.2 0.7 copy-start.5
  14.2 3.7 %copy-start = (bf16[1,1,288,128,128]{4,3,2,1,0:T(8,128)(2,1)S(1)}, bf16[1,1,288,128,128]{4,3,2,1,0:T(8,128)(2,1)}, u32[]{:S(2)}) copy-start(bf16[1,1,288,128,128]{4,3,2,1,0:T(8,128)(2,1)} %param.10) | copy-start | bytes 28311556
  17.9 0.8 copy-start.3
  18.7 59.6 %slice-start = ((s8[9437184]{0:T(1024)(128)(4,1)}), s8[4194304]{0:T(1024)(128)(4,1)S(1)}, s32[]{:S(2)}) async-start(s8[9437184]{0:T(1024)(128)(4,1)} %bitcast.9), calls=%async_computation | async-start | bytes 8388608
  18.7 59.6 %slice-start.1 = ((s8[9437184]{0:T(1024)(128)(4,1)}), s8[4194304]{0:T(1024)(128)(4,1)S(1)}, s32[]{:S(2)}) async-start(s8[9437184]{0:T(1024)(128)(4,1)} %bitcast.9), calls=%async_computation.1 | async-start | bytes 8388608
  22.9 25.3 %collective-permute-start.7 = (bf16[48,16,128]{2,1,0:T(8,128)(2,1)S(1)}, bf16[48,16,128]{2,1,0:T(8,128)(2,1)S(1)}, u32[]{:S(2)}, u32[]{:S(2)}) collective-permute-start(bf16[48,16,128]{2,1,0:T(8,128)(2,1)S(1)} %get-tuple-element.37), channel_id=1, source_target_pairs={{0,8},{8,0},{16,24},{24,16},{1,9},{9,1},{17,25},{25,17},{2,10},{10... | collective-permute-start | bytes 589832 | tf_op jit(solution)/shard_map/ppermute | solution.py:29
  24.5 5.5 %collective-permute-start.16 = (bf16[8,3072]{1,0:T(8,128)(2,1)}, bf16[8,3072]{1,0:T(8,128)(2,1)S(1)}, u32[]{:S(2)}, u32[]{:S(2)}) collective-permute-start(bf16[8,3072]{1,0:T(8,128)(2,1)} %refs_0_.5), channel_id=1, source_target_pairs={{0,4},{1,5},{2,6},{3,7},{4,0},{5,1},{6,2},{7,3},{8,12},{9,13},{10,... | collective-permute-start | bytes 147464 | tf_op jit(solution)/shard_map/ppermute | solution.py:29
  24.6 5.4 %collective-permute-start.14 = (bf16[8,3072]{1,0:T(8,128)(2,1)}, bf16[8,3072]{1,0:T(8,128)(2,1)S(1)}, u32[]{:S(2)}, u32[]{:S(2)}) collective-permute-start(bf16[8,3072]{1,0:T(8,128)(2,1)} %refs_0_.5), channel_id=1, source_target_pairs={{0,2},{1,3},{2,0},{3,1},{4,6},{5,7},{6,4},{7,5},{8,10},{9,11},{10,... | collective-permute-start | bytes 147464 | tf_op jit(solution)/shard_map/ppermute | solution.py:29
  25.7 6.1 %collective-permute-start.18 = (bf16[8,3072]{1,0:T(8,128)(2,1)}, bf16[8,3072]{1,0:T(8,128)(2,1)S(1)}, u32[]{:S(2)}, u32[]{:S(2)}) collective-permute-start(bf16[8,3072]{1,0:T(8,128)(2,1)} %refs_0_.5), channel_id=1, source_target_pairs={{0,6},{1,7},{2,4},{3,5},{4,2},{5,3},{6,0},{7,1},{8,14},{9,15},{10,... | collective-permute-start | bytes 147464 | tf_op jit(solution)/shard_map/ppermute | solution.py:29
  28.9 2.9 %collective-permute-start.13 = (bf16[8,3072]{1,0:T(8,128)(2,1)}, bf16[8,3072]{1,0:T(8,128)(2,1)S(1)}, u32[]{:S(2)}, u32[]{:S(2)}) collective-permute-start(bf16[8,3072]{1,0:T(8,128)(2,1)} %refs_0_.5), channel_id=1, source_target_pairs={{0,1},{1,0},{2,3},{3,2},{4,5},{5,4},{6,7},{7,6},{8,9},{9,8},{10,11... | collective-permute-start | bytes 147464 | tf_op jit(solution)/shard_map/ppermute | solution.py:29
  30.0 1.8 %collective-permute-start.17 = (bf16[8,3072]{1,0:T(8,128)(2,1)S(1)}, bf16[8,3072]{1,0:T(8,128)(2,1)S(1)}, u32[]{:S(2)}, u32[]{:S(2)}) collective-permute-start(bf16[8,3072]{1,0:T(8,128)(2,1)S(1)} %collective-permute-done.16.refs_4_), channel_id=1, source_target_pairs={{0,1},{1,0},{2,3},{3,2},{4,5},{5,4},{6,7},{7,6},{8,9},{9,8},{10,11... | collective-permute-start | bytes 147464 | tf_op jit(solution)/shard_map/ppermute | solution.py:29
  30.0 1.8 %collective-permute-start.15 = (bf16[8,3072]{1,0:T(8,128)(2,1)S(1)}, bf16[8,3072]{1,0:T(8,128)(2,1)S(1)}, u32[]{:S(2)}, u32[]{:S(2)}) collective-permute-start(bf16[8,3072]{1,0:T(8,128)(2,1)S(1)} %collective-permute-done.14.refs_2_), channel_id=1, source_target_pairs={{0,1},{1,0},{2,3},{3,2},{4,5},{5,4},{6,7},{7,6},{8,9},{9,8},{10,11... | collective-permute-start | bytes 147464 | tf_op jit(solution)/shard_map/ppermute | solution.py:29
  31.8 1.2 %collective-permute-start.19 = (bf16[8,3072]{1,0:T(8,128)(2,1)S(1)}, bf16[8,3072]{1,0:T(8,128)(2,1)S(1)}, u32[]{:S(2)}, u32[]{:S(2)}) collective-permute-start(bf16[8,3072]{1,0:T(8,128)(2,1)S(1)} %collective-permute-done.18.refs_6_), channel_id=1, source_target_pairs={{0,1},{1,0},{2,3},{3,2},{4,5},{5,4},{6,7},{7,6},{8,9},{9,8},{10,11... | collective-permute-start | bytes 147464 | tf_op jit(solution)/shard_map/ppermute | solution.py:29
  33.0 3.7 %copy-start.1 = (bf16[1,1,288,128,128]{4,3,2,1,0:T(8,128)(2,1)S(1)}, bf16[1,1,288,128,128]{4,3,2,1,0:T(8,128)(2,1)}, u32[]{:S(2)}) copy-start(bf16[1,1,288,128,128]{4,3,2,1,0:T(8,128)(2,1)} %param.13) | copy-start | bytes 28311556
  36.7 0.8 copy-start.4
  37.5 40.8 %slice-start.2 = ((s8[9437184]{0:T(1024)(128)(4,1)}), s8[1048576]{0:T(1024)(128)(4,1)S(1)}, s32[]{:S(2)}) async-start(s8[9437184]{0:T(1024)(128)(4,1)} %bitcast.9), calls=%async_computation.2 | async-start | bytes 2097152
  43.2 20.4 %collective-permute-start.24 = (bf16[48,16,128]{2,1,0:T(8,128)(2,1)S(1)}, bf16[48,16,128]{2,1,0:T(8,128)(2,1)S(1)}, u32[]{:S(2)}, u32[]{:S(2)}) collective-permute-start(bf16[48,16,128]{2,1,0:T(8,128)(2,1)S(1)} %get-tuple-element.50), channel_id=1, source_target_pairs={{0,8},{8,0},{16,24},{24,16},{1,9},{9,1},{17,25},{25,17},{2,10},{10... | collective-permute-start | bytes 589832 | tf_op jit(solution)/shard_map/ppermute | solution.py:29
  43.8 19.7 %collective-permute-start.25 = (bf16[48,16,128]{2,1,0:T(8,128)(2,1)S(1)}, bf16[48,16,128]{2,1,0:T(8,128)(2,1)S(1)}, u32[]{:S(2)}, u32[]{:S(2)}) collective-permute-start(bf16[48,16,128]{2,1,0:T(8,128)(2,1)S(1)} %get-tuple-element.51), channel_id=1, source_target_pairs={{0,16},{8,24},{16,0},{24,8},{1,17},{9,25},{17,1},{25,9},{2,18},{10... | collective-permute-start | bytes 589832 | tf_op jit(solution)/shard_map/ppermute | solution.py:29
  45.3 18.2 %collective-permute-start.26 = (bf16[48,16,128]{2,1,0:T(8,128)(2,1)S(1)}, bf16[48,16,128]{2,1,0:T(8,128)(2,1)S(1)}, u32[]{:S(2)}, u32[]{:S(2)}) collective-permute-start(bf16[48,16,128]{2,1,0:T(8,128)(2,1)S(1)} %get-tuple-element.52), channel_id=1, source_target_pairs={{0,24},{8,16},{16,8},{24,0},{1,25},{9,17},{17,9},{25,1},{2,26},{10... | collective-permute-start | bytes 589832 | tf_op jit(solution)/shard_map/ppermute | solution.py:29
  46.7 16.4 %collective-permute-start.8 = (bf16[48,16,128]{2,1,0:T(8,128)(2,1)S(1)}, bf16[48,16,128]{2,1,0:T(8,128)(2,1)S(1)}, u32[]{:S(2)}, u32[]{:S(2)}) collective-permute-start(bf16[48,16,128]{2,1,0:T(8,128)(2,1)S(1)} %get-tuple-element.38), channel_id=1, source_target_pairs={{0,16},{8,24},{16,0},{24,8},{1,17},{9,25},{17,1},{25,9},{2,18},{10... | collective-permute-start | bytes 589832 | tf_op jit(solution)/shard_map/ppermute | solution.py:29
  48.2 14.9 %collective-permute-start.9 = (bf16[48,16,128]{2,1,0:T(8,128)(2,1)S(1)}, bf16[48,16,128]{2,1,0:T(8,128)(2,1)S(1)}, u32[]{:S(2)}, u32[]{:S(2)}) collective-permute-start(bf16[48,16,128]{2,1,0:T(8,128)(2,1)S(1)} %get-tuple-element.39), channel_id=1, source_target_pairs={{0,24},{8,16},{16,8},{24,0},{1,25},{9,17},{17,9},{25,1},{2,26},{10... | collective-permute-start | bytes 589832 | tf_op jit(solution)/shard_map/ppermute | solution.py:29
  63.7 8.6 %collective-permute-start.29 = (bf16[48,16,128]{2,1,0:T(8,128)(2,1)S(1)}, bf16[48,16,128]{2,1,0:T(8,128)(2,1)S(1)}, u32[]{:S(2)}, u32[]{:S(2)}) collective-permute-start(bf16[48,16,128]{2,1,0:T(8,128)(2,1)S(1)} %shard_map.117.refs_0_), channel_id=1, source_target_pairs={{0,24},{8,16},{16,8},{24,0},{1,25},{9,17},{17,9},{25,1},{2,26},{10... | collective-permute-start | bytes 589832 | tf_op jit(solution)/shard_map/ppermute | solution.py:29
  66.2 12.1 %collective-permute-start.28 = (bf16[48,16,128]{2,1,0:T(8,128)(2,1)S(1)}, bf16[48,16,128]{2,1,0:T(8,128)(2,1)S(1)}, u32[]{:S(2)}, u32[]{:S(2)}) collective-permute-start(bf16[48,16,128]{2,1,0:T(8,128)(2,1)S(1)} %shard_map.117.refs_0_), channel_id=1, source_target_pairs={{0,16},{8,24},{16,0},{24,8},{1,17},{9,25},{17,1},{25,9},{2,18},{10... | collective-permute-start | bytes 589832 | tf_op jit(solution)/shard_map/ppermute | solution.py:29
  66.7 11.6 %collective-permute-start.27 = (bf16[48,16,128]{2,1,0:T(8,128)(2,1)S(1)}, bf16[48,16,128]{2,1,0:T(8,128)(2,1)S(1)}, u32[]{:S(2)}, u32[]{:S(2)}) collective-permute-start(bf16[48,16,128]{2,1,0:T(8,128)(2,1)S(1)} %shard_map.117.refs_0_), channel_id=1, source_target_pairs={{0,8},{8,0},{16,24},{24,16},{1,9},{9,1},{17,25},{25,17},{2,10},{10... | collective-permute-start | bytes 589832 | tf_op jit(solution)/shard_map/ppermute | solution.py:29
  67.2 17.1 %collective-permute-start.12 = (bf16[48,16,128]{2,1,0:T(8,128)(2,1)S(1)}, bf16[48,16,128]{2,1,0:T(8,128)(2,1)S(1)}, u32[]{:S(2)}, u32[]{:S(2)}) collective-permute-start(bf16[48,16,128]{2,1,0:T(8,128)(2,1)S(1)} %get-tuple-element.40.refs_0_), channel_id=1, source_target_pairs={{0,24},{8,16},{16,8},{24,0},{1,25},{9,17},{17,9},{25,1},{2,26},{10... | collective-permute-start | bytes 589832 | tf_op jit(solution)/shard_map/ppermute | solution.py:29
  69.6 14.7 %collective-permute-start.11 = (bf16[48,16,128]{2,1,0:T(8,128)(2,1)S(1)}, bf16[48,16,128]{2,1,0:T(8,128)(2,1)S(1)}, u32[]{:S(2)}, u32[]{:S(2)}) collective-permute-start(bf16[48,16,128]{2,1,0:T(8,128)(2,1)S(1)} %get-tuple-element.40.refs_0_), channel_id=1, source_target_pairs={{0,16},{8,24},{16,0},{24,8},{1,17},{9,25},{17,1},{25,9},{2,18},{10... | collective-permute-start | bytes 589832 | tf_op jit(solution)/shard_map/ppermute | solution.py:29
  72.2 12.1 %collective-permute-start.10 = (bf16[48,16,128]{2,1,0:T(8,128)(2,1)S(1)}, bf16[48,16,128]{2,1,0:T(8,128)(2,1)S(1)}, u32[]{:S(2)}, u32[]{:S(2)}) collective-permute-start(bf16[48,16,128]{2,1,0:T(8,128)(2,1)S(1)} %get-tuple-element.40.refs_0_), channel_id=1, source_target_pairs={{0,8},{8,0},{16,24},{24,16},{1,9},{9,1},{17,25},{25,17},{2,10},{10... | collective-permute-start | bytes 589832 | tf_op jit(solution)/shard_map/ppermute | solution.py:29
  84.3 14.4 %collective-permute-start.30 = (bf16[4,8,3072]{2,1,0:T(8,128)(2,1)S(1)}, bf16[4,8,3072]{2,1,0:T(8,128)(2,1)S(1)}, u32[]{:S(2)}, u32[]{:S(2)}) collective-permute-start(bf16[4,8,3072]{2,1,0:T(8,128)(2,1)S(1)} %get-tuple-element.54), channel_id=1, source_target_pairs={{0,1},{1,0},{2,3},{3,2},{4,5},{5,4},{6,7},{7,6},{8,9},{9,8},{10,11... | collective-permute-start | bytes 589832 | tf_op jit(solution)/shard_map/ppermute | solution.py:29
  84.3 3.7 %copy-start.2 = (bf16[1,1,288,128,128]{4,3,2,1,0:T(8,128)(2,1)S(1)}, bf16[1,1,288,128,128]{4,3,2,1,0:T(8,128)(2,1)}, u32[]{:S(2)}) copy-start(bf16[1,1,288,128,128]{4,3,2,1,0:T(8,128)(2,1)} %param.13) | copy-start | bytes 28311556
  98.2 5.0 %collective-permute-start.20 = (bf16[4,8,3072]{2,1,0:T(8,128)(2,1)S(1)}, bf16[4,8,3072]{2,1,0:T(8,128)(2,1)S(1)}, u32[]{:S(2)}, u32[]{:S(2)}) collective-permute-start(bf16[4,8,3072]{2,1,0:T(8,128)(2,1)S(1)} %get-tuple-element.43), channel_id=1, source_target_pairs={{0,1},{1,0},{2,3},{3,2},{4,5},{5,4},{6,7},{7,6},{8,9},{9,8},{10,11... | collective-permute-start | bytes 589832 | tf_op jit(solution)/shard_map/ppermute | solution.py:29
  98.8 8.4 %collective-permute-start.31 = (bf16[8,3072]{1,0:T(8,128)(2,1)S(1)}, bf16[8,3072]{1,0:T(8,128)(2,1)S(1)}, u32[]{:S(2)}, u32[]{:S(2)}) collective-permute-start(bf16[8,3072]{1,0:T(8,128)(2,1)S(1)} %get-tuple-element.56), channel_id=1, source_target_pairs={{0,2},{1,3},{2,0},{3,1},{4,6},{5,7},{6,4},{7,5},{8,10},{9,11},{10,... | collective-permute-start | bytes 147464 | tf_op jit(solution)/shard_map/ppermute | solution.py:29
  98.9 17.6 %collective-permute-start.32 = (bf16[8,3072]{1,0:T(8,128)(2,1)S(1)}, bf16[8,3072]{1,0:T(8,128)(2,1)S(1)}, u32[]{:S(2)}, u32[]{:S(2)}) collective-permute-start(bf16[8,3072]{1,0:T(8,128)(2,1)S(1)} %get-tuple-element.57), channel_id=1, source_target_pairs={{0,4},{1,5},{2,6},{3,7},{4,0},{5,1},{6,2},{7,3},{8,12},{9,13},{10,... | collective-permute-start | bytes 147464 | tf_op jit(solution)/shard_map/ppermute | solution.py:29
  102.7 13.8 %collective-permute-start.33 = (bf16[8,3072]{1,0:T(8,128)(2,1)S(1)}, bf16[8,3072]{1,0:T(8,128)(2,1)S(1)}, u32[]{:S(2)}, u32[]{:S(2)}) collective-permute-start(bf16[8,3072]{1,0:T(8,128)(2,1)S(1)} %get-tuple-element.58), channel_id=1, source_target_pairs={{0,6},{1,7},{2,4},{3,5},{4,2},{5,3},{6,0},{7,1},{8,14},{9,15},{10,... | collective-permute-start | bytes 147464 | tf_op jit(solution)/shard_map/ppermute | solution.py:29
  103.3 13.9 %collective-permute-start.21 = (bf16[8,3072]{1,0:T(8,128)(2,1)S(1)}, bf16[8,3072]{1,0:T(8,128)(2,1)S(1)}, u32[]{:S(2)}, u32[]{:S(2)}) collective-permute-start(bf16[8,3072]{1,0:T(8,128)(2,1)S(1)} %get-tuple-element.45), channel_id=1, source_target_pairs={{0,2},{1,3},{2,0},{3,1},{4,6},{5,7},{6,4},{7,5},{8,10},{9,11},{10,... | collective-permute-start | bytes 147464 | tf_op jit(solution)/shard_map/ppermute | solution.py:29
  103.4 13.8 %collective-permute-start.22 = (bf16[8,3072]{1,0:T(8,128)(2,1)S(1)}, bf16[8,3072]{1,0:T(8,128)(2,1)S(1)}, u32[]{:S(2)}, u32[]{:S(2)}) collective-permute-start(bf16[8,3072]{1,0:T(8,128)(2,1)S(1)} %get-tuple-element.46), channel_id=1, source_target_pairs={{0,4},{1,5},{2,6},{3,7},{4,0},{5,1},{6,2},{7,3},{8,12},{9,13},{10,... | collective-permute-start | bytes 147464 | tf_op jit(solution)/shard_map/ppermute | solution.py:29
  107.2 10.0 %collective-permute-start.23 = (bf16[8,3072]{1,0:T(8,128)(2,1)S(1)}, bf16[8,3072]{1,0:T(8,128)(2,1)S(1)}, u32[]{:S(2)}, u32[]{:S(2)}) collective-permute-start(bf16[8,3072]{1,0:T(8,128)(2,1)S(1)} %get-tuple-element.47), channel_id=1, source_target_pairs={{0,6},{1,7},{2,4},{3,5},{4,2},{5,3},{6,0},{7,1},{8,14},{9,15},{10,... | collective-permute-start | bytes 147464 | tf_op jit(solution)/shard_map/ppermute | solution.py:29

commit v2 on v1

v2 whole, which is shorter than its diff:
```python
import math

import jax
import jax.numpy as jnp
from jax import lax
from jax.experimental import pallas as pl
from jax.experimental.pallas import tpu as pltpu
from jax.sharding import PartitionSpec as P

BLK = 128
F32 = jnp.float32
BF16 = jnp.bfloat16
VMEM_LIMIT = 12 * 1024 * 1024
VMEM_GRAD = 28 * 1024 * 1024
RING = 24
FETCH_PARTS = (6, 4, 3, 2, 1)
GRAD_PARTS = (24, 16, 12, 8, 6, 4, 3, 2, 1)

slope_const = math.sqrt(2.0 / math.pi)


def gelu_parts(values):
    inner = slope_const * (values + 0.044715 * values * values * values)
    tangent = jnp.tanh(inner)
    value = 0.5 * values * (1.0 + tangent)
    slope = 0.5 * (1.0 + tangent) + 0.5 * values * (1.0 - tangent * tangent) * slope_const * (
        1.0 + 3.0 * 0.044715 * values * values
    )
    return value, slope


def swap(array, axis, size, mask):
    return lax.ppermute(array, axis, [(place, place ^ mask) for place in range(size)])


def call(body, outs, in_specs, args, scratch=(), grid=None, out_specs=None, flops=0, moved=0, limit=VMEM_LIMIT):
    whole = pl.BlockSpec(memory_space=pltpu.VMEM)
    extra = {} if grid is None else {"grid": grid}
    return pl.pallas_call(
        body,
        out_shape=outs,
        in_specs=in_specs,
        out_specs=[whole] * len(outs) if out_specs is None else out_specs,
        scratch_shapes=list(scratch),
        compiler_params=pltpu.CompilerParams(vmem_limit_bytes=limit),
        cost_estimate=pl.CostEstimate(flops=flops, bytes_accessed=moved, transcendentals=0),
        **extra,
    )(*args)


VM = pl.BlockSpec(memory_space=pltpu.VMEM)
SM = pl.BlockSpec(memory_space=pltpu.SMEM)


def shape_of(shape, dtype):
    return jax.ShapeDtypeStruct(shape, dtype)


def dot(left, right, left_dim, right_dim):
    return lax.dot_general(
        left, right, (((left_dim,), (right_dim,)), ((), ())), preferred_element_type=F32
    )


class Slots:
    def __init__(self, mask_shape, capacity):
        self.rows, self.cols = mask_shape
        self.capacity = capacity
        self.even = self.cols % 8 == 0 and self.cols // 4 <= BLK and capacity == self.rows * (self.cols // 4)
        self.group = self.cols // 4 if self.even else 1
        self.groups = capacity // self.group
        self.spare = 0 if self.even else 1

    def index_args(self, mask):
        flat = mask.reshape(-1)
        count = flat.shape[0]
        places = jnp.arange(count, dtype=jnp.int32)
        lane = jnp.arange(self.cols, dtype=jnp.int32)
        within = jnp.sum(jnp.where(lane[None, :] <= lane[:, None], mask[:, None, :], 0), axis=2)
        row_sum = jnp.sum(mask, axis=1)
        line = jnp.arange(self.rows, dtype=jnp.int32)
        before = jnp.sum(jnp.where(line[None, :] < line[:, None], row_sum[None, :], 0), axis=1)
        rank = (within + before[:, None] - 1).reshape(-1)
        slot = jnp.arange(self.capacity, dtype=jnp.int32)
        hit = (rank[None, :] == slot[:, None]) & (flat[None, :] > 0)
        order = jnp.sum(jnp.where(hit, places[None, :], 0), axis=1)
        live = slot < jnp.sum(flat)
        row = jnp.where(live, order // self.cols, self.rows)
        col = jnp.where(live, order % self.cols, self.cols)
        return row, col


def index_kernel(layout, mask_ref, out_ref):
    rows, cols, group = layout.rows, layout.cols, layout.group
    mask = mask_ref[...].astype(F32)
    lower = lax.broadcasted_iota(jnp.int32, (cols, cols), 0)
    upper = lax.broadcasted_iota(jnp.int32, (cols, cols), 1)
    ramp = jnp.where(lower <= upper, 1.0, 0.0).astype(BF16)
    rank = dot(mask.astype(BF16), ramp, 1, 0)
    place = lax.broadcasted_iota(jnp.int32, (rows, cols), 1).astype(F32)
    lane = lax.broadcasted_iota(jnp.int32, (rows, BLK), 1)
    found = jnp.zeros((rows, BLK), F32)
    for slot in range(group):
        hit = (rank == float(slot + 1)) & (mask > 0.0)
        column = jnp.sum(jnp.where(hit, place, 0.0), axis=1, keepdims=True)
        found = jnp.where(lane == slot, column, found)
    out_ref[...] = found.astype(jnp.int32)


def slot_indices(layout, mask):
    if layout.even:
        out = call(
            lambda mask_ref, out_ref: index_kernel(layout, mask_ref, out_ref),
            [shape_of((layout.rows, BLK), jnp.int32)],
            [VM],
            [mask],
        )[0]
        return out, out
    return layout.index_args(mask)


def read_slot(layout, row_ref, col_ref, group, member):
    if layout.even:
        return group, col_ref[group, member]
    return row_ref[group], col_ref[group]


def add_forward(layout, row_ref, col_ref, first, here, source, blocks, total):
    group = layout.group
    for near in range(here):
        if layout.even:
            left = source[first + near]
            width = 2 if group % 2 == 0 else 1
            for member in range(0, group, width):
                place = near * group + member
                right = [blocks[place + more] for more in range(width)]
                right = right[0] if width == 1 else jnp.concatenate(right, axis=1)
                product = dot(left, right, 1, 0)
                for more in range(width):
                    col = col_ref[first + near, member + more]
                    total[col] += product[:, more * BLK : (more + 1) * BLK]
        else:
            row, col = read_slot(layout, row_ref, col_ref, first + near, 0)
            total[col] += dot(source[row], blocks[near], 1, 0)


def add_backward(layout, row_ref, col_ref, first, here, source, blocks, total):
    group = layout.group
    for near in range(here):
        if layout.even:
            width = 2 if group % 2 == 0 else 1
            result = None
            for member in range(0, group, width):
                place = near * group + member
                cols = [col_ref[first + near, member + more] for more in range(width)]
                left = [source[col] for col in cols]
                right = [blocks[place + more] for more in range(width)]
                left = left[0] if width == 1 else jnp.concatenate(left, axis=1)
                right = right[0] if width == 1 else jnp.concatenate(right, axis=1)
                product = dot(left, right, 1, 1)
                result = product if result is None else result + product
            total[first + near] = result
        else:
            row, col = read_slot(layout, row_ref, col_ref, first + near, 0)
            total[row] += dot(source[col], blocks[near], 1, 1)


def block_products(layout, row_ref, col_ref, first, here, left, right, out):
    group = layout.group
    for near in range(here):
        if layout.even:
            turned = left[first + near].T
            width = 2 if group % 2 == 0 else 1
            for member in range(0, group, width):
                place = near * group + member
                cols = [col_ref[first + near, member + more] for more in range(width)]
                wide = [right[col] for col in cols]
                wide = wide[0] if width == 1 else jnp.concatenate(wide, axis=1)
                product = dot(turned, wide, 1, 0)
                for more in range(width):
                    out[place + more] = product[:, more * BLK : (more + 1) * BLK]
        else:
            row, col = read_slot(layout, row_ref, col_ref, first + near, 0)
            live = row < layout.rows
            product = dot(left[row].T, right[col], 1, 0)
            out[near] = jnp.where(live, product, 0.0)


def gather_model(me, shards, which, stage, full):
    piece = shards[0].shape[1]
    for mask, shard in enumerate(shards):
        start = pl.multiple_of((me ^ mask) * piece, piece)
        stage[pl.ds(start, piece), :] = shard[which].astype(F32)
    for block in range(shards[0].shape[2] // BLK):
        full[block] = stage[:, block * BLK : (block + 1) * BLK].astype(full.dtype)


def gather_hidden(me, shares, full):
    blocks, piece, _ = shares[0].shape
    for mask, share in enumerate(shares):
        start = pl.multiple_of((me ^ mask) * piece, piece)
        full[pl.ds(0, blocks), pl.ds(start, piece), :] = share[...]


def parts_of(layout, choices):
    parts = next(parts for parts in choices if layout.groups % parts == 0)
    return parts, layout.groups // parts, layout.capacity // parts


def apply_cost(layout, tokens):
    return 2 * layout.capacity * BLK * BLK * tokens, 2 * layout.capacity * BLK * BLK


def together(first, second):
    def body(first_ref, second_ref, out_ref):
        out_ref[0] = first_ref[...]
        out_ref[1] = second_ref[...]

    block = pl.BlockSpec(first.shape, lambda step: (0, 0))
    return call(
        body,
        [shape_of((2, *first.shape), first.dtype)],
        [block, block],
        [pltpu.with_memory_space_constraint(array, pltpu.HBM) for array in (first, second)],
        grid=(1,),
        moved=8 * first.size,
    )[0]


def model_to_hidden(layout, rows_cols, shards, which, blocks, forward, hidden_blocks, n_row, after=()):
    count = len(shards)
    _, part, width = shards[0].shape
    tokens = part * count
    model_blocks = width // BLK
    piece = tokens // n_row
    spare = layout.spare
    parts, here, size = parts_of(layout, FETCH_PARTS)

    def body(row_ref, col_ref, *refs):
        shard_refs = refs[:count]
        weights, own, *sends, whole, held, stage, full, total, done = refs[count + len(after) :]
        places = [pl.ds(part * size, size) for part in range(parts)]
        copies = [
            pltpu.make_async_copy(weights.at[place], held.at[place], done.at[part])
            for part, place in enumerate(places)
        ]
        for copy in copies:
            copy.start()
        gather_model(lax.axis_index("col"), shard_refs, which, stage, full)
        if spare:
            full[model_blocks] = jnp.zeros((tokens, BLK), BF16)
        if forward or spare:
            total[...] = jnp.zeros_like(total)
        whole[...] = full[pl.ds(0, model_blocks)]
        work = add_forward if forward else add_backward
        for part, place in enumerate(places):
            copies[part].wait()
            work(layout, row_ref, col_ref, part * here, here, full, held.at[place], total)
        me = lax.axis_index("row")
        for mask, out in enumerate([own] + sends):
            start = pl.multiple_of((me ^ mask) * piece, piece)
            out[...] = total[pl.ds(0, hidden_blocks), pl.ds(start, piece), :].astype(out.dtype)

    share = (hidden_blocks, piece, BLK)
    outs = [shape_of(share, F32)] + [shape_of(share, BF16)] * (n_row - 1)
    outs += [shape_of((model_blocks, tokens, BLK), BF16), pltpu.VMEM(blocks.shape, blocks.dtype)]
    flops, moved = apply_cost(layout, tokens)
    args = [*rows_cols, *shards, *after, pltpu.with_memory_space_constraint(blocks, pltpu.HBM)]
    own, *sends, whole, held = call(
        body,
        outs,
        [SM, SM] + [VM] * (len(args) - 3) + [pl.BlockSpec(memory_space=pltpu.HBM)],
        args,
        scratch=[
            pltpu.VMEM((tokens, width), F32),
            pltpu.VMEM((model_blocks + spare, tokens, BLK), BF16),
            pltpu.VMEM((hidden_blocks + spare, tokens, BLK), F32),
            pltpu.SemaphoreType.DMA((parts,)),
        ],
        flops=flops,
        moved=moved,
    )
    return own, sends, whole, held


def hidden_to_model(layout, rows_cols, shares, blocks, forward, model_blocks, n_col, other=None, after=()):
    count = len(shares)
    hidden_blocks, part, _ = shares[0].shape
    tokens = part * count
    piece = tokens // n_col
    half = n_col // 2
    spare = layout.spare
    grads = other is not None

    def body(row_ref, col_ref, *refs):
        share_refs, refs = refs[:count], refs[count + len(after) :]
        if grads:
            other_ref, weights, keep, send, token, grad, full, total, other_full, made, done = refs
            token[...] = jnp.zeros_like(token)
        else:
            weights, keep, send, full, total = refs
        gather_hidden(lax.axis_index("row"), share_refs, full)
        if spare:
            full[hidden_blocks] = jnp.zeros((tokens, BLK), BF16)
        if forward or spare:
            total[...] = jnp.zeros_like(total)
        if grads:
            if spare:
                other_full[pl.ds(0, model_blocks)] = other_ref[...]
                other_full[model_blocks] = jnp.zeros((tokens, BLK), BF16)
                other_ref = other_full
            copies = send_products(layout, row_ref, col_ref, full, other_ref, made, grad, done)
        work = add_forward if forward else add_backward
        work(layout, row_ref, col_ref, 0, layout.groups, full, weights, total)
        me = lax.axis_index("col")
        for entry in range(half):
            mine = pl.multiple_of((me ^ (2 * entry)) * piece, piece)
            theirs = pl.multiple_of((me ^ (2 * entry + 1)) * piece, piece)
            for block in range(model_blocks):
                lanes = pl.ds(block * BLK, BLK)
                keep[entry, :, lanes] = total[block, pl.ds(mine, piece), :]
                send[entry, :, lanes] = total[block, pl.ds(theirs, piece), :].astype(BF16)
        if grads:
            for copy in copies:
                copy.wait()

    pair = (half, piece, model_blocks * BLK)
    outs = [shape_of(pair, F32), shape_of(pair, BF16)]
    out_specs = [VM] * (4 if grads else 2)
    args = [*rows_cols, *shares, *after]
    scratch = [
        pltpu.VMEM((hidden_blocks + spare, tokens, BLK), BF16),
        pltpu.VMEM((model_blocks + spare, tokens, BLK), F32),
    ]
    flops, moved = apply_cost(layout, tokens)
    if grads:
        outs += [shape_of((8, BLK), F32), shape_of((layout.capacity, BLK, BLK), F32)]
        out_specs[3] = pl.BlockSpec(memory_space=pltpu.HBM)
        args += [other]
        scratch += [
            pltpu.VMEM((model_blocks + spare, tokens, BLK), BF16),
            *ring_scratch(layout),
        ]
        flops, moved = 2 * flops, 3 * moved
    args += [pltpu.with_memory_space_constraint(blocks, pltpu.VMEM)]
    return call(
        body,
        outs,
        [SM, SM] + [VM] * (len(args) - 2),
        args,
        scratch=scratch,
        out_specs=out_specs,
        flops=flops,
        moved=moved,
        limit=VMEM_GRAD if grads else VMEM_LIMIT,
    )


def ring_scratch(layout):
    parts, _, size = parts_of(layout, GRAD_PARTS)
    slots = min(RING, parts)
    return [pltpu.VMEM((slots, size, BLK, BLK), F32), pltpu.SemaphoreType.DMA((slots,))]


def send_products(layout, row_ref, col_ref, left, right, ring, grad, done):
    parts, here, size = parts_of(layout, GRAD_PARTS)
    slots = ring.shape[0]
    copies = []
    for part in range(parts):
        slot = part % slots
        if part >= slots:
            copies[part - slots].wait()
        block_products(layout, row_ref, col_ref, part * here, here, left, right, ring.at[slot])
        place = pl.ds(part * size, size)
        copies.append(pltpu.make_async_copy(ring.at[slot], grad.at[place], done.at[slot]))
        copies[-1].start()
    return copies[-slots:]


def weight_grad(layout, rows_cols, left, shares):
    spare = layout.spare
    count = len(shares)
    left_blocks, tokens, _ = left.shape
    hidden_blocks = shares[0].shape[0]

    def body(row_ref, col_ref, left_ref, *refs):
        share_refs, (grad, sum_ref, made, done, full, *wide) = refs[:count], refs[count:]
        gather_hidden(lax.axis_index("row"), share_refs, full)
        if spare:
            full[hidden_blocks] = jnp.zeros((tokens, BLK), BF16)
            wide[0][pl.ds(0, left_blocks)] = left_ref[...]
            wide[0][left_blocks] = jnp.zeros((tokens, BLK), BF16)
            left_ref = wide[0]
        copies = send_products(layout, row_ref, col_ref, left_ref, full, made, grad, done)
        for block in range(hidden_blocks):
            sum_ref[pl.ds(block, 1), :] = jnp.sum(full[block].astype(F32), axis=0, keepdims=True)
        for copy in copies:
            copy.wait()

    flops, moved = apply_cost(layout, tokens)
    out = shape_of((layout.capacity, BLK, BLK), F32)
    scratch = ring_scratch(layout)
    scratch += [pltpu.VMEM((hidden_blocks + spare, tokens, BLK), BF16)]
    if spare:
        scratch += [pltpu.VMEM((left_blocks + 1, tokens, BLK), BF16)]
    return call(
        body,
        [out, shape_of((hidden_blocks, BLK), F32)],
        [SM, SM, VM] + [VM] * count,
        [*rows_cols, left, *shares],
        scratch=scratch,
        out_specs=[pl.BlockSpec(memory_space=pltpu.HBM), VM],
        flops=flops,
        moved=2 * moved,
        limit=VMEM_GRAD,
    )


def add_up(own_ref, parts):
    total = own_ref[...]
    for part in parts:
        total = total + part[...].astype(F32)
    return total


def activate(own, parts, bias):
    def body(own_ref, bias_ref, *refs):
        parts, (value_ref, slope_ref) = refs[:-2], refs[-2:]
        hidden = add_up(own_ref, parts) + bias_ref[...][:, None, :]
        value, slope = gelu_parts(hidden)
        value_ref[...] = value.astype(BF16)
        slope_ref[...] = slope

    outs = [shape_of(own.shape, BF16), shape_of(own.shape, F32)]
    return call(body, outs, [VM] * (2 + len(parts)), [own, bias, *parts], moved=own.size * 20)


def scale_by_slope(own, parts, slope):
    def body(own_ref, slope_ref, *refs):
        parts, out_ref = refs[:-1], refs[-1]
        out_ref[...] = (add_up(own_ref, parts) * slope_ref[...]).astype(BF16)

    outs = [shape_of(own.shape, BF16)]
    return call(body, outs, [VM] * (2 + len(parts)), [own, slope, *parts], moved=own.size * 16)[0]


def pair_sums(*pairs):
    half, piece, width = pairs[0][0].shape
    count = len(pairs)

    def body(*refs):
        sources, owns, sends = refs[: 2 * count], refs[2 * count : 3 * count], refs[3 * count :]
        for which in range(count):
            keep, came = sources[2 * which : 2 * which + 2]
            owns[which][...] = keep[0] + came[0].astype(F32)
            for entry, send in enumerate(sends, 1):
                send[which] = (keep[entry] + came[entry].astype(F32)).astype(BF16)

    outs = [shape_of((piece, width), F32)] * count + [shape_of((count, piece, width), BF16)] * (half - 1)
    args = [array for pair in pairs for array in pair]
    results = call(body, outs, [VM] * len(args), args, moved=8 * count * half * piece * width)
    return results[:count], results[count:]


def final_sums(owns, parts):
    def body(*refs):
        sources, came, outs = refs[: len(owns)], refs[len(owns) : -len(owns)], refs[-len(owns) :]
        for which, (own, out) in enumerate(zip(sources, outs)):
            total = own[...]
            for part in came:
                total = total + part[which].astype(F32)
            out[...] = total.astype(BF16)

    outs = [shape_of(own.shape, BF16) for own in owns]
    return call(body, outs, [VM] * (len(owns) + len(parts)), [*owns, *parts], moved=8 * sum(own.size for own in owns))


def gather_col(shard, n_col):
    shards = [None] * n_col
    shards[0] = shard
    for mask in range(2, n_col, 2):
        shards[mask] = swap(shard, "col", n_col, mask)
    for mask in range(0, n_col, 2):
        shards[mask + 1] = swap(shards[mask], "col", n_col, 1)
    return shards


def gather_row(share, n_row):
    return [share] + [swap(share, "row", n_row, mask) for mask in range(1, n_row)]


def send_row(sends, n_row):
    return [swap(send, "row", n_row, mask) for mask, send in enumerate(sends, 1)]


def local(n_row, n_col, tokens, cotangent, w1_mask, w1_blocks, bias, w2_mask, w2_blocks):
    first_blocks = w1_blocks[0, 0]
    second_blocks = w2_blocks[0, 0]
    model_blocks, hidden_blocks = w1_mask.shape
    first = Slots(w1_mask.shape, first_blocks.shape[0])
    second = Slots(w2_mask.shape, second_blocks.shape[0])
    first_at, second_at = slot_indices(first, w1_mask), slot_indices(second, w2_mask)
    bias_wide = bias.astype(F32).reshape(hidden_blocks, BLK)

    shards = gather_col(together(tokens, cotangent), n_col)

    hidden_own, hidden_sends, full_tokens, first_held = model_to_hidden(
        first, first_at, shards, 0, first_blocks, True, hidden_blocks, n_row
    )
    hidden_parts = send_row(hidden_sends, n_row)
    act_own, act_sends, full_cotangent, second_held = model_to_hidden(
        second, second_at, shards, 1, second_blocks, False, hidden_blocks, n_row, after=(full_tokens,)
    )
    act_parts = send_row(act_sends, n_row)

    activated, slope = activate(hidden_own, hidden_parts, bias_wide)
    activated_shares = gather_row(activated, n_row)
    grad_hidden = scale_by_slope(act_own, act_parts, slope)
    grad_shares = gather_row(grad_hidden, n_row)

    out_keep, out_send, out_done, w2_grad = hidden_to_model(
        second, second_at, activated_shares, second_held, True, model_blocks, n_col, other=full_cotangent
    )
    out_came = swap(out_send, "col", n_col, 1)
    in_keep, in_send = hidden_to_model(
        first, first_at, grad_shares, first_held, False, model_blocks, n_col, after=(out_done,)
    )
    in_came = swap(in_send, "col", n_col, 1)
    owns, sends = pair_sums((out_keep, out_came), (in_keep, in_came))
    parts = [swap(send, "col", n_col, 2 * entry) for entry, send in enumerate(sends, 1)]
    w1_grad, bias_sum = weight_grad(first, first_at, full_tokens, grad_shares)
    out, tokens_grad = final_sums(owns, parts)
    return (
        out,
        tokens_grad,
        w1_grad[None, None],
        w2_grad[None, None],
        bias_sum.reshape(-1),
    )


def solution(mesh):
    n_row, n_col = mesh.shape["row"], mesh.shape["col"]
    return jax.shard_map(
        lambda *args: local(n_row, n_col, *args),
        mesh=mesh,
        in_specs=(
            P("col", "row"),
            P("col", "row"),
            P("row", "col"),
            P("row", "col", None, None, None),
            P("col"),
            P("col", "row"),
            P("row", "col", None, None, None),
        ),
        out_specs=(
            P("col", "row"),
            P("col", "row"),
            P("row", "col", None, None, None),
            P("row", "col", None, None, None),
            P("col"),
        ),
        check_vma=False,
    )
```

time: 118 us -> 86.7 us (0.73)
  local copies, waits for them, and re-layouts: 14.1 us -> 1.5 us
  waiting for transfers between devices: 30.5 us -> 20.3 us
  starting transfers between devices: 35.3 us -> 27.5 us
    unnamed x21 -> x5, local copies, waits for them, and re-layouts: 14.1 us -> 1.5 us
    ppermute x34 -> x24, waiting for transfers between devices: 30.5 us -> 20.3 us  [swap(): lax.ppermute(array, axis, [(place, place ^ mask) for place in range(size)])]
    ppermute x34 -> x24, starting transfers between devices: 35.3 us -> 27.5 us  [swap(): lax.ppermute(array, axis, [(place, place ^ mask) for place in range(size)])]
  transfers between devices with their start and end apart: 34 -> 24, of which waited for: 9 -> 6; matrix products, arithmetic and copies ran while one was open for 1% -> 1% of each run, Pallas kernels for 27% -> 34%
where the time goes in v2:
time: 86.7 us; the launch traced here: 86.4 us
  Pallas kernels  36.3 us (42%)
  starting transfers between devices  27.5 us (32%)
  waiting for transfers between devices  20.3 us (23%)
  local copies, waits for them, and re-layouts  1.5 us (2%)
    pallas_call x12, Pallas kernels, call(): pl.pallas_call(body, out_shape=outs, in_specs=in_specs, out_specs=[whole]...  36.3 us
    ppermute x24, starting transfers between devices, swap(): lax.ppermute(array, axis, [(place, place ^ mask) for place in range(size)])  27.5 us
    ppermute x24, waiting for transfers between devices, swap(): lax.ppermute(array, axis, [(place, place ^ mask) for place in range(size)])  20.3 us
  transfers between devices with their start and end apart: 24, of which 6 were waited for; matrix products, arithmetic and copies ran while one was open for 1% of the time, Pallas kernels for 34%

profile of v2, /device:TPU:0, one launch (start us, length us, event | category | flops | bytes accessed | tf_op | source)
XLA Modules:
  0.0 86.4 jit_solution(3464484274406471138)
XLA Ops:
  0.6 0.8 shard_map.112.refs_0_
  1.5 5.1 %collective-permute-start.5 = (bf16[2,8,3072]{2,1,0:T(8,128)(2,1)S(1)}, bf16[2,8,3072]{2,1,0:T(8,128)(2,1)S(1)}, u32[]{:S(2)}, u32[]{:S(2)}) collective-permute-start(bf16[2,8,3072]{2,1,0:T(8,128)(2,1)S(1)} %shard_map.112.refs_0_), channel_id=1, source_target_pairs={{0,6},{1,7},{2,4},{3,5},{4,2},{5,3},{6,0},{7,1},{8,14},{9,15},{10,... | collective-permute-start | bytes 294920 | tf_op jit(solution)/shard_map/ppermute | solution.py:33
  6.6 0.0 collective-permute-start.3
  6.6 0.6 collective-permute-start.1
  7.2 0.0 collective-permute-start
  7.2 3.1 %collective-permute-done.5.refs_6_ = bf16[2,8,3072]{2,1,0:T(8,128)(2,1)S(1)} collective-permute-done((bf16[2,8,3072]{2,1,0:T(8,128)(2,1)S(1)}, bf16[2,8,3072]{2,1,0:T(8,128)(2,1)S(1)}, u32[]{:S(2)}, u32[]{:S(2)}) %collective-permute-start.5) | collective-permute-done | bytes 98336 | tf_op jit(solution)/shard_map/ppermute | solution.py:33
  10.3 0.0 collective-permute-start.6
  10.3 4.6 %collective-permute-done.3.refs_4_ = bf16[2,8,3072]{2,1,0:T(8,128)(2,1)S(1)} collective-permute-done((bf16[2,8,3072]{2,1,0:T(8,128)(2,1)S(1)}, bf16[2,8,3072]{2,1,0:T(8,128)(2,1)S(1)}, u32[]{:S(2)}, u32[]{:S(2)}) %collective-permute-start.3) | collective-permute-done | bytes 98336 | tf_op jit(solution)/shard_map/ppermute | solution.py:33
  14.8 0.0 collective-permute-start.4
  14.8 0.0 collective-permute-done.1.refs_2_
  14.8 0.5 collective-permute-start.2
  15.3 0.7 copy-done
  16.0 0.2 shard_map.111.row_ref.col_ref
  16.3 0.8 copy.12.mask_ref
  17.1 0.2 shard_map.110.row_ref.col_ref
  17.3 0.0 collective-permute-done.refs_1_
  17.3 0.0 collective-permute-done.6.refs_7_
  17.3 0.0 collective-permute-done.4.refs_5_
  17.3 0.0 collective-permute-done.2.refs_3_
  17.4 0.0 copy-start.1
  17.4 5.3 %shard_map.113 = (f32[48,16,128]{2,1,0:T(8,128)S(1)}, bf16[48,16,128]{2,1,0:T(8,128)(2,1)S(1)}, bf16[48,16,128]{2,1,0:T(8,128)(2,1)S(1)}, bf16[48,16,128]{2,1,0:...) custom-call(s32[24,128]{1,0:T(8,128)S(1)} %shard_map.111.row_ref.col_ref, ...), custom_call_target="tpu_custom_call" | custom-call | flops 603979776 | bytes 9437184 | tf_op jit(solution)/shard_map/pallas_call | solution.py:39
  22.7 1.6 %collective-permute-start.7 = (bf16[48,16,128]{2,1,0:T(8,128)(2,1)S(1)}, bf16[48,16,128]{2,1,0:T(8,128)(2,1)S(1)}, u32[]{:S(2)}, u32[]{:S(2)}) collective-permute-start(bf16[48,16,128]{2,1,0:T(8,128)(2,1)S(1)} %get-tuple-element.35), channel_id=1, source_target_pairs={{0,8},{8,0},{16,24},{24,16},{1,9},{9,1},{17,25},{25,17},{2,10},{10... | collective-permute-start | bytes 589832 | tf_op jit(solution)/shard_map/ppermute | solution.py:33
  24.2 1.5 %collective-permute-start.8 = (bf16[48,16,128]{2,1,0:T(8,128)(2,1)S(1)}, bf16[48,16,128]{2,1,0:T(8,128)(2,1)S(1)}, u32[]{:S(2)}, u32[]{:S(2)}) collective-permute-start(bf16[48,16,128]{2,1,0:T(8,128)(2,1)S(1)} %get-tuple-element.36), channel_id=1, source_target_pairs={{0,16},{8,24},{16,0},{24,8},{1,17},{9,25},{17,1},{25,9},{2,18},{10... | collective-permute-start | bytes 589832 | tf_op jit(solution)/shard_map/ppermute | solution.py:33
  25.8 0.5 collective-permute-start.9
  26.2 6.8 %shard_map.115 = (f32[48,16,128]{2,1,0:T(8,128)S(1)}, bf16[48,16,128]{2,1,0:T(8,128)(2,1)S(1)}, bf16[48,16,128]{2,1,0:T(8,128)(2,1)S(1)}, bf16[48,16,128]{2,1,0:...) custom-call(s32[48,128]{1,0:T(8,128)S(1)} %shard_map.110.row_ref.col_ref, ...), custom_call_target="tpu_custom_call" | custom-call | flops 603979776 | bytes 9437184 | tf_op jit(solution)/shard_map/pallas_call | solution.py:39
  33.1 1.6 %collective-permute-start.14 = (bf16[48,16,128]{2,1,0:T(8,128)(2,1)S(1)}, bf16[48,16,128]{2,1,0:T(8,128)(2,1)S(1)}, u32[]{:S(2)}, u32[]{:S(2)}) collective-permute-start(bf16[48,16,128]{2,1,0:T(8,128)(2,1)S(1)} %get-tuple-element.46), channel_id=1, source_target_pairs={{0,8},{8,0},{16,24},{24,16},{1,9},{9,1},{17,25},{25,17},{2,10},{10... | collective-permute-start | bytes 589832 | tf_op jit(solution)/shard_map/ppermute | solution.py:33
  34.6 0.0 copy-done.1
  34.6 1.6 %collective-permute-start.15 = (bf16[48,16,128]{2,1,0:T(8,128)(2,1)S(1)}, bf16[48,16,128]{2,1,0:T(8,128)(2,1)S(1)}, u32[]{:S(2)}, u32[]{:S(2)}) collective-permute-start(bf16[48,16,128]{2,1,0:T(8,128)(2,1)S(1)} %get-tuple-element.47), channel_id=1, source_target_pairs={{0,16},{8,24},{16,0},{24,8},{1,17},{9,25},{17,1},{25,9},{2,18},{10... | collective-permute-start | bytes 589832 | tf_op jit(solution)/shard_map/ppermute | solution.py:33
  36.2 0.0 collective-permute-done.7.refs_0_
  36.2 0.4 collective-permute-start.16
  36.6 0.0 collective-permute-done.8.refs_1_
  36.6 0.0 collective-permute-done.9.refs_2_
  36.6 0.4 shard_map.114
  37.0 2.6 %collective-permute-start.12 = (bf16[48,16,128]{2,1,0:T(8,128)(2,1)S(1)}, bf16[48,16,128]{2,1,0:T(8,128)(2,1)S(1)}, u32[]{:S(2)}, u32[]{:S(2)}) collective-permute-start(bf16[48,16,128]{2,1,0:T(8,128)(2,1)S(1)} %get-tuple-element.38.refs_0_), channel_id=1, source_target_pairs={{0,24},{8,16},{16,8},{24,0},{1,25},{9,17},{17,9},{25,1},{2,26},{10... | collective-permute-start | bytes 589832 | tf_op jit(solution)/shard_map/ppermute | solution.py:33
  39.6 0.5 collective-permute-start.11
  40.1 0.9 %collective-permute-done.14.refs_0_ = bf16[48,16,128]{2,1,0:T(8,128)(2,1)S(1)} collective-permute-done((bf16[48,16,128]{2,1,0:T(8,128)(2,1)S(1)}, bf16[48,16,128]{2,1,0:T(8,128)(2,1)S(1)}, u32[]{:S(2)}, u32[]{:S(2)}) %collective-permute-start.14) | collective-permute-done | bytes 196640 | tf_op jit(solution)/shard_map/ppermute | solution.py:33
  40.9 1.5 %collective-permute-start.10 = (bf16[48,16,128]{2,1,0:T(8,128)(2,1)S(1)}, bf16[48,16,128]{2,1,0:T(8,128)(2,1)S(1)}, u32[]{:S(2)}, u32[]{:S(2)}) collective-permute-start(bf16[48,16,128]{2,1,0:T(8,128)(2,1)S(1)} %get-tuple-element.38.refs_0_), channel_id=1, source_target_pairs={{0,8},{8,0},{16,24},{24,16},{1,9},{9,1},{17,25},{25,17},{2,10},{10... | collective-permute-start | bytes 589832 | tf_op jit(solution)/shard_map/ppermute | solution.py:33
  42.5 7.0 %collective-permute-done.15.refs_1_ = bf16[48,16,128]{2,1,0:T(8,128)(2,1)S(1)} collective-permute-done((bf16[48,16,128]{2,1,0:T(8,128)(2,1)S(1)}, bf16[48,16,128]{2,1,0:T(8,128)(2,1)S(1)}, u32[]{:S(2)}, u32[]{:S(2)}) %collective-permute-start.15) | collective-permute-done | bytes 196640 | tf_op jit(solution)/shard_map/ppermute | solution.py:33
  49.5 0.0 collective-permute-done.16.refs_2_
  49.5 0.1 shard_map.117.refs_0_
  49.6 2.5 %collective-permute-start.19 = (bf16[48,16,128]{2,1,0:T(8,128)(2,1)S(1)}, bf16[48,16,128]{2,1,0:T(8,128)(2,1)S(1)}, u32[]{:S(2)}, u32[]{:S(2)}) collective-permute-start(bf16[48,16,128]{2,1,0:T(8,128)(2,1)S(1)} %shard_map.117.refs_0_), channel_id=1, source_target_pairs={{0,24},{8,16},{16,8},{24,0},{1,25},{9,17},{17,9},{25,1},{2,26},{10... | collective-permute-start | bytes 589832 | tf_op jit(solution)/shard_map/ppermute | solution.py:33
  52.1 0.6 collective-permute-start.18
  52.8 0.0 collective-permute-done.12.refs_3_
  52.8 1.4 %collective-permute-start.17 = (bf16[48,16,128]{2,1,0:T(8,128)(2,1)S(1)}, bf16[48,16,128]{2,1,0:T(8,128)(2,1)S(1)}, u32[]{:S(2)}, u32[]{:S(2)}) collective-permute-start(bf16[48,16,128]{2,1,0:T(8,128)(2,1)S(1)} %shard_map.117.refs_0_), channel_id=1, source_target_pairs={{0,8},{8,0},{16,24},{24,16},{1,9},{9,1},{17,25},{25,17},{2,10},{10... | collective-permute-start | bytes 589832 | tf_op jit(solution)/shard_map/ppermute | solution.py:33
  54.1 3.6 %collective-permute-done.11.refs_2_ = bf16[48,16,128]{2,1,0:T(8,128)(2,1)S(1)} collective-permute-done((bf16[48,16,128]{2,1,0:T(8,128)(2,1)S(1)}, bf16[48,16,128]{2,1,0:T(8,128)(2,1)S(1)}, u32[]{:S(2)}, u32[]{:S(2)}) %collective-permute-start.11) | collective-permute-done | bytes 196640 | tf_op jit(solution)/shard_map/ppermute | solution.py:33
  57.8 0.0 collective-permute-done.10.refs_1_
  57.8 8.4 %shard_map.116 = (f32[4,8,3072]{2,1,0:T(8,128)S(1)}, bf16[4,8,3072]{2,1,0:T(8,128)(2,1)S(1)}, f32[8,128]{1,0:T(8,128)S(1)}, f32[288,128,128]{2,1,0:T(8,128)}) custom-call(s32[48,128]{1,0:T(8,128)S(1)} %shard_map.110.row_ref.col_ref, s32[48,128]{1,0:T(8,128)S(1)} %shard_map.110.row_ref.col_ref, bf16[48,16,128]{2,1,0:T(8,128)(2,1)S(1)} %get-tuple-element.38.refs_0_, ...), custom_call_target="tpu_custom_call" | custom-call | flops 1207959552 | bytes 28311552 | tf_op jit(solution)/shard_map/pallas_call | solution.py:39
  66.2 0.1 collective-permute-start.13
  66.3 0.0 collective-permute-done.19.refs_3_
  66.3 0.0 collective-permute-done.18.refs_2_
  66.3 0.0 collective-permute-done.17.refs_1_
  66.3 4.6 %shard_map.118 = (f32[4,8,3072]{2,1,0:T(8,128)S(1)}, bf16[4,8,3072]{2,1,0:T(8,128)(2,1)S(1)}) custom-call(s32[24,128]{1,0:T(8,128)S(1)} %shard_map.111.row_ref.col_ref, s32[24,128]{1,0:T(8,128)S(1)} %shard_map.111.row_ref.col_ref, bf16[48,16,128]{2,1,0:T(8,128)(2,1)S(1)} %shard_map.117.refs_0_, bf16[48,16,128]{2,1,0:T(8,128)(2,1)S(1)} %collective-permute-done.17.refs_1_, ...), custom_call_target="tpu_custom_call" | custom-call | flops 603979776 | bytes 9437184 | tf_op jit(solution)/shard_map/pallas_call | solution.py:39
  70.9 0.6 collective-permute-start.20
  71.5 0.0 collective-permute-done.13.refs_1_
  71.5 1.1 %collective-permute-done.20.refs_3_ = bf16[4,8,3072]{2,1,0:T(8,128)(2,1)S(1)} collective-permute-done((bf16[4,8,3072]{2,1,0:T(8,128)(2,1)S(1)}, bf16[4,8,3072]{2,1,0:T(8,128)(2,1)S(1)}, u32[]{:S(2)}, u32[]{:S(2)}) %collective-permute-start.20) | collective-permute-done | bytes 196640 | tf_op jit(solution)/shard_map/ppermute | solution.py:33
  72.5 0.1 shard_map.119
  72.6 0.5 collective-permute-start.21
  73.2 2.6 %collective-permute-start.22 = (bf16[2,8,3072]{2,1,0:T(8,128)(2,1)S(1)}, bf16[2,8,3072]{2,1,0:T(8,128)(2,1)S(1)}, u32[]{:S(2)}, u32[]{:S(2)}) collective-permute-start(bf16[2,8,3072]{2,1,0:T(8,128)(2,1)S(1)} %get-tuple-element.56), channel_id=1, source_target_pairs={{0,4},{1,5},{2,6},{3,7},{4,0},{5,1},{6,2},{7,3},{8,12},{9,13},{10,... | collective-permute-start | bytes 294920 | tf_op jit(solution)/shard_map/ppermute | solution.py:33
  75.8 1.3 %collective-permute-start.23 = (bf16[2,8,3072]{2,1,0:T(8,128)(2,1)S(1)}, bf16[2,8,3072]{2,1,0:T(8,128)(2,1)S(1)}, u32[]{:S(2)}, u32[]{:S(2)}) collective-permute-start(bf16[2,8,3072]{2,1,0:T(8,128)(2,1)S(1)} %get-tuple-element.57), channel_id=1, source_target_pairs={{0,6},{1,7},{2,4},{3,5},{4,2},{5,3},{6,0},{7,1},{8,14},{9,15},{10,... | collective-permute-start | bytes 294920 | tf_op jit(solution)/shard_map/ppermute | solution.py:33
  77.1 8.6 %shard_map.121 = (f32[288,128,128]{2,1,0:T(8,128)}, f32[48,128]{1,0:T(8,128)}) custom-call(s32[24,128]{1,0:T(8,128)S(1)} %shard_map.111.row_ref.col_ref, s32[24,128]{1,0:T(8,128)S(1)} %shard_map.111.row_ref.col_ref, bf16[24,64,128]{2,1,0:T(8,128)(2,1)S(1)} %get-tuple-element.39.refs_8_.left_ref, bf16[48,16,128]{2,1,0:T(8,128)(2,1)S(1)} %shard_map.117.refs_0_, ...), custom_call_target="tpu_custom_call" | custom-call | flops 603979776 | bytes 18874368 | tf_op jit(solution)/shard_map/pallas_call | solution.py:39
  85.7 0.0 collective-permute-done.21.refs_2_
  85.7 0.0 collective-permute-done.22.refs_3_
  85.7 0.0 collective-permute-done.23.refs_4_
  85.7 0.7 shard_map.120
  (2 shorter events, 0.0 us)
Async XLA Ops:
  1.5 8.8 %collective-permute-start.5 = (bf16[2,8,3072]{2,1,0:T(8,128)(2,1)S(1)}, bf16[2,8,3072]{2,1,0:T(8,128)(2,1)S(1)}, u32[]{:S(2)}, u32[]{:S(2)}) collective-permute-start(bf16[2,8,3072]{2,1,0:T(8,128)(2,1)S(1)} %shard_map.112.refs_0_), channel_id=1, source_target_pairs={{0,6},{1,7},{2,4},{3,5},{4,2},{5,3},{6,0},{7,1},{8,14},{9,15},{10,... | collective-permute-start | bytes 294920 | tf_op jit(solution)/shard_map/ppermute | solution.py:33
  6.6 8.3 %collective-permute-start.3 = (bf16[2,8,3072]{2,1,0:T(8,128)(2,1)S(1)}, bf16[2,8,3072]{2,1,0:T(8,128)(2,1)S(1)}, u32[]{:S(2)}, u32[]{:S(2)}) collective-permute-start(bf16[2,8,3072]{2,1,0:T(8,128)(2,1)S(1)} %shard_map.112.refs_0_), channel_id=1, source_target_pairs={{0,4},{1,5},{2,6},{3,7},{4,0},{5,1},{6,2},{7,3},{8,12},{9,13},{10,... | collective-permute-start | bytes 294920 | tf_op jit(solution)/shard_map/ppermute | solution.py:33
  6.6 8.3 %collective-permute-start.1 = (bf16[2,8,3072]{2,1,0:T(8,128)(2,1)S(1)}, bf16[2,8,3072]{2,1,0:T(8,128)(2,1)S(1)}, u32[]{:S(2)}, u32[]{:S(2)}) collective-permute-start(bf16[2,8,3072]{2,1,0:T(8,128)(2,1)S(1)} %shard_map.112.refs_0_), channel_id=1, source_target_pairs={{0,2},{1,3},{2,0},{3,1},{4,6},{5,7},{6,4},{7,5},{8,10},{9,11},{10,... | collective-permute-start | bytes 294920 | tf_op jit(solution)/shard_map/ppermute | solution.py:33
  7.2 10.1 %collective-permute-start = (bf16[2,8,3072]{2,1,0:T(8,128)(2,1)S(1)}, bf16[2,8,3072]{2,1,0:T(8,128)(2,1)S(1)}, u32[]{:S(2)}, u32[]{:S(2)}) collective-permute-start(bf16[2,8,3072]{2,1,0:T(8,128)(2,1)S(1)} %shard_map.112.refs_0_), channel_id=1, source_target_pairs={{0,1},{1,0},{2,3},{3,2},{4,5},{5,4},{6,7},{7,6},{8,9},{9,8},{10,11... | collective-permute-start | bytes 294920 | tf_op jit(solution)/shard_map/ppermute | solution.py:33
  10.3 7.1 %collective-permute-start.6 = (bf16[2,8,3072]{2,1,0:T(8,128)(2,1)S(1)}, bf16[2,8,3072]{2,1,0:T(8,128)(2,1)S(1)}, u32[]{:S(2)}, u32[]{:S(2)}) collective-permute-start(bf16[2,8,3072]{2,1,0:T(8,128)(2,1)S(1)} %collective-permute-done.5.refs_6_), channel_id=1, source_target_pairs={{0,1},{1,0},{2,3},{3,2},{4,5},{5,4},{6,7},{7,6},{8,9},{9,8},{10,11... | collective-permute-start | bytes 294920 | tf_op jit(solution)/shard_map/ppermute | solution.py:33
  14.8 2.5 %collective-permute-start.4 = (bf16[2,8,3072]{2,1,0:T(8,128)(2,1)S(1)}, bf16[2,8,3072]{2,1,0:T(8,128)(2,1)S(1)}, u32[]{:S(2)}, u32[]{:S(2)}) collective-permute-start(bf16[2,8,3072]{2,1,0:T(8,128)(2,1)S(1)} %collective-permute-done.3.refs_4_), channel_id=1, source_target_pairs={{0,1},{1,0},{2,3},{3,2},{4,5},{5,4},{6,7},{7,6},{8,9},{9,8},{10,11... | collective-permute-start | bytes 294920 | tf_op jit(solution)/shard_map/ppermute | solution.py:33
  14.8 2.5 %collective-permute-start.2 = (bf16[2,8,3072]{2,1,0:T(8,128)(2,1)S(1)}, bf16[2,8,3072]{2,1,0:T(8,128)(2,1)S(1)}, u32[]{:S(2)}, u32[]{:S(2)}) collective-permute-start(bf16[2,8,3072]{2,1,0:T(8,128)(2,1)S(1)} %collective-permute-done.1.refs_2_), channel_id=1, source_target_pairs={{0,1},{1,0},{2,3},{3,2},{4,5},{5,4},{6,7},{7,6},{8,9},{9,8},{10,11... | collective-permute-start | bytes 294920 | tf_op jit(solution)/shard_map/ppermute | solution.py:33
  15.3 0.7 copy-start
  17.4 17.3 %copy-start.1 = (bf16[6144]{0:T(1024)(128)(2,1)S(1)}, bf16[6144]{0:T(1024)(128)(2,1)}, u32[]{:S(2)}) copy-start(bf16[6144]{0:T(1024)(128)(2,1)} %param.11) | copy-start | bytes 36868
  22.7 13.5 %collective-permute-start.7 = (bf16[48,16,128]{2,1,0:T(8,128)(2,1)S(1)}, bf16[48,16,128]{2,1,0:T(8,128)(2,1)S(1)}, u32[]{:S(2)}, u32[]{:S(2)}) collective-permute-start(bf16[48,16,128]{2,1,0:T(8,128)(2,1)S(1)} %get-tuple-element.35), channel_id=1, source_target_pairs={{0,8},{8,0},{16,24},{24,16},{1,9},{9,1},{17,25},{25,17},{2,10},{10... | collective-permute-start | bytes 589832 | tf_op jit(solution)/shard_map/ppermute | solution.py:33
  24.2 12.4 %collective-permute-start.8 = (bf16[48,16,128]{2,1,0:T(8,128)(2,1)S(1)}, bf16[48,16,128]{2,1,0:T(8,128)(2,1)S(1)}, u32[]{:S(2)}, u32[]{:S(2)}) collective-permute-start(bf16[48,16,128]{2,1,0:T(8,128)(2,1)S(1)} %get-tuple-element.36), channel_id=1, source_target_pairs={{0,16},{8,24},{16,0},{24,8},{1,17},{9,25},{17,1},{25,9},{2,18},{10... | collective-permute-start | bytes 589832 | tf_op jit(solution)/shard_map/ppermute | solution.py:33
  25.8 10.9 %collective-permute-start.9 = (bf16[48,16,128]{2,1,0:T(8,128)(2,1)S(1)}, bf16[48,16,128]{2,1,0:T(8,128)(2,1)S(1)}, u32[]{:S(2)}, u32[]{:S(2)}) collective-permute-start(bf16[48,16,128]{2,1,0:T(8,128)(2,1)S(1)} %get-tuple-element.37), channel_id=1, source_target_pairs={{0,24},{8,16},{16,8},{24,0},{1,25},{9,17},{17,9},{25,1},{2,26},{10... | collective-permute-start | bytes 589832 | tf_op jit(solution)/shard_map/ppermute | solution.py:33
  33.1 7.9 %collective-permute-start.14 = (bf16[48,16,128]{2,1,0:T(8,128)(2,1)S(1)}, bf16[48,16,128]{2,1,0:T(8,128)(2,1)S(1)}, u32[]{:S(2)}, u32[]{:S(2)}) collective-permute-start(bf16[48,16,128]{2,1,0:T(8,128)(2,1)S(1)} %get-tuple-element.46), channel_id=1, source_target_pairs={{0,8},{8,0},{16,24},{24,16},{1,9},{9,1},{17,25},{25,17},{2,10},{10... | collective-permute-start | bytes 589832 | tf_op jit(solution)/shard_map/ppermute | solution.py:33
  34.6 14.9 %collective-permute-start.15 = (bf16[48,16,128]{2,1,0:T(8,128)(2,1)S(1)}, bf16[48,16,128]{2,1,0:T(8,128)(2,1)S(1)}, u32[]{:S(2)}, u32[]{:S(2)}) collective-permute-start(bf16[48,16,128]{2,1,0:T(8,128)(2,1)S(1)} %get-tuple-element.47), channel_id=1, source_target_pairs={{0,16},{8,24},{16,0},{24,8},{1,17},{9,25},{17,1},{25,9},{2,18},{10... | collective-permute-start | bytes 589832 | tf_op jit(solution)/shard_map/ppermute | solution.py:33
  36.2 13.3 %collective-permute-start.16 = (bf16[48,16,128]{2,1,0:T(8,128)(2,1)S(1)}, bf16[48,16,128]{2,1,0:T(8,128)(2,1)S(1)}, u32[]{:S(2)}, u32[]{:S(2)}) collective-permute-start(bf16[48,16,128]{2,1,0:T(8,128)(2,1)S(1)} %get-tuple-element.48), channel_id=1, source_target_pairs={{0,24},{8,16},{16,8},{24,0},{1,25},{9,17},{17,9},{25,1},{2,26},{10... | collective-permute-start | bytes 589832 | tf_op jit(solution)/shard_map/ppermute | solution.py:33
  37.0 15.7 %collective-permute-start.12 = (bf16[48,16,128]{2,1,0:T(8,128)(2,1)S(1)}, bf16[48,16,128]{2,1,0:T(8,128)(2,1)S(1)}, u32[]{:S(2)}, u32[]{:S(2)}) collective-permute-start(bf16[48,16,128]{2,1,0:T(8,128)(2,1)S(1)} %get-tuple-element.38.refs_0_), channel_id=1, source_target_pairs={{0,24},{8,16},{16,8},{24,0},{1,25},{9,17},{17,9},{25,1},{2,26},{10... | collective-permute-start | bytes 589832 | tf_op jit(solution)/shard_map/ppermute | solution.py:33
  39.6 18.2 %collective-permute-start.11 = (bf16[48,16,128]{2,1,0:T(8,128)(2,1)S(1)}, bf16[48,16,128]{2,1,0:T(8,128)(2,1)S(1)}, u32[]{:S(2)}, u32[]{:S(2)}) collective-permute-start(bf16[48,16,128]{2,1,0:T(8,128)(2,1)S(1)} %get-tuple-element.38.refs_0_), channel_id=1, source_target_pairs={{0,16},{8,24},{16,0},{24,8},{1,17},{9,25},{17,1},{25,9},{2,18},{10... | collective-permute-start | bytes 589832 | tf_op jit(solution)/shard_map/ppermute | solution.py:33
  40.9 16.8 %collective-permute-start.10 = (bf16[48,16,128]{2,1,0:T(8,128)(2,1)S(1)}, bf16[48,16,128]{2,1,0:T(8,128)(2,1)S(1)}, u32[]{:S(2)}, u32[]{:S(2)}) collective-permute-start(bf16[48,16,128]{2,1,0:T(8,128)(2,1)S(1)} %get-tuple-element.38.refs_0_), channel_id=1, source_target_pairs={{0,8},{8,0},{16,24},{24,16},{1,9},{9,1},{17,25},{25,17},{2,10},{10... | collective-permute-start | bytes 589832 | tf_op jit(solution)/shard_map/ppermute | solution.py:33
  49.6 16.6 %collective-permute-start.19 = (bf16[48,16,128]{2,1,0:T(8,128)(2,1)S(1)}, bf16[48,16,128]{2,1,0:T(8,128)(2,1)S(1)}, u32[]{:S(2)}, u32[]{:S(2)}) collective-permute-start(bf16[48,16,128]{2,1,0:T(8,128)(2,1)S(1)} %shard_map.117.refs_0_), channel_id=1, source_target_pairs={{0,24},{8,16},{16,8},{24,0},{1,25},{9,17},{17,9},{25,1},{2,26},{10... | collective-permute-start | bytes 589832 | tf_op jit(solution)/shard_map/ppermute | solution.py:33
  52.1 14.1 %collective-permute-start.18 = (bf16[48,16,128]{2,1,0:T(8,128)(2,1)S(1)}, bf16[48,16,128]{2,1,0:T(8,128)(2,1)S(1)}, u32[]{:S(2)}, u32[]{:S(2)}) collective-permute-start(bf16[48,16,128]{2,1,0:T(8,128)(2,1)S(1)} %shard_map.117.refs_0_), channel_id=1, source_target_pairs={{0,16},{8,24},{16,0},{24,8},{1,17},{9,25},{17,1},{25,9},{2,18},{10... | collective-permute-start | bytes 589832 | tf_op jit(solution)/shard_map/ppermute | solution.py:33
  52.8 13.5 %collective-permute-start.17 = (bf16[48,16,128]{2,1,0:T(8,128)(2,1)S(1)}, bf16[48,16,128]{2,1,0:T(8,128)(2,1)S(1)}, u32[]{:S(2)}, u32[]{:S(2)}) collective-permute-start(bf16[48,16,128]{2,1,0:T(8,128)(2,1)S(1)} %shard_map.117.refs_0_), channel_id=1, source_target_pairs={{0,8},{8,0},{16,24},{24,16},{1,9},{9,1},{17,25},{25,17},{2,10},{10... | collective-permute-start | bytes 589832 | tf_op jit(solution)/shard_map/ppermute | solution.py:33
  66.2 5.3 %collective-permute-start.13 = (bf16[4,8,3072]{2,1,0:T(8,128)(2,1)S(1)}, bf16[4,8,3072]{2,1,0:T(8,128)(2,1)S(1)}, u32[]{:S(2)}, u32[]{:S(2)}) collective-permute-start(bf16[4,8,3072]{2,1,0:T(8,128)(2,1)S(1)} %get-tuple-element.43), channel_id=1, source_target_pairs={{0,1},{1,0},{2,3},{3,2},{4,5},{5,4},{6,7},{7,6},{8,9},{9,8},{10,11... | collective-permute-start | bytes 589832 | tf_op jit(solution)/shard_map/ppermute | solution.py:33
  70.9 1.6 %collective-permute-start.20 = (bf16[4,8,3072]{2,1,0:T(8,128)(2,1)S(1)}, bf16[4,8,3072]{2,1,0:T(8,128)(2,1)S(1)}, u32[]{:S(2)}, u32[]{:S(2)}) collective-permute-start(bf16[4,8,3072]{2,1,0:T(8,128)(2,1)S(1)} %get-tuple-element.52), channel_id=1, source_target_pairs={{0,1},{1,0},{2,3},{3,2},{4,5},{5,4},{6,7},{7,6},{8,9},{9,8},{10,11... | collective-permute-start | bytes 589832 | tf_op jit(solution)/shard_map/ppermute | solution.py:33
  72.6 13.0 %collective-permute-start.21 = (bf16[2,8,3072]{2,1,0:T(8,128)(2,1)S(1)}, bf16[2,8,3072]{2,1,0:T(8,128)(2,1)S(1)}, u32[]{:S(2)}, u32[]{:S(2)}) collective-permute-start(bf16[2,8,3072]{2,1,0:T(8,128)(2,1)S(1)} %get-tuple-element.55), channel_id=1, source_target_pairs={{0,2},{1,3},{2,0},{3,1},{4,6},{5,7},{6,4},{7,5},{8,10},{9,11},{10,... | collective-permute-start | bytes 294920 | tf_op jit(solution)/shard_map/ppermute | solution.py:33
  73.2 12.5 %collective-permute-start.22 = (bf16[2,8,3072]{2,1,0:T(8,128)(2,1)S(1)}, bf16[2,8,3072]{2,1,0:T(8,128)(2,1)S(1)}, u32[]{:S(2)}, u32[]{:S(2)}) collective-permute-start(bf16[2,8,3072]{2,1,0:T(8,128)(2,1)S(1)} %get-tuple-element.56), channel_id=1, source_target_pairs={{0,4},{1,5},{2,6},{3,7},{4,0},{5,1},{6,2},{7,3},{8,12},{9,13},{10,... | collective-permute-start | bytes 294920 | tf_op jit(solution)/shard_map/ppermute | solution.py:33
  75.8 9.9 %collective-permute-start.23 = (bf16[2,8,3072]{2,1,0:T(8,128)(2,1)S(1)}, bf16[2,8,3072]{2,1,0:T(8,128)(2,1)S(1)}, u32[]{:S(2)}, u32[]{:S(2)}) collective-permute-start(bf16[2,8,3072]{2,1,0:T(8,128)(2,1)S(1)} %get-tuple-element.57), channel_id=1, source_target_pairs={{0,6},{1,7},{2,4},{3,5},{4,2},{5,3},{6,0},{7,1},{8,14},{9,15},{10,... | collective-permute-start | bytes 294920 | tf_op jit(solution)/shard_map/ppermute | solution.py:33

commit v3 on v2

--- a/solution.py
+++ b/solution.py
@@ -13,7 +13,6 @@
 VMEM_LIMIT = 12 * 1024 * 1024
 VMEM_GRAD = 28 * 1024 * 1024
 RING = 24
-FETCH_PARTS = (6, 4, 3, 2, 1)
 GRAD_PARTS = (24, 16, 12, 8, 6, 4, 3, 2, 1)
 
 slope_const = math.sqrt(2.0 / math.pi)
@@ -71,7 +70,8 @@
         self.groups = capacity // self.group
         self.spare = 0 if self.even else 1
 
-    def index_args(self, mask):
+    def uneven_slots(self, mask):
+        self.even, self.group, self.groups, self.spare = False, 1, self.capacity, 1
         flat = mask.reshape(-1)
         count = flat.shape[0]
         places = jnp.arange(count, dtype=jnp.int32)
@@ -90,9 +90,8 @@
         return row, col
 
 
-def index_kernel(layout, mask_ref, out_ref):
+def index_kernel(layout, mask, out_ref):
     rows, cols, group = layout.rows, layout.cols, layout.group
-    mask = mask_ref[...].astype(F32)
     lower = lax.broadcasted_iota(jnp.int32, (cols, cols), 0)
     upper = lax.broadcasted_iota(jnp.int32, (cols, cols), 1)
     ramp = jnp.where(lower <= upper, 1.0, 0.0).astype(BF16)
@@ -107,16 +106,25 @@
     out_ref[...] = found.astype(jnp.int32)
 
 
-def slot_indices(layout, mask):
-    if layout.even:
-        out = call(
-            lambda mask_ref, out_ref: index_kernel(layout, mask_ref, out_ref),
-            [shape_of((layout.rows, BLK), jnp.int32)],
-            [VM],
-            [mask],
-        )[0]
-        return out, out
-    return layout.index_args(mask)
+def slot_indices(layouts, masks):
+    if not all(layout.even for layout in layouts):
+        return [layout.uneven_slots(mask) for layout, mask in zip(layouts, masks)]
+    turned = [layout.rows > layout.cols for layout in layouts]
+    arrays = [mask.T if turn else mask for mask, turn in zip(masks, turned)]
+
+    def body(*refs):
+        for which, (layout, turn) in enumerate(zip(layouts, turned)):
+            mask = refs[which][...].astype(F32)
+            index_kernel(layout, mask.T if turn else mask, refs[len(layouts) + which])
+
+    outs = call(
+        body,
+        [shape_of((layout.rows, BLK), jnp.int32) for layout in layouts],
+        [pl.BlockSpec(array.shape, lambda step: (0, 0)) for array in arrays],
+        [pltpu.with_memory_space_constraint(array, pltpu.HBM) for array in arrays],
+        grid=(1,),
+    )
+    return [(out, out) for out in outs]
 
 
 def read_slot(layout, row_ref, col_ref, group, member):
@@ -227,6 +235,31 @@
     )[0]
 
 
+def fetch(blocks):
+    def body(from_ref, to_ref, token, done):
+        copy = pltpu.make_async_copy(from_ref, to_ref, done)
+        copy.start()
+        token[...] = jnp.zeros_like(token)
+        copy.wait()
+
+    return call(
+        body,
+        [pltpu.VMEM(blocks.shape, blocks.dtype), shape_of((8, BLK), F32)],
+        [pl.BlockSpec(memory_space=pltpu.HBM)],
+        [pltpu.with_memory_space_constraint(blocks, pltpu.HBM)],
+        scratch=[pltpu.SemaphoreType.DMA],
+        moved=4 * blocks.size,
+    )
+
+
+def follow(array, *before):
+    def body(array_ref, *refs):
+        refs[-1][...] = array_ref[...]
+
+    specs = [VM] * (1 + len(before))
+    return call(body, [shape_of(array.shape, array.dtype)], specs, [array, *before], moved=4 * array.size)[0]
+
+
 def model_to_hidden(layout, rows_cols, shards, which, blocks, forward, hidden_blocks, n_row, after=()):
     count = len(shards)
     _, part, width = shards[0].shape
@@ -234,53 +267,42 @@
     model_blocks = width // BLK
     piece = tokens // n_row
     spare = layout.spare
-    parts, here, size = parts_of(layout, FETCH_PARTS)
 
     def body(row_ref, col_ref, *refs):
         shard_refs = refs[:count]
-        weights, own, *sends, whole, held, stage, full, total, done = refs[count + len(after) :]
-        places = [pl.ds(part * size, size) for part in range(parts)]
-        copies = [
-            pltpu.make_async_copy(weights.at[place], held.at[place], done.at[part])
-            for part, place in enumerate(places)
-        ]
-        for copy in copies:
-            copy.start()
+        weights, own, *sends, whole, stage, full, total = refs[count + len(after) :]
         gather_model(lax.axis_index("col"), shard_refs, which, stage, full)
         if spare:
             full[model_blocks] = jnp.zeros((tokens, BLK), BF16)
         if forward or spare:
             total[...] = jnp.zeros_like(total)
-        whole[...] = full[pl.ds(0, model_blocks)]
         work = add_forward if forward else add_backward
-        for part, place in enumerate(places):
-            copies[part].wait()
-            work(layout, row_ref, col_ref, part * here, here, full, held.at[place], total)
+        work(layout, row_ref, col_ref, 0, layout.groups, full, weights, total)
         me = lax.axis_index("row")
         for mask, out in enumerate([own] + sends):
             start = pl.multiple_of((me ^ mask) * piece, piece)
             out[...] = total[pl.ds(0, hidden_blocks), pl.ds(start, piece), :].astype(out.dtype)
+        whole[...] = full[pl.ds(0, model_blocks)]
 
     share = (hidden_blocks, piece, BLK)
     outs = [shape_of(share, F32)] + [shape_of(share, BF16)] * (n_row - 1)
-    outs += [shape_of((model_blocks, tokens, BLK), BF16), pltpu.VMEM(blocks.shape, blocks.dtype)]
+    outs += [shape_of((model_blocks, tokens, BLK), BF16)]
     flops, moved = apply_cost(layout, tokens)
-    args = [*rows_cols, *shards, *after, pltpu.with_memory_space_constraint(blocks, pltpu.HBM)]
-    own, *sends, whole, held = call(
+    args = [*rows_cols, *shards, *after, pltpu.with_memory_space_constraint(blocks, pltpu.VMEM)]
+    own, *sends, whole = call(
         body,
         outs,
-        [SM, SM] + [VM] * (len(args) - 3) + [pl.BlockSpec(memory_space=pltpu.HBM)],
+        [SM, SM] + [VM] * (len(args) - 2),
         args,
         scratch=[
             pltpu.VMEM((tokens, width), F32),
             pltpu.VMEM((model_blocks + spare, tokens, BLK), BF16),
             pltpu.VMEM((hidden_blocks + spare, tokens, BLK), F32),
-            pltpu.SemaphoreType.DMA((parts,)),
         ],
         flops=flops,
         moved=moved,
     )
-    return own, sends, whole, held
+    return own, sends, whole
 
 
 def hidden_to_model(layout, rows_cols, shares, blocks, forward, model_blocks, n_col, other=None, after=()):
@@ -475,11 +497,13 @@
     return call(body, outs, [VM] * (len(owns) + len(parts)), [*owns, *parts], moved=8 * sum(own.size for own in owns))
 
 
-def gather_col(shard, n_col):
+def gather_col(shard, n_col, *before):
     shards = [None] * n_col
     shards[0] = shard
     for mask in range(2, n_col, 2):
         shards[mask] = swap(shard, "col", n_col, mask)
+    for mask in range(2, n_col, 2):
+        shards[mask] = follow(shards[mask], *before)
     for mask in range(0, n_col, 2):
         shards[mask + 1] = swap(shards[mask], "col", n_col, 1)
     return shards
@@ -499,17 +523,19 @@
     model_blocks, hidden_blocks = w1_mask.shape
     first = Slots(w1_mask.shape, first_blocks.shape[0])
     second = Slots(w2_mask.shape, second_blocks.shape[0])
-    first_at, second_at = slot_indices(first, w1_mask), slot_indices(second, w2_mask)
+    first_at, second_at = slot_indices([first, second], [w1_mask, w2_mask])
     bias_wide = bias.astype(F32).reshape(hidden_blocks, BLK)
 
-    shards = gather_col(together(tokens, cotangent), n_col)
-
-    hidden_own, hidden_sends, full_tokens, first_held = model_to_hidden(
-        first, first_at, shards, 0, first_blocks, True, hidden_blocks, n_row
+    first_held, first_there = fetch(first_blocks)
+    second_held, second_there = fetch(second_blocks)
+    shards = gather_col(together(tokens, cotangent), n_col, first_there, second_there)
+
+    hidden_own, hidden_sends, full_tokens = model_to_hidden(
+        first, first_at, shards, 0, first_held, True, hidden_blocks, n_row
     )
     hidden_parts = send_row(hidden_sends, n_row)
-    act_own, act_sends, full_cotangent, second_held = model_to_hidden(
-        second, second_at, shards, 1, second_blocks, False, hidden_blocks, n_row, after=(full_tokens,)
+    act_own, act_sends, full_cotangent = model_to_hidden(
+        second, second_at, shards, 1, second_held, False, hidden_blocks, n_row, after=(full_tokens,)
     )
     act_parts = send_row(act_sends, n_row)
 

time: 86.7 us -> 83.3 us (0.961)
  waiting for transfers between devices: 20.3 us -> 14.8 us
  Pallas kernels: 36.3 us -> 40.4 us
  local copies, waits for them, and re-layouts: 1.5 us -> 0.01 us
    ppermute x24, waiting for transfers between devices: 20.3 us -> 14.8 us  [swap(): lax.ppermute(array, axis, [(place, place ^ mask) for place in range(size)])]
    pallas_call x12 -> x16, Pallas kernels: 36.3 us -> 40.4 us  [call(): pl.pallas_call(body, out_shape=outs, in_specs=in_specs, out_specs=[whole]...]
    unnamed x5 -> x2, local copies, waits for them, and re-layouts: 1.5 us -> 0.01 us
  transfers between devices with their start and end apart: 24 -> 24, of which waited for: 6 -> 5; matrix products, arithmetic and copies ran while one was open for 1% -> 0% of each run, Pallas kernels for 34% -> 43%
where the time goes in v3:
time: 83.3 us; the launch traced here: 83 us
  Pallas kernels  40.4 us (48%)
  starting transfers between devices  27 us (32%)
  waiting for transfers between devices  14.8 us (18%)
  between operations  0.84 us (1%)
    pallas_call x16, Pallas kernels, call(): pl.pallas_call(body, out_shape=outs, in_specs=in_specs, out_specs=[whole]...  40.4 us
    ppermute x24, starting transfers between devices, swap(): lax.ppermute(array, axis, [(place, place ^ mask) for place in range(size)])  27 us
    ppermute x24, waiting for transfers between devices, swap(): lax.ppermute(array, axis, [(place, place ^ mask) for place in range(size)])  14.8 us
  transfers between devices with their start and end apart: 24, of which 5 were waited for; matrix products, arithmetic and copies ran while one was open for 0% of the time, Pallas kernels for 43%

profile of v3, /device:TPU:0, one launch (start us, length us, event | category | flops | bytes accessed | tf_op | source)
XLA Modules:
  0.0 83.0 jit_solution(17387024473930049718)
XLA Ops:
  0.6 0.8 %shard_map.111.refs_0_ = bf16[2,8,3072]{2,1,0:T(8,128)(2,1)S(1)} custom-call(bf16[8,3072]{1,0:T(8,128)(2,1)} %first_ref.1, bf16[8,3072]{1,0:T(8,128)(2,1)} %second_ref.1), custom_call_target="tpu_custom_call" | custom-call | bytes 196608 | tf_op jit(solution)/shard_map/pallas_call | solution.py:38
  1.5 3.1 %collective-permute-start.1 = (bf16[2,8,3072]{2,1,0:T(8,128)(2,1)S(1)}, bf16[2,8,3072]{2,1,0:T(8,128)(2,1)S(1)}, u32[]{:S(2)}, u32[]{:S(2)}) collective-permute-start(bf16[2,8,3072]{2,1,0:T(8,128)(2,1)S(1)} %shard_map.111.refs_0_), channel_id=1, source_target_pairs={{0,2},{1,3},{2,0},{3,1},{4,6},{5,7},{6,4},{7,5},{8,10},{9,11},{10,... | collective-permute-start | bytes 294920 | tf_op jit(solution)/shard_map/ppermute | solution.py:32
  4.5 2.6 %collective-permute-start.3 = (bf16[2,8,3072]{2,1,0:T(8,128)(2,1)S(1)}, bf16[2,8,3072]{2,1,0:T(8,128)(2,1)S(1)}, u32[]{:S(2)}, u32[]{:S(2)}) collective-permute-start(bf16[2,8,3072]{2,1,0:T(8,128)(2,1)S(1)} %shard_map.111.refs_0_), channel_id=1, source_target_pairs={{0,4},{1,5},{2,6},{3,7},{4,0},{5,1},{6,2},{7,3},{8,12},{9,13},{10,... | collective-permute-start | bytes 294920 | tf_op jit(solution)/shard_map/ppermute | solution.py:32
  7.1 0.0 collective-permute-start.5
  7.1 0.0 collective-permute-start
  7.1 3.7 %shard_map.112 = (bf16[288,128,128]{2,1,0:T(8,128)(2,1)S(1)}, f32[8,128]{1,0:T(8,128)S(1)}) custom-call(bf16[288,128,128]{2,1,0:T(8,128)(2,1)} %bitcast.9), custom_call_target="tpu_custom_call" | custom-call | bytes 18874368 | tf_op jit(solution)/shard_map/pallas_call | solution.py:38
  10.8 3.7 %shard_map.113 = (bf16[288,128,128]{2,1,0:T(8,128)(2,1)S(1)}, f32[8,128]{1,0:T(8,128)S(1)}) custom-call(bf16[288,128,128]{2,1,0:T(8,128)(2,1)} %bitcast.10), custom_call_target="tpu_custom_call" | custom-call | bytes 18874368 | tf_op jit(solution)/shard_map/pallas_call | solution.py:38
  14.5 0.0 collective-permute-done.1.array_ref
  14.6 0.6 collective-permute-start.2
  15.1 0.0 collective-permute-done.3.array_ref
  15.1 0.1 collective-permute-start.4
  15.2 0.0 collective-permute-done.5.array_ref
  15.2 0.5 collective-permute-start.6
  15.8 1.0 %shard_map.110 = (s32[24,128]{1,0:T(8,128)S(1)}, s32[48,128]{1,0:T(8,128)S(1)}) custom-call(s32[24,48]{1,0:T(8,128)} %refs_0_.1, s32[24,48]{1,0:T(8,128)} %bitcast.11), custom_call_target="tpu_custom_call" | custom-call | tf_op jit(solution)/shard_map/pallas_call | solution.py:38
  16.8 0.0 collective-permute-done.refs_1_
  16.8 0.0 collective-permute-done.2.refs_3_
  16.8 0.0 collective-permute-done.4.refs_5_
  16.9 0.0 collective-permute-done.6.refs_7_
  16.9 0.0 copy-start
  16.9 3.5 %shard_map.117 = (f32[48,16,128]{2,1,0:T(8,128)S(1)}, bf16[48,16,128]{2,1,0:T(8,128)(2,1)S(1)}, bf16[48,16,128]{2,1,0:T(8,128)(2,1)S(1)}, bf16[48,16,128]{2,1,0:T(8,128)(2,1)S(1)}, bf16[24,64,128]{2,1,0:T(8,128)(2,1)S(1)}) custom-call(s32[24,128]{1,0:T(8,128)S(1)} %get-tuple-element.39.row_ref.col_ref, s32[24,128]{1,0:T(8,128)S(1)} %get-tuple-element.39.row_ref.col_ref, ...), custom_call_target="tpu_custom_call" | custom-call | flops 603979776 | bytes 9437184 | tf_op jit(solution)/shard_map/pallas_call | solution.py:38
  20.4 1.8 %collective-permute-start.7 = (bf16[48,16,128]{2,1,0:T(8,128)(2,1)S(1)}, bf16[48,16,128]{2,1,0:T(8,128)(2,1)S(1)}, u32[]{:S(2)}, u32[]{:S(2)}) collective-permute-start(bf16[48,16,128]{2,1,0:T(8,128)(2,1)S(1)} %get-tuple-element.44), channel_id=1, source_target_pairs={{0,8},{8,0},{16,24},{24,16},{1,9},{9,1},{17,25},{25,17},{2,10},{10... | collective-permute-start | bytes 589832 | tf_op jit(solution)/shard_map/ppermute | solution.py:32
  22.2 1.5 %collective-permute-start.8 = (bf16[48,16,128]{2,1,0:T(8,128)(2,1)S(1)}, bf16[48,16,128]{2,1,0:T(8,128)(2,1)S(1)}, u32[]{:S(2)}, u32[]{:S(2)}) collective-permute-start(bf16[48,16,128]{2,1,0:T(8,128)(2,1)S(1)} %get-tuple-element.45), channel_id=1, source_target_pairs={{0,16},{8,24},{16,0},{24,8},{1,17},{9,25},{17,1},{25,9},{2,18},{10... | collective-permute-start | bytes 589832 | tf_op jit(solution)/shard_map/ppermute | solution.py:32
  23.7 0.3 collective-permute-start.9
  24.0 4.8 %shard_map.119 = (f32[48,16,128]{2,1,0:T(8,128)S(1)}, bf16[48,16,128]{2,1,0:T(8,128)(2,1)S(1)}, bf16[48,16,128]{2,1,0:T(8,128)(2,1)S(1)}, bf16[48,16,128]{2,1,0:T(8,128)(2,1)S(1)}, bf16[24,64,128]{2,1,0:T(8,128)(2,1)S(1)}) custom-call(s32[48,128]{1,0:T(8,128)S(1)} %get-tuple-element.38.row_ref.col_ref, s32[48,128]{1,0:T(8,128)S(1)} %get-tuple-element.38.row_ref.col_ref, ...), custom_call_target="tpu_custom_call" | custom-call | flops 603979776 | bytes 9437184 | tf_op jit(solution)/shard_map/pallas_call | solution.py:38
  28.8 1.8 %collective-permute-start.14 = (bf16[48,16,128]{2,1,0:T(8,128)(2,1)S(1)}, bf16[48,16,128]{2,1,0:T(8,128)(2,1)S(1)}, u32[]{:S(2)}, u32[]{:S(2)}) collective-permute-start(bf16[48,16,128]{2,1,0:T(8,128)(2,1)S(1)} %get-tuple-element.55), channel_id=1, source_target_pairs={{0,8},{8,0},{16,24},{24,16},{1,9},{9,1},{17,25},{25,17},{2,10},{10... | collective-permute-start | bytes 589832 | tf_op jit(solution)/shard_map/ppermute | solution.py:32
  30.6 0.0 copy-done
  30.6 1.6 %collective-permute-start.15 = (bf16[48,16,128]{2,1,0:T(8,128)(2,1)S(1)}, bf16[48,16,128]{2,1,0:T(8,128)(2,1)S(1)}, u32[]{:S(2)}, u32[]{:S(2)}) collective-permute-start(bf16[48,16,128]{2,1,0:T(8,128)(2,1)S(1)} %get-tuple-element.56), channel_id=1, source_target_pairs={{0,16},{8,24},{16,0},{24,8},{1,17},{9,25},{17,1},{25,9},{2,18},{10... | collective-permute-start | bytes 589832 | tf_op jit(solution)/shard_map/ppermute | solution.py:32
  32.1 0.0 collective-permute-done.7.refs_0_
  32.2 0.2 collective-permute-start.16
  32.4 0.5 collective-permute-done.8.refs_1_
  32.9 0.8 collective-permute-done.9.refs_2_
  33.6 0.4 shard_map.118
  34.0 1.5 %collective-permute-start.12 = (bf16[48,16,128]{2,1,0:T(8,128)(2,1)S(1)}, bf16[48,16,128]{2,1,0:T(8,128)(2,1)S(1)}, u32[]{:S(2)}, u32[]{:S(2)}) collective-permute-start(bf16[48,16,128]{2,1,0:T(8,128)(2,1)S(1)} %get-tuple-element.47.refs_0_), channel_id=1, source_target_pairs={{0,24},{8,16},{16,8},{24,0},{1,25},{9,17},{17,9},{25,1},{2,26},{10... | collective-permute-start | bytes 589832 | tf_op jit(solution)/shard_map/ppermute | solution.py:32
  35.5 1.4 %collective-permute-start.11 = (bf16[48,16,128]{2,1,0:T(8,128)(2,1)S(1)}, bf16[48,16,128]{2,1,0:T(8,128)(2,1)S(1)}, u32[]{:S(2)}, u32[]{:S(2)}) collective-permute-start(bf16[48,16,128]{2,1,0:T(8,128)(2,1)S(1)} %get-tuple-element.47.refs_0_), channel_id=1, source_target_pairs={{0,16},{8,24},{16,0},{24,8},{1,17},{9,25},{17,1},{25,9},{2,18},{10... | collective-permute-start | bytes 589832 | tf_op jit(solution)/shard_map/ppermute | solution.py:32
  37.0 0.0 collective-permute-done.14.refs_0_
  37.0 1.4 %collective-permute-start.10 = (bf16[48,16,128]{2,1,0:T(8,128)(2,1)S(1)}, bf16[48,16,128]{2,1,0:T(8,128)(2,1)S(1)}, u32[]{:S(2)}, u32[]{:S(2)}) collective-permute-start(bf16[48,16,128]{2,1,0:T(8,128)(2,1)S(1)} %get-tuple-element.47.refs_0_), channel_id=1, source_target_pairs={{0,8},{8,0},{16,24},{24,16},{1,9},{9,1},{17,25},{25,17},{2,10},{10... | collective-permute-start | bytes 589832 | tf_op jit(solution)/shard_map/ppermute | solution.py:32
  38.4 8.2 %collective-permute-done.15.refs_1_ = bf16[48,16,128]{2,1,0:T(8,128)(2,1)S(1)} collective-permute-done((bf16[48,16,128]{2,1,0:T(8,128)(2,1)S(1)}, bf16[48,16,128]{2,1,0:T(8,128)(2,1)S(1)}, u32[]{:S(2)}, u32[]{:S(2)}) %collective-permute-start.15) | collective-permute-done | bytes 196640 | tf_op jit(solution)/shard_map/ppermute | solution.py:32
  46.6 0.0 collective-permute-done.16.refs_2_
  46.6 0.1 shard_map.121.refs_0_
  46.7 1.6 %collective-permute-start.19 = (bf16[48,16,128]{2,1,0:T(8,128)(2,1)S(1)}, bf16[48,16,128]{2,1,0:T(8,128)(2,1)S(1)}, u32[]{:S(2)}, u32[]{:S(2)}) collective-permute-start(bf16[48,16,128]{2,1,0:T(8,128)(2,1)S(1)} %shard_map.121.refs_0_), channel_id=1, source_target_pairs={{0,24},{8,16},{16,8},{24,0},{1,25},{9,17},{17,9},{25,1},{2,26},{10... | collective-permute-start | bytes 589832 | tf_op jit(solution)/shard_map/ppermute | solution.py:32
  48.3 0.4 collective-permute-start.18
  48.7 0.0 collective-permute-done.12.refs_3_
  48.7 1.6 %collective-permute-start.17 = (bf16[48,16,128]{2,1,0:T(8,128)(2,1)S(1)}, bf16[48,16,128]{2,1,0:T(8,128)(2,1)S(1)}, u32[]{:S(2)}, u32[]{:S(2)}) collective-permute-start(bf16[48,16,128]{2,1,0:T(8,128)(2,1)S(1)} %shard_map.121.refs_0_), channel_id=1, source_target_pairs={{0,8},{8,0},{16,24},{24,16},{1,9},{9,1},{17,25},{25,17},{2,10},{10... | collective-permute-start | bytes 589832 | tf_op jit(solution)/shard_map/ppermute | solution.py:32
  50.3 4.2 %collective-permute-done.11.refs_2_ = bf16[48,16,128]{2,1,0:T(8,128)(2,1)S(1)} collective-permute-done((bf16[48,16,128]{2,1,0:T(8,128)(2,1)S(1)}, bf16[48,16,128]{2,1,0:T(8,128)(2,1)S(1)}, u32[]{:S(2)}, u32[]{:S(2)}) %collective-permute-start.11) | collective-permute-done | bytes 196640 | tf_op jit(solution)/shard_map/ppermute | solution.py:32
  54.5 0.0 collective-permute-done.10.refs_1_
  54.5 8.4 %shard_map.120 = (f32[4,8,3072]{2,1,0:T(8,128)S(1)}, bf16[4,8,3072]{2,1,0:T(8,128)(2,1)S(1)}, f32[8,128]{1,0:T(8,128)S(1)}, f32[288,128,128]{2,1,0:T(8,128)}) custom-call(s32[48,128]{1,0:T(8,128)S(1)} %get-tuple-element.38.row_ref.col_ref, s32[48,128]{1,0:T(8,128)S(1)} %get-tuple-element.38.row_ref.col_ref, ...), custom_call_target="tpu_custom_call" | custom-call | flops 1207959552 | bytes 28311552 | tf_op jit(solution)/shard_map/pallas_call | solution.py:38
  62.9 0.1 collective-permute-start.13
  62.9 0.0 collective-permute-done.19.refs_3_
  62.9 0.0 collective-permute-done.18.refs_2_
  63.0 0.0 collective-permute-done.17.refs_1_
  63.0 4.6 %shard_map.122 = (f32[4,8,3072]{2,1,0:T(8,128)S(1)}, bf16[4,8,3072]{2,1,0:T(8,128)(2,1)S(1)}) custom-call(s32[24,128]{1,0:T(8,128)S(1)} %get-tuple-element.39.row_ref.col_ref, s32[24,128]{1,0:T(8,128)S(1)} %get-tuple-element.39.row_ref.col_ref, bf16[48,16,128]{2,1,0:T(8,128)(2,1)S(1)} %shard_map.121.refs_0_, ...), custom_call_target="tpu_custom_call" | custom-call | flops 603979776 | bytes 9437184 | tf_op jit(solution)/shard_map/pallas_call | solution.py:38
  67.6 0.5 collective-permute-start.20
  68.1 0.0 collective-permute-done.13.refs_1_
  68.1 1.1 %collective-permute-done.20.refs_3_ = bf16[4,8,3072]{2,1,0:T(8,128)(2,1)S(1)} collective-permute-done((bf16[4,8,3072]{2,1,0:T(8,128)(2,1)S(1)}, bf16[4,8,3072]{2,1,0:T(8,128)(2,1)S(1)}, u32[]{:S(2)}, u32[]{:S(2)}) %collective-permute-start.20) | collective-permute-done | bytes 196640 | tf_op jit(solution)/shard_map/ppermute | solution.py:32
  69.2 0.1 shard_map.123
  69.3 0.9 %collective-permute-start.21 = (bf16[2,8,3072]{2,1,0:T(8,128)(2,1)S(1)}, bf16[2,8,3072]{2,1,0:T(8,128)(2,1)S(1)}, u32[]{:S(2)}, u32[]{:S(2)}) collective-permute-start(bf16[2,8,3072]{2,1,0:T(8,128)(2,1)S(1)} %get-tuple-element.63), channel_id=1, source_target_pairs={{0,2},{1,3},{2,0},{3,1},{4,6},{5,7},{6,4},{7,5},{8,10},{9,11},{10,... | collective-permute-start | bytes 294920 | tf_op jit(solution)/shard_map/ppermute | solution.py:32
  70.2 3.3 %collective-permute-start.22 = (bf16[2,8,3072]{2,1,0:T(8,128)(2,1)S(1)}, bf16[2,8,3072]{2,1,0:T(8,128)(2,1)S(1)}, u32[]{:S(2)}, u32[]{:S(2)}) collective-permute-start(bf16[2,8,3072]{2,1,0:T(8,128)(2,1)S(1)} %get-tuple-element.64), channel_id=1, source_target_pairs={{0,4},{1,5},{2,6},{3,7},{4,0},{5,1},{6,2},{7,3},{8,12},{9,13},{10,... | collective-permute-start | bytes 294920 | tf_op jit(solution)/shard_map/ppermute | solution.py:32
  73.5 0.2 collective-permute-start.23
  73.8 8.6 %shard_map.125 = (f32[288,128,128]{2,1,0:T(8,128)}, f32[48,128]{1,0:T(8,128)}) custom-call(s32[24,128]{1,0:T(8,128)S(1)} %get-tuple-element.39.row_ref.col_ref, s32[24,128]{1,0:T(8,128)S(1)} %get-tuple-element.39.row_ref.col_ref, bf16[24,64,128]{2,1,0:T(8,128)(2,1)S(1)} %get-tuple-element.48.refs_8_.left_ref, bf16[48,16,128]{2,1,0:T(8,128)(2,1)S(1)} %shard_map.121.refs_0_, ...), custom_call_target="tpu_custom_call" | custom-call | flops 603979776 | bytes 18874368 | tf_op jit(solution)/shard_map/pallas_call | solution.py:38
  82.3 0.0 collective-permute-done.21.refs_2_
  82.3 0.0 collective-permute-done.22.refs_3_
  82.3 0.0 collective-permute-done.23.refs_4_
  82.4 0.7 shard_map.124
  (4 shorter events, 0.0 us)
Async XLA Ops:
  1.5 13.1 %collective-permute-start.1 = (bf16[2,8,3072]{2,1,0:T(8,128)(2,1)S(1)}, bf16[2,8,3072]{2,1,0:T(8,128)(2,1)S(1)}, u32[]{:S(2)}, u32[]{:S(2)}) collective-permute-start(bf16[2,8,3072]{2,1,0:T(8,128)(2,1)S(1)} %shard_map.111.refs_0_), channel_id=1, source_target_pairs={{0,2},{1,3},{2,0},{3,1},{4,6},{5,7},{6,4},{7,5},{8,10},{9,11},{10,... | collective-permute-start | bytes 294920 | tf_op jit(solution)/shard_map/ppermute | solution.py:32
  4.5 10.6 %collective-permute-start.3 = (bf16[2,8,3072]{2,1,0:T(8,128)(2,1)S(1)}, bf16[2,8,3072]{2,1,0:T(8,128)(2,1)S(1)}, u32[]{:S(2)}, u32[]{:S(2)}) collective-permute-start(bf16[2,8,3072]{2,1,0:T(8,128)(2,1)S(1)} %shard_map.111.refs_0_), channel_id=1, source_target_pairs={{0,4},{1,5},{2,6},{3,7},{4,0},{5,1},{6,2},{7,3},{8,12},{9,13},{10,... | collective-permute-start | bytes 294920 | tf_op jit(solution)/shard_map/ppermute | solution.py:32
  7.1 8.1 %collective-permute-start.5 = (bf16[2,8,3072]{2,1,0:T(8,128)(2,1)S(1)}, bf16[2,8,3072]{2,1,0:T(8,128)(2,1)S(1)}, u32[]{:S(2)}, u32[]{:S(2)}) collective-permute-start(bf16[2,8,3072]{2,1,0:T(8,128)(2,1)S(1)} %shard_map.111.refs_0_), channel_id=1, source_target_pairs={{0,6},{1,7},{2,4},{3,5},{4,2},{5,3},{6,0},{7,1},{8,14},{9,15},{10,... | collective-permute-start | bytes 294920 | tf_op jit(solution)/shard_map/ppermute | solution.py:32
  7.1 9.7 %collective-permute-start = (bf16[2,8,3072]{2,1,0:T(8,128)(2,1)S(1)}, bf16[2,8,3072]{2,1,0:T(8,128)(2,1)S(1)}, u32[]{:S(2)}, u32[]{:S(2)}) collective-permute-start(bf16[2,8,3072]{2,1,0:T(8,128)(2,1)S(1)} %shard_map.111.refs_0_), channel_id=1, source_target_pairs={{0,1},{1,0},{2,3},{3,2},{4,5},{5,4},{6,7},{7,6},{8,9},{9,8},{10,11... | collective-permute-start | bytes 294920 | tf_op jit(solution)/shard_map/ppermute | solution.py:32
  14.6 2.3 %collective-permute-start.2 = (bf16[2,8,3072]{2,1,0:T(8,128)(2,1)S(1)}, bf16[2,8,3072]{2,1,0:T(8,128)(2,1)S(1)}, u32[]{:S(2)}, u32[]{:S(2)}) collective-permute-start(bf16[2,8,3072]{2,1,0:T(8,128)(2,1)S(1)} %shard_map.114.refs_2_), channel_id=1, source_target_pairs={{0,1},{1,0},{2,3},{3,2},{4,5},{5,4},{6,7},{7,6},{8,9},{9,8},{10,11... | collective-permute-start | bytes 294920 | tf_op jit(solution)/shard_map/ppermute | solution.py:32
  15.1 1.7 %collective-permute-start.4 = (bf16[2,8,3072]{2,1,0:T(8,128)(2,1)S(1)}, bf16[2,8,3072]{2,1,0:T(8,128)(2,1)S(1)}, u32[]{:S(2)}, u32[]{:S(2)}) collective-permute-start(bf16[2,8,3072]{2,1,0:T(8,128)(2,1)S(1)} %shard_map.115.refs_4_), channel_id=1, source_target_pairs={{0,1},{1,0},{2,3},{3,2},{4,5},{5,4},{6,7},{7,6},{8,9},{9,8},{10,11... | collective-permute-start | bytes 294920 | tf_op jit(solution)/shard_map/ppermute | solution.py:32
  15.2 1.6 %collective-permute-start.6 = (bf16[2,8,3072]{2,1,0:T(8,128)(2,1)S(1)}, bf16[2,8,3072]{2,1,0:T(8,128)(2,1)S(1)}, u32[]{:S(2)}, u32[]{:S(2)}) collective-permute-start(bf16[2,8,3072]{2,1,0:T(8,128)(2,1)S(1)} %shard_map.116.refs_6_), channel_id=1, source_target_pairs={{0,1},{1,0},{2,3},{3,2},{4,5},{5,4},{6,7},{7,6},{8,9},{9,8},{10,11... | collective-permute-start | bytes 294920 | tf_op jit(solution)/shard_map/ppermute | solution.py:32
  16.9 13.7 %copy-start = (bf16[6144]{0:T(1024)(128)(2,1)S(1)}, bf16[6144]{0:T(1024)(128)(2,1)}, u32[]{:S(2)}) copy-start(bf16[6144]{0:T(1024)(128)(2,1)} %param.11) | copy-start | bytes 36868
  20.4 11.8 %collective-permute-start.7 = (bf16[48,16,128]{2,1,0:T(8,128)(2,1)S(1)}, bf16[48,16,128]{2,1,0:T(8,128)(2,1)S(1)}, u32[]{:S(2)}, u32[]{:S(2)}) collective-permute-start(bf16[48,16,128]{2,1,0:T(8,128)(2,1)S(1)} %get-tuple-element.44), channel_id=1, source_target_pairs={{0,8},{8,0},{16,24},{24,16},{1,9},{9,1},{17,25},{25,17},{2,10},{10... | collective-permute-start | bytes 589832 | tf_op jit(solution)/shard_map/ppermute | solution.py:32
  22.2 10.7 %collective-permute-start.8 = (bf16[48,16,128]{2,1,0:T(8,128)(2,1)S(1)}, bf16[48,16,128]{2,1,0:T(8,128)(2,1)S(1)}, u32[]{:S(2)}, u32[]{:S(2)}) collective-permute-start(bf16[48,16,128]{2,1,0:T(8,128)(2,1)S(1)} %get-tuple-element.45), channel_id=1, source_target_pairs={{0,16},{8,24},{16,0},{24,8},{1,17},{9,25},{17,1},{25,9},{2,18},{10... | collective-permute-start | bytes 589832 | tf_op jit(solution)/shard_map/ppermute | solution.py:32
  23.7 9.9 %collective-permute-start.9 = (bf16[48,16,128]{2,1,0:T(8,128)(2,1)S(1)}, bf16[48,16,128]{2,1,0:T(8,128)(2,1)S(1)}, u32[]{:S(2)}, u32[]{:S(2)}) collective-permute-start(bf16[48,16,128]{2,1,0:T(8,128)(2,1)S(1)} %get-tuple-element.46), channel_id=1, source_target_pairs={{0,24},{8,16},{16,8},{24,0},{1,25},{9,17},{17,9},{25,1},{2,26},{10... | collective-permute-start | bytes 589832 | tf_op jit(solution)/shard_map/ppermute | solution.py:32
  28.8 8.2 %collective-permute-start.14 = (bf16[48,16,128]{2,1,0:T(8,128)(2,1)S(1)}, bf16[48,16,128]{2,1,0:T(8,128)(2,1)S(1)}, u32[]{:S(2)}, u32[]{:S(2)}) collective-permute-start(bf16[48,16,128]{2,1,0:T(8,128)(2,1)S(1)} %get-tuple-element.55), channel_id=1, source_target_pairs={{0,8},{8,0},{16,24},{24,16},{1,9},{9,1},{17,25},{25,17},{2,10},{10... | collective-permute-start | bytes 589832 | tf_op jit(solution)/shard_map/ppermute | solution.py:32
  30.6 16.0 %collective-permute-start.15 = (bf16[48,16,128]{2,1,0:T(8,128)(2,1)S(1)}, bf16[48,16,128]{2,1,0:T(8,128)(2,1)S(1)}, u32[]{:S(2)}, u32[]{:S(2)}) collective-permute-start(bf16[48,16,128]{2,1,0:T(8,128)(2,1)S(1)} %get-tuple-element.56), channel_id=1, source_target_pairs={{0,16},{8,24},{16,0},{24,8},{1,17},{9,25},{17,1},{25,9},{2,18},{10... | collective-permute-start | bytes 589832 | tf_op jit(solution)/shard_map/ppermute | solution.py:32
  32.2 14.4 %collective-permute-start.16 = (bf16[48,16,128]{2,1,0:T(8,128)(2,1)S(1)}, bf16[48,16,128]{2,1,0:T(8,128)(2,1)S(1)}, u32[]{:S(2)}, u32[]{:S(2)}) collective-permute-start(bf16[48,16,128]{2,1,0:T(8,128)(2,1)S(1)} %get-tuple-element.57), channel_id=1, source_target_pairs={{0,24},{8,16},{16,8},{24,0},{1,25},{9,17},{17,9},{25,1},{2,26},{10... | collective-permute-start | bytes 589832 | tf_op jit(solution)/shard_map/ppermute | solution.py:32
  34.0 14.7 %collective-permute-start.12 = (bf16[48,16,128]{2,1,0:T(8,128)(2,1)S(1)}, bf16[48,16,128]{2,1,0:T(8,128)(2,1)S(1)}, u32[]{:S(2)}, u32[]{:S(2)}) collective-permute-start(bf16[48,16,128]{2,1,0:T(8,128)(2,1)S(1)} %get-tuple-element.47.refs_0_), channel_id=1, source_target_pairs={{0,24},{8,16},{16,8},{24,0},{1,25},{9,17},{17,9},{25,1},{2,26},{10... | collective-permute-start | bytes 589832 | tf_op jit(solution)/shard_map/ppermute | solution.py:32
  35.5 18.9 %collective-permute-start.11 = (bf16[48,16,128]{2,1,0:T(8,128)(2,1)S(1)}, bf16[48,16,128]{2,1,0:T(8,128)(2,1)S(1)}, u32[]{:S(2)}, u32[]{:S(2)}) collective-permute-start(bf16[48,16,128]{2,1,0:T(8,128)(2,1)S(1)} %get-tuple-element.47.refs_0_), channel_id=1, source_target_pairs={{0,16},{8,24},{16,0},{24,8},{1,17},{9,25},{17,1},{25,9},{2,18},{10... | collective-permute-start | bytes 589832 | tf_op jit(solution)/shard_map/ppermute | solution.py:32
  37.0 17.5 %collective-permute-start.10 = (bf16[48,16,128]{2,1,0:T(8,128)(2,1)S(1)}, bf16[48,16,128]{2,1,0:T(8,128)(2,1)S(1)}, u32[]{:S(2)}, u32[]{:S(2)}) collective-permute-start(bf16[48,16,128]{2,1,0:T(8,128)(2,1)S(1)} %get-tuple-element.47.refs_0_), channel_id=1, source_target_pairs={{0,8},{8,0},{16,24},{24,16},{1,9},{9,1},{17,25},{25,17},{2,10},{10... | collective-permute-start | bytes 589832 | tf_op jit(solution)/shard_map/ppermute | solution.py:32
  46.7 16.2 %collective-permute-start.19 = (bf16[48,16,128]{2,1,0:T(8,128)(2,1)S(1)}, bf16[48,16,128]{2,1,0:T(8,128)(2,1)S(1)}, u32[]{:S(2)}, u32[]{:S(2)}) collective-permute-start(bf16[48,16,128]{2,1,0:T(8,128)(2,1)S(1)} %shard_map.121.refs_0_), channel_id=1, source_target_pairs={{0,24},{8,16},{16,8},{24,0},{1,25},{9,17},{17,9},{25,1},{2,26},{10... | collective-permute-start | bytes 589832 | tf_op jit(solution)/shard_map/ppermute | solution.py:32
  48.3 14.7 %collective-permute-start.18 = (bf16[48,16,128]{2,1,0:T(8,128)(2,1)S(1)}, bf16[48,16,128]{2,1,0:T(8,128)(2,1)S(1)}, u32[]{:S(2)}, u32[]{:S(2)}) collective-permute-start(bf16[48,16,128]{2,1,0:T(8,128)(2,1)S(1)} %shard_map.121.refs_0_), channel_id=1, source_target_pairs={{0,16},{8,24},{16,0},{24,8},{1,17},{9,25},{17,1},{25,9},{2,18},{10... | collective-permute-start | bytes 589832 | tf_op jit(solution)/shard_map/ppermute | solution.py:32
  48.7 14.3 %collective-permute-start.17 = (bf16[48,16,128]{2,1,0:T(8,128)(2,1)S(1)}, bf16[48,16,128]{2,1,0:T(8,128)(2,1)S(1)}, u32[]{:S(2)}, u32[]{:S(2)}) collective-permute-start(bf16[48,16,128]{2,1,0:T(8,128)(2,1)S(1)} %shard_map.121.refs_0_), channel_id=1, source_target_pairs={{0,8},{8,0},{16,24},{24,16},{1,9},{9,1},{17,25},{25,17},{2,10},{10... | collective-permute-start | bytes 589832 | tf_op jit(solution)/shard_map/ppermute | solution.py:32
  62.9 5.3 %collective-permute-start.13 = (bf16[4,8,3072]{2,1,0:T(8,128)(2,1)S(1)}, bf16[4,8,3072]{2,1,0:T(8,128)(2,1)S(1)}, u32[]{:S(2)}, u32[]{:S(2)}) collective-permute-start(bf16[4,8,3072]{2,1,0:T(8,128)(2,1)S(1)} %get-tuple-element.52), channel_id=1, source_target_pairs={{0,1},{1,0},{2,3},{3,2},{4,5},{5,4},{6,7},{7,6},{8,9},{9,8},{10,11... | collective-permute-start | bytes 589832 | tf_op jit(solution)/shard_map/ppermute | solution.py:32
  67.6 1.6 %collective-permute-start.20 = (bf16[4,8,3072]{2,1,0:T(8,128)(2,1)S(1)}, bf16[4,8,3072]{2,1,0:T(8,128)(2,1)S(1)}, u32[]{:S(2)}, u32[]{:S(2)}) collective-permute-start(bf16[4,8,3072]{2,1,0:T(8,128)(2,1)S(1)} %get-tuple-element.60), channel_id=1, source_target_pairs={{0,1},{1,0},{2,3},{3,2},{4,5},{5,4},{6,7},{7,6},{8,9},{9,8},{10,11... | collective-permute-start | bytes 589832 | tf_op jit(solution)/shard_map/ppermute | solution.py:32
  69.3 13.0 %collective-permute-start.21 = (bf16[2,8,3072]{2,1,0:T(8,128)(2,1)S(1)}, bf16[2,8,3072]{2,1,0:T(8,128)(2,1)S(1)}, u32[]{:S(2)}, u32[]{:S(2)}) collective-permute-start(bf16[2,8,3072]{2,1,0:T(8,128)(2,1)S(1)} %get-tuple-element.63), channel_id=1, source_target_pairs={{0,2},{1,3},{2,0},{3,1},{4,6},{5,7},{6,4},{7,5},{8,10},{9,11},{10,... | collective-permute-start | bytes 294920 | tf_op jit(solution)/shard_map/ppermute | solution.py:32
  70.2 12.1 %collective-permute-start.22 = (bf16[2,8,3072]{2,1,0:T(8,128)(2,1)S(1)}, bf16[2,8,3072]{2,1,0:T(8,128)(2,1)S(1)}, u32[]{:S(2)}, u32[]{:S(2)}) collective-permute-start(bf16[2,8,3072]{2,1,0:T(8,128)(2,1)S(1)} %get-tuple-element.64), channel_id=1, source_target_pairs={{0,4},{1,5},{2,6},{3,7},{4,0},{5,1},{6,2},{7,3},{8,12},{9,13},{10,... | collective-permute-start | bytes 294920 | tf_op jit(solution)/shard_map/ppermute | solution.py:32
  73.5 8.8 %collective-permute-start.23 = (bf16[2,8,3072]{2,1,0:T(8,128)(2,1)S(1)}, bf16[2,8,3072]{2,1,0:T(8,128)(2,1)S(1)}, u32[]{:S(2)}, u32[]{:S(2)}) collective-permute-start(bf16[2,8,3072]{2,1,0:T(8,128)(2,1)S(1)} %get-tuple-element.65), channel_id=1, source_target_pairs={{0,6},{1,7},{2,4},{3,5},{4,2},{5,3},{6,0},{7,1},{8,14},{9,15},{10,... | collective-permute-start | bytes 294920 | tf_op jit(solution)/shard_map/ppermute | solution.py:32

commit v4 on v3

--- a/solution.py
+++ b/solution.py
@@ -459,11 +459,12 @@
 
 def scale_by_slope(own, parts, slope):
     def body(own_ref, slope_ref, *refs):
-        parts, out_ref = refs[:-1], refs[-1]
+        parts, (out_ref, token) = refs[:-2], refs[-2:]
         out_ref[...] = (add_up(own_ref, parts) * slope_ref[...]).astype(BF16)
-
-    outs = [shape_of(own.shape, BF16)]
-    return call(body, outs, [VM] * (2 + len(parts)), [own, slope, *parts], moved=own.size * 16)[0]
+        token[...] = jnp.zeros_like(token)
+
+    outs = [shape_of(own.shape, BF16), shape_of((8, BLK), F32)]
+    return call(body, outs, [VM] * (2 + len(parts)), [own, slope, *parts], moved=own.size * 16)
 
 
 def pair_sums(*pairs):
@@ -541,8 +542,12 @@
 
     activated, slope = activate(hidden_own, hidden_parts, bias_wide)
     activated_shares = gather_row(activated, n_row)
-    grad_hidden = scale_by_slope(act_own, act_parts, slope)
-    grad_shares = gather_row(grad_hidden, n_row)
+    grad_hidden, grad_there = scale_by_slope(act_own, act_parts, slope)
+    met = swap(grad_there, "col", n_col, 1)
+    grad_later = follow(grad_hidden, met)
+    grad_shares = [grad_hidden]
+    for mask in range(1, n_row):
+        grad_shares += [swap(grad_hidden if mask == n_row - 1 else grad_later, "row", n_row, mask)]
 
     out_keep, out_send, out_done, w2_grad = hidden_to_model(
         second, second_at, activated_shares, second_held, True, model_blocks, n_col, other=full_cotangent

time: 83.3 us -> 79.9 us (0.959)
  waiting for transfers between devices: 14.8 us -> 11.6 us
    ppermute x24 -> x25, waiting for transfers between devices: 14.8 us -> 11.6 us  [swap(): lax.ppermute(array, axis, [(place, place ^ mask) for place in range(size)])]
    ppermute x24 -> x25, starting transfers between devices: 27 us -> 26.6 us  [swap(): lax.ppermute(array, axis, [(place, place ^ mask) for place in range(size)])]
    pallas_call x16 -> x17, Pallas kernels: 40.4 us -> 40.5 us  [call(): pl.pallas_call(body, out_shape=outs, in_specs=in_specs, out_specs=[whole]...]
  transfers between devices with their start and end apart: 24 -> 25, of which waited for: 5 -> 6; matrix products, arithmetic and copies ran while one was open for 0% -> 0% of each run, Pallas kernels for 43% -> 44%
where the time goes in v4:
time: 79.9 us; the launch traced here: 79.6 us
  Pallas kernels  40.5 us (51%)
  starting transfers between devices  26.6 us (33%)
  waiting for transfers between devices  11.6 us (15%)
  between operations  0.85 us (1%)
    pallas_call x17, Pallas kernels, call(): pl.pallas_call(body, out_shape=outs, in_specs=in_specs, out_specs=[whole]...  40.5 us
    ppermute x25, starting transfers between devices, swap(): lax.ppermute(array, axis, [(place, place ^ mask) for place in range(size)])  26.6 us
    ppermute x25, waiting for transfers between devices, swap(): lax.ppermute(array, axis, [(place, place ^ mask) for place in range(size)])  11.6 us
  transfers between devices with their start and end apart: 25, of which 6 were waited for; matrix products, arithmetic and copies ran while one was open for 0% of the time, Pallas kernels for 44%

profile of v4, /device:TPU:0, one launch (start us, length us, event | category | flops | bytes accessed | tf_op | source)
XLA Modules:
  0.0 79.6 jit_solution(16120328917260265117)
XLA Ops:
  0.6 0.8 %shard_map.111.refs_0_ = bf16[2,8,3072]{2,1,0:T(8,128)(2,1)S(1)} custom-call(bf16[8,3072]{1,0:T(8,128)(2,1)} %first_ref.1, bf16[8,3072]{1,0:T(8,128)(2,1)} %second_ref.1), custom_call_target="tpu_custom_call" | custom-call | bytes 196608 | tf_op jit(solution)/shard_map/pallas_call | solution.py:38
  1.5 3.1 %collective-permute-start.1 = (bf16[2,8,3072]{2,1,0:T(8,128)(2,1)S(1)}, bf16[2,8,3072]{2,1,0:T(8,128)(2,1)S(1)}, u32[]{:S(2)}, u32[]{:S(2)}) collective-permute-start(bf16[2,8,3072]{2,1,0:T(8,128)(2,1)S(1)} %shard_map.111.refs_0_), channel_id=1, source_target_pairs={{0,2},{1,3},{2,0},{3,1},{4,6},{5,7},{6,4},{7,5},{8,10},{9,11},{10,... | collective-permute-start | bytes 294920 | tf_op jit(solution)/shard_map/ppermute | solution.py:32
  4.5 2.6 %collective-permute-start.3 = (bf16[2,8,3072]{2,1,0:T(8,128)(2,1)S(1)}, bf16[2,8,3072]{2,1,0:T(8,128)(2,1)S(1)}, u32[]{:S(2)}, u32[]{:S(2)}) collective-permute-start(bf16[2,8,3072]{2,1,0:T(8,128)(2,1)S(1)} %shard_map.111.refs_0_), channel_id=1, source_target_pairs={{0,4},{1,5},{2,6},{3,7},{4,0},{5,1},{6,2},{7,3},{8,12},{9,13},{10,... | collective-permute-start | bytes 294920 | tf_op jit(solution)/shard_map/ppermute | solution.py:32
  7.1 0.0 collective-permute-start.5
  7.1 0.0 collective-permute-start
  7.1 3.7 %shard_map.112 = (bf16[288,128,128]{2,1,0:T(8,128)(2,1)S(1)}, f32[8,128]{1,0:T(8,128)S(1)}) custom-call(bf16[288,128,128]{2,1,0:T(8,128)(2,1)} %bitcast.9), custom_call_target="tpu_custom_call" | custom-call | bytes 18874368 | tf_op jit(solution)/shard_map/pallas_call | solution.py:38
  10.8 3.7 %shard_map.113 = (bf16[288,128,128]{2,1,0:T(8,128)(2,1)S(1)}, f32[8,128]{1,0:T(8,128)S(1)}) custom-call(bf16[288,128,128]{2,1,0:T(8,128)(2,1)} %bitcast.10), custom_call_target="tpu_custom_call" | custom-call | bytes 18874368 | tf_op jit(solution)/shard_map/pallas_call | solution.py:38
  14.5 0.0 collective-permute-done.1.array_ref
  14.6 0.6 collective-permute-start.2
  15.1 0.0 collective-permute-done.3.array_ref
  15.1 0.1 collective-permute-start.4
  15.2 0.0 collective-permute-done.5.array_ref
  15.2 0.5 collective-permute-start.6
  15.8 1.0 %shard_map.110 = (s32[24,128]{1,0:T(8,128)S(1)}, s32[48,128]{1,0:T(8,128)S(1)}) custom-call(s32[24,48]{1,0:T(8,128)} %refs_0_.1, s32[24,48]{1,0:T(8,128)} %bitcast.11), custom_call_target="tpu_custom_call" | custom-call | tf_op jit(solution)/shard_map/pallas_call | solution.py:38
  16.8 0.0 collective-permute-done.refs_1_
  16.8 0.0 collective-permute-done.2.refs_3_
  16.8 0.0 collective-permute-done.4.refs_5_
  16.9 0.0 collective-permute-done.6.refs_7_
  16.9 0.0 copy-start
  16.9 3.5 %shard_map.117 = (f32[48,16,128]{2,1,0:T(8,128)S(1)}, bf16[48,16,128]{2,1,0:T(8,128)(2,1)S(1)}, bf16[48,16,128]{2,1,0:T(8,128)(2,1)S(1)}, bf16[48,16,128]{2,1,0:T(8,128)(2,1)S(1)}, bf16[24,64,128]{2,1,0:T(8,128)(2,1)S(1)}) custom-call(s32[24,128]{1,0:T(8,128)S(1)} %get-tuple-element.41.row_ref.col_ref, s32[24,128]{1,0:T(8,128)S(1)} %get-tuple-element.41.row_ref.col_ref, ...), custom_call_target="tpu_custom_call" | custom-call | flops 603979776 | bytes 9437184 | tf_op jit(solution)/shard_map/pallas_call | solution.py:38
  20.4 1.8 %collective-permute-start.7 = (bf16[48,16,128]{2,1,0:T(8,128)(2,1)S(1)}, bf16[48,16,128]{2,1,0:T(8,128)(2,1)S(1)}, u32[]{:S(2)}, u32[]{:S(2)}) collective-permute-start(bf16[48,16,128]{2,1,0:T(8,128)(2,1)S(1)} %get-tuple-element.46), channel_id=1, source_target_pairs={{0,8},{8,0},{16,24},{24,16},{1,9},{9,1},{17,25},{25,17},{2,10},{10... | collective-permute-start | bytes 589832 | tf_op jit(solution)/shard_map/ppermute | solution.py:32
  22.2 1.5 %collective-permute-start.8 = (bf16[48,16,128]{2,1,0:T(8,128)(2,1)S(1)}, bf16[48,16,128]{2,1,0:T(8,128)(2,1)S(1)}, u32[]{:S(2)}, u32[]{:S(2)}) collective-permute-start(bf16[48,16,128]{2,1,0:T(8,128)(2,1)S(1)} %get-tuple-element.47), channel_id=1, source_target_pairs={{0,16},{8,24},{16,0},{24,8},{1,17},{9,25},{17,1},{25,9},{2,18},{10... | collective-permute-start | bytes 589832 | tf_op jit(solution)/shard_map/ppermute | solution.py:32
  23.7 0.3 collective-permute-start.9
  24.0 4.8 %shard_map.119 = (f32[48,16,128]{2,1,0:T(8,128)S(1)}, bf16[48,16,128]{2,1,0:T(8,128)(2,1)S(1)}, bf16[48,16,128]{2,1,0:T(8,128)(2,1)S(1)}, bf16[48,16,128]{2,1,0:T(8,128)(2,1)S(1)}, bf16[24,64,128]{2,1,0:T(8,128)(2,1)S(1)}) custom-call(s32[48,128]{1,0:T(8,128)S(1)} %get-tuple-element.40.row_ref.col_ref, s32[48,128]{1,0:T(8,128)S(1)} %get-tuple-element.40.row_ref.col_ref, ...), custom_call_target="tpu_custom_call" | custom-call | flops 603979776 | bytes 9437184 | tf_op jit(solution)/shard_map/pallas_call | solution.py:38
  28.8 1.8 %collective-permute-start.14 = (bf16[48,16,128]{2,1,0:T(8,128)(2,1)S(1)}, bf16[48,16,128]{2,1,0:T(8,128)(2,1)S(1)}, u32[]{:S(2)}, u32[]{:S(2)}) collective-permute-start(bf16[48,16,128]{2,1,0:T(8,128)(2,1)S(1)} %get-tuple-element.57), channel_id=1, source_target_pairs={{0,8},{8,0},{16,24},{24,16},{1,9},{9,1},{17,25},{25,17},{2,10},{10... | collective-permute-start | bytes 589832 | tf_op jit(solution)/shard_map/ppermute | solution.py:32
  30.6 1.6 %collective-permute-start.15 = (bf16[48,16,128]{2,1,0:T(8,128)(2,1)S(1)}, bf16[48,16,128]{2,1,0:T(8,128)(2,1)S(1)}, u32[]{:S(2)}, u32[]{:S(2)}) collective-permute-start(bf16[48,16,128]{2,1,0:T(8,128)(2,1)S(1)} %get-tuple-element.58), channel_id=1, source_target_pairs={{0,16},{8,24},{16,0},{24,8},{1,17},{9,25},{17,1},{25,9},{2,18},{10... | collective-permute-start | bytes 589832 | tf_op jit(solution)/shard_map/ppermute | solution.py:32
  32.1 0.0 collective-permute-done.7.refs_0_
  32.1 0.2 collective-permute-start.16
  32.4 0.5 collective-permute-done.8.refs_1_
  32.9 0.8 collective-permute-done.9.refs_2_
  33.6 0.4 shard_map.118
  34.0 1.5 %collective-permute-start.12 = (bf16[48,16,128]{2,1,0:T(8,128)(2,1)S(1)}, bf16[48,16,128]{2,1,0:T(8,128)(2,1)S(1)}, u32[]{:S(2)}, u32[]{:S(2)}) collective-permute-start(bf16[48,16,128]{2,1,0:T(8,128)(2,1)S(1)} %get-tuple-element.49.refs_0_), channel_id=1, source_target_pairs={{0,24},{8,16},{16,8},{24,0},{1,25},{9,17},{17,9},{25,1},{2,26},{10... | collective-permute-start | bytes 589832 | tf_op jit(solution)/shard_map/ppermute | solution.py:32
  35.6 1.4 %collective-permute-start.11 = (bf16[48,16,128]{2,1,0:T(8,128)(2,1)S(1)}, bf16[48,16,128]{2,1,0:T(8,128)(2,1)S(1)}, u32[]{:S(2)}, u32[]{:S(2)}) collective-permute-start(bf16[48,16,128]{2,1,0:T(8,128)(2,1)S(1)} %get-tuple-element.49.refs_0_), channel_id=1, source_target_pairs={{0,16},{8,24},{16,0},{24,8},{1,17},{9,25},{17,1},{25,9},{2,18},{10... | collective-permute-start | bytes 589832 | tf_op jit(solution)/shard_map/ppermute | solution.py:32
  37.0 0.0 collective-permute-done.14.refs_0_
  37.0 1.4 %collective-permute-start.10 = (bf16[48,16,128]{2,1,0:T(8,128)(2,1)S(1)}, bf16[48,16,128]{2,1,0:T(8,128)(2,1)S(1)}, u32[]{:S(2)}, u32[]{:S(2)}) collective-permute-start(bf16[48,16,128]{2,1,0:T(8,128)(2,1)S(1)} %get-tuple-element.49.refs_0_), channel_id=1, source_target_pairs={{0,8},{8,0},{16,24},{24,16},{1,9},{9,1},{17,25},{25,17},{2,10},{10... | collective-permute-start | bytes 589832 | tf_op jit(solution)/shard_map/ppermute | solution.py:32
  38.4 8.2 %collective-permute-done.15.refs_1_ = bf16[48,16,128]{2,1,0:T(8,128)(2,1)S(1)} collective-permute-done((bf16[48,16,128]{2,1,0:T(8,128)(2,1)S(1)}, bf16[48,16,128]{2,1,0:T(8,128)(2,1)S(1)}, u32[]{:S(2)}, u32[]{:S(2)}) %collective-permute-start.15) | collective-permute-done | bytes 196640 | tf_op jit(solution)/shard_map/ppermute | solution.py:32
  46.6 0.0 collective-permute-done.16.refs_2_
  46.6 0.1 shard_map.121
  46.7 0.1 collective-permute-start.17
  46.8 1.6 %collective-permute-start.20 = (bf16[48,16,128]{2,1,0:T(8,128)(2,1)S(1)}, bf16[48,16,128]{2,1,0:T(8,128)(2,1)S(1)}, u32[]{:S(2)}, u32[]{:S(2)}) collective-permute-start(bf16[48,16,128]{2,1,0:T(8,128)(2,1)S(1)} %get-tuple-element.60.array_ref.refs_0_), channel_id=1, source_target_pairs={{0,24},{8,16},{16,8},{24,0},{1,25},{9,17},{17,9},{25,1},{2,26},{10... | collective-permute-start | bytes 589832 | tf_op jit(solution)/shard_map/ppermute | solution.py:32
  48.4 0.0 collective-permute-done.17.refs_0_
  48.4 1.5 %collective-permute-start.19 = (bf16[48,16,128]{2,1,0:T(8,128)(2,1)S(1)}, bf16[48,16,128]{2,1,0:T(8,128)(2,1)S(1)}, u32[]{:S(2)}, u32[]{:S(2)}) collective-permute-start(bf16[48,16,128]{2,1,0:T(8,128)(2,1)S(1)} %shard_map.122), channel_id=1, source_target_pairs={{0,16},{8,24},{16,0},{24,8},{1,17},{9,25},{17,1},{25,9},{2,18},{10... | collective-permute-start | bytes 589832 | tf_op jit(solution)/shard_map/ppermute | solution.py:32
  49.8 0.0 collective-permute-done.12.refs_3_
  49.9 0.6 collective-permute-start.18
  50.4 0.0 collective-permute-done.11.refs_2_
  50.4 0.0 collective-permute-done.10.refs_1_
  50.4 8.4 %shard_map.120 = (f32[4,8,3072]{2,1,0:T(8,128)S(1)}, bf16[4,8,3072]{2,1,0:T(8,128)(2,1)S(1)}, f32[8,128]{1,0:T(8,128)S(1)}, f32[288,128,128]{2,1,0:T(8,128)}) custom-call(s32[48,128]{1,0:T(8,128)S(1)} %get-tuple-element.40.row_ref.col_ref, s32[48,128]{1,0:T(8,128)S(1)} %get-tuple-element.40.row_ref.col_ref, ...), custom_call_target="tpu_custom_call" | custom-call | flops 1207959552 | bytes 28311552 | tf_op jit(solution)/shard_map/pallas_call | solution.py:38
  58.8 0.1 collective-permute-start.13
  58.9 0.0 collective-permute-done.20.refs_3_
  58.9 0.3 collective-permute-done.19.refs_2_
  59.2 0.4 collective-permute-done.18.refs_1_
  59.6 4.6 %shard_map.123 = (f32[4,8,3072]{2,1,0:T(8,128)S(1)}, bf16[4,8,3072]{2,1,0:T(8,128)(2,1)S(1)}) custom-call(s32[24,128]{1,0:T(8,128)S(1)} %get-tuple-element.41.row_ref.col_ref, s32[24,128]{1,0:T(8,128)S(1)} %get-tuple-element.41.row_ref.col_ref, bf16[48,16,128]{2,1,0:T(8,128)(2,1)S(1)} %get-tuple-element.60.array_ref.refs_0_, ...), custom_call_target="tpu_custom_call" | custom-call | flops 603979776 | bytes 9437184 | tf_op jit(solution)/shard_map/pallas_call | solution.py:38
  64.2 0.1 collective-permute-start.21
  64.3 0.0 collective-permute-done.13.refs_1_
  64.3 1.4 %collective-permute-done.21.refs_3_ = bf16[4,8,3072]{2,1,0:T(8,128)(2,1)S(1)} collective-permute-done((bf16[4,8,3072]{2,1,0:T(8,128)(2,1)S(1)}, bf16[4,8,3072]{2,1,0:T(8,128)(2,1)S(1)}, u32[]{:S(2)}, u32[]{:S(2)}) %collective-permute-start.21) | collective-permute-done | bytes 196640 | tf_op jit(solution)/shard_map/ppermute | solution.py:32
  65.8 0.1 shard_map.124
  65.8 0.9 %collective-permute-start.22 = (bf16[2,8,3072]{2,1,0:T(8,128)(2,1)S(1)}, bf16[2,8,3072]{2,1,0:T(8,128)(2,1)S(1)}, u32[]{:S(2)}, u32[]{:S(2)}) collective-permute-start(bf16[2,8,3072]{2,1,0:T(8,128)(2,1)S(1)} %get-tuple-element.67), channel_id=1, source_target_pairs={{0,2},{1,3},{2,0},{3,1},{4,6},{5,7},{6,4},{7,5},{8,10},{9,11},{10,... | collective-permute-start | bytes 294920 | tf_op jit(solution)/shard_map/ppermute | solution.py:32
  66.8 3.3 %collective-permute-start.23 = (bf16[2,8,3072]{2,1,0:T(8,128)(2,1)S(1)}, bf16[2,8,3072]{2,1,0:T(8,128)(2,1)S(1)}, u32[]{:S(2)}, u32[]{:S(2)}) collective-permute-start(bf16[2,8,3072]{2,1,0:T(8,128)(2,1)S(1)} %get-tuple-element.68), channel_id=1, source_target_pairs={{0,4},{1,5},{2,6},{3,7},{4,0},{5,1},{6,2},{7,3},{8,12},{9,13},{10,... | collective-permute-start | bytes 294920 | tf_op jit(solution)/shard_map/ppermute | solution.py:32
  70.1 0.2 collective-permute-start.24
  70.3 8.6 %shard_map.126 = (f32[288,128,128]{2,1,0:T(8,128)}, f32[48,128]{1,0:T(8,128)}) custom-call(s32[24,128]{1,0:T(8,128)S(1)} %get-tuple-element.41.row_ref.col_ref, s32[24,128]{1,0:T(8,128)S(1)} %get-tuple-element.41.row_ref.col_ref, bf16[24,64,128]{2,1,0:T(8,128)(2,1)S(1)} %get-tuple-element.50.refs_8_.left_ref, ...), custom_call_target="tpu_custom_call" | custom-call | flops 603979776 | bytes 18874368 | tf_op jit(solution)/shard_map/pallas_call | solution.py:38
  78.9 0.0 collective-permute-done.22.refs_2_
  78.9 0.0 collective-permute-done.23.refs_3_
  78.9 0.0 collective-permute-done.24.refs_4_
  78.9 0.7 shard_map.125
  (6 shorter events, 0.0 us)
Async XLA Ops:
  1.5 13.1 %collective-permute-start.1 = (bf16[2,8,3072]{2,1,0:T(8,128)(2,1)S(1)}, bf16[2,8,3072]{2,1,0:T(8,128)(2,1)S(1)}, u32[]{:S(2)}, u32[]{:S(2)}) collective-permute-start(bf16[2,8,3072]{2,1,0:T(8,128)(2,1)S(1)} %shard_map.111.refs_0_), channel_id=1, source_target_pairs={{0,2},{1,3},{2,0},{3,1},{4,6},{5,7},{6,4},{7,5},{8,10},{9,11},{10,... | collective-permute-start | bytes 294920 | tf_op jit(solution)/shard_map/ppermute | solution.py:32
  4.5 10.6 %collective-permute-start.3 = (bf16[2,8,3072]{2,1,0:T(8,128)(2,1)S(1)}, bf16[2,8,3072]{2,1,0:T(8,128)(2,1)S(1)}, u32[]{:S(2)}, u32[]{:S(2)}) collective-permute-start(bf16[2,8,3072]{2,1,0:T(8,128)(2,1)S(1)} %shard_map.111.refs_0_), channel_id=1, source_target_pairs={{0,4},{1,5},{2,6},{3,7},{4,0},{5,1},{6,2},{7,3},{8,12},{9,13},{10,... | collective-permute-start | bytes 294920 | tf_op jit(solution)/shard_map/ppermute | solution.py:32
  7.1 8.1 %collective-permute-start.5 = (bf16[2,8,3072]{2,1,0:T(8,128)(2,1)S(1)}, bf16[2,8,3072]{2,1,0:T(8,128)(2,1)S(1)}, u32[]{:S(2)}, u32[]{:S(2)}) collective-permute-start(bf16[2,8,3072]{2,1,0:T(8,128)(2,1)S(1)} %shard_map.111.refs_0_), channel_id=1, source_target_pairs={{0,6},{1,7},{2,4},{3,5},{4,2},{5,3},{6,0},{7,1},{8,14},{9,15},{10,... | collective-permute-start | bytes 294920 | tf_op jit(solution)/shard_map/ppermute | solution.py:32
  7.1 9.7 %collective-permute-start = (bf16[2,8,3072]{2,1,0:T(8,128)(2,1)S(1)}, bf16[2,8,3072]{2,1,0:T(8,128)(2,1)S(1)}, u32[]{:S(2)}, u32[]{:S(2)}) collective-permute-start(bf16[2,8,3072]{2,1,0:T(8,128)(2,1)S(1)} %shard_map.111.refs_0_), channel_id=1, source_target_pairs={{0,1},{1,0},{2,3},{3,2},{4,5},{5,4},{6,7},{7,6},{8,9},{9,8},{10,11... | collective-permute-start | bytes 294920 | tf_op jit(solution)/shard_map/ppermute | solution.py:32
  14.6 2.3 %collective-permute-start.2 = (bf16[2,8,3072]{2,1,0:T(8,128)(2,1)S(1)}, bf16[2,8,3072]{2,1,0:T(8,128)(2,1)S(1)}, u32[]{:S(2)}, u32[]{:S(2)}) collective-permute-start(bf16[2,8,3072]{2,1,0:T(8,128)(2,1)S(1)} %shard_map.114.refs_2_), channel_id=1, source_target_pairs={{0,1},{1,0},{2,3},{3,2},{4,5},{5,4},{6,7},{7,6},{8,9},{9,8},{10,11... | collective-permute-start | bytes 294920 | tf_op jit(solution)/shard_map/ppermute | solution.py:32
  15.1 1.7 %collective-permute-start.4 = (bf16[2,8,3072]{2,1,0:T(8,128)(2,1)S(1)}, bf16[2,8,3072]{2,1,0:T(8,128)(2,1)S(1)}, u32[]{:S(2)}, u32[]{:S(2)}) collective-permute-start(bf16[2,8,3072]{2,1,0:T(8,128)(2,1)S(1)} %shard_map.115.refs_4_), channel_id=1, source_target_pairs={{0,1},{1,0},{2,3},{3,2},{4,5},{5,4},{6,7},{7,6},{8,9},{9,8},{10,11... | collective-permute-start | bytes 294920 | tf_op jit(solution)/shard_map/ppermute | solution.py:32
  15.2 1.6 %collective-permute-start.6 = (bf16[2,8,3072]{2,1,0:T(8,128)(2,1)S(1)}, bf16[2,8,3072]{2,1,0:T(8,128)(2,1)S(1)}, u32[]{:S(2)}, u32[]{:S(2)}) collective-permute-start(bf16[2,8,3072]{2,1,0:T(8,128)(2,1)S(1)} %shard_map.116.refs_6_), channel_id=1, source_target_pairs={{0,1},{1,0},{2,3},{3,2},{4,5},{5,4},{6,7},{7,6},{8,9},{9,8},{10,11... | collective-permute-start | bytes 294920 | tf_op jit(solution)/shard_map/ppermute | solution.py:32
  16.9 15.5 %copy-start = (bf16[6144]{0:T(1024)(128)(2,1)S(1)}, bf16[6144]{0:T(1024)(128)(2,1)}, u32[]{:S(2)}) copy-start(bf16[6144]{0:T(1024)(128)(2,1)} %param.11) | copy-start | bytes 36868
  20.4 11.7 %collective-permute-start.7 = (bf16[48,16,128]{2,1,0:T(8,128)(2,1)S(1)}, bf16[48,16,128]{2,1,0:T(8,128)(2,1)S(1)}, u32[]{:S(2)}, u32[]{:S(2)}) collective-permute-start(bf16[48,16,128]{2,1,0:T(8,128)(2,1)S(1)} %get-tuple-element.46), channel_id=1, source_target_pairs={{0,8},{8,0},{16,24},{24,16},{1,9},{9,1},{17,25},{25,17},{2,10},{10... | collective-permute-start | bytes 589832 | tf_op jit(solution)/shard_map/ppermute | solution.py:32
  22.2 10.7 %collective-permute-start.8 = (bf16[48,16,128]{2,1,0:T(8,128)(2,1)S(1)}, bf16[48,16,128]{2,1,0:T(8,128)(2,1)S(1)}, u32[]{:S(2)}, u32[]{:S(2)}) collective-permute-start(bf16[48,16,128]{2,1,0:T(8,128)(2,1)S(1)} %get-tuple-element.47), channel_id=1, source_target_pairs={{0,16},{8,24},{16,0},{24,8},{1,17},{9,25},{17,1},{25,9},{2,18},{10... | collective-permute-start | bytes 589832 | tf_op jit(solution)/shard_map/ppermute | solution.py:32
  23.7 9.9 %collective-permute-start.9 = (bf16[48,16,128]{2,1,0:T(8,128)(2,1)S(1)}, bf16[48,16,128]{2,1,0:T(8,128)(2,1)S(1)}, u32[]{:S(2)}, u32[]{:S(2)}) collective-permute-start(bf16[48,16,128]{2,1,0:T(8,128)(2,1)S(1)} %get-tuple-element.48), channel_id=1, source_target_pairs={{0,24},{8,16},{16,8},{24,0},{1,25},{9,17},{17,9},{25,1},{2,26},{10... | collective-permute-start | bytes 589832 | tf_op jit(solution)/shard_map/ppermute | solution.py:32
  28.8 8.2 %collective-permute-start.14 = (bf16[48,16,128]{2,1,0:T(8,128)(2,1)S(1)}, bf16[48,16,128]{2,1,0:T(8,128)(2,1)S(1)}, u32[]{:S(2)}, u32[]{:S(2)}) collective-permute-start(bf16[48,16,128]{2,1,0:T(8,128)(2,1)S(1)} %get-tuple-element.57), channel_id=1, source_target_pairs={{0,8},{8,0},{16,24},{24,16},{1,9},{9,1},{17,25},{25,17},{2,10},{10... | collective-permute-start | bytes 589832 | tf_op jit(solution)/shard_map/ppermute | solution.py:32
  30.6 16.0 %collective-permute-start.15 = (bf16[48,16,128]{2,1,0:T(8,128)(2,1)S(1)}, bf16[48,16,128]{2,1,0:T(8,128)(2,1)S(1)}, u32[]{:S(2)}, u32[]{:S(2)}) collective-permute-start(bf16[48,16,128]{2,1,0:T(8,128)(2,1)S(1)} %get-tuple-element.58), channel_id=1, source_target_pairs={{0,16},{8,24},{16,0},{24,8},{1,17},{9,25},{17,1},{25,9},{2,18},{10... | collective-permute-start | bytes 589832 | tf_op jit(solution)/shard_map/ppermute | solution.py:32
  32.1 14.4 %collective-permute-start.16 = (bf16[48,16,128]{2,1,0:T(8,128)(2,1)S(1)}, bf16[48,16,128]{2,1,0:T(8,128)(2,1)S(1)}, u32[]{:S(2)}, u32[]{:S(2)}) collective-permute-start(bf16[48,16,128]{2,1,0:T(8,128)(2,1)S(1)} %get-tuple-element.59), channel_id=1, source_target_pairs={{0,24},{8,16},{16,8},{24,0},{1,25},{9,17},{17,9},{25,1},{2,26},{10... | collective-permute-start | bytes 589832 | tf_op jit(solution)/shard_map/ppermute | solution.py:32
  34.0 15.8 %collective-permute-start.12 = (bf16[48,16,128]{2,1,0:T(8,128)(2,1)S(1)}, bf16[48,16,128]{2,1,0:T(8,128)(2,1)S(1)}, u32[]{:S(2)}, u32[]{:S(2)}) collective-permute-start(bf16[48,16,128]{2,1,0:T(8,128)(2,1)S(1)} %get-tuple-element.49.refs_0_), channel_id=1, source_target_pairs={{0,24},{8,16},{16,8},{24,0},{1,25},{9,17},{17,9},{25,1},{2,26},{10... | collective-permute-start | bytes 589832 | tf_op jit(solution)/shard_map/ppermute | solution.py:32
  35.6 14.9 %collective-permute-start.11 = (bf16[48,16,128]{2,1,0:T(8,128)(2,1)S(1)}, bf16[48,16,128]{2,1,0:T(8,128)(2,1)S(1)}, u32[]{:S(2)}, u32[]{:S(2)}) collective-permute-start(bf16[48,16,128]{2,1,0:T(8,128)(2,1)S(1)} %get-tuple-element.49.refs_0_), channel_id=1, source_target_pairs={{0,16},{8,24},{16,0},{24,8},{1,17},{9,25},{17,1},{25,9},{2,18},{10... | collective-permute-start | bytes 589832 | tf_op jit(solution)/shard_map/ppermute | solution.py:32
  37.0 13.4 %collective-permute-start.10 = (bf16[48,16,128]{2,1,0:T(8,128)(2,1)S(1)}, bf16[48,16,128]{2,1,0:T(8,128)(2,1)S(1)}, u32[]{:S(2)}, u32[]{:S(2)}) collective-permute-start(bf16[48,16,128]{2,1,0:T(8,128)(2,1)S(1)} %get-tuple-element.49.refs_0_), channel_id=1, source_target_pairs={{0,8},{8,0},{16,24},{24,16},{1,9},{9,1},{17,25},{25,17},{2,10},{10... | collective-permute-start | bytes 589832 | tf_op jit(solution)/shard_map/ppermute | solution.py:32
  46.7 1.7 %collective-permute-start.17 = (f32[8,128]{1,0:T(8,128)S(1)}, f32[8,128]{1,0:T(8,128)S(1)}, u32[]{:S(2)}, u32[]{:S(2)}) collective-permute-start(f32[8,128]{1,0:T(8,128)S(1)} %get-tuple-element.61), channel_id=1, source_target_pairs={{0,1},{1,0},{2,3},{3,2},{4,5},{5,4},{6,7},{7,6},{8,9},{9,8},{10,11... | collective-permute-start | bytes 12296 | tf_op jit(solution)/shard_map/ppermute | solution.py:32
  46.8 12.1 %collective-permute-start.20 = (bf16[48,16,128]{2,1,0:T(8,128)(2,1)S(1)}, bf16[48,16,128]{2,1,0:T(8,128)(2,1)S(1)}, u32[]{:S(2)}, u32[]{:S(2)}) collective-permute-start(bf16[48,16,128]{2,1,0:T(8,128)(2,1)S(1)} %get-tuple-element.60.array_ref.refs_0_), channel_id=1, source_target_pairs={{0,24},{8,16},{16,8},{24,0},{1,25},{9,17},{17,9},{25,1},{2,26},{10... | collective-permute-start | bytes 589832 | tf_op jit(solution)/shard_map/ppermute | solution.py:32
  48.4 10.8 %collective-permute-start.19 = (bf16[48,16,128]{2,1,0:T(8,128)(2,1)S(1)}, bf16[48,16,128]{2,1,0:T(8,128)(2,1)S(1)}, u32[]{:S(2)}, u32[]{:S(2)}) collective-permute-start(bf16[48,16,128]{2,1,0:T(8,128)(2,1)S(1)} %shard_map.122), channel_id=1, source_target_pairs={{0,16},{8,24},{16,0},{24,8},{1,17},{9,25},{17,1},{25,9},{2,18},{10... | collective-permute-start | bytes 589832 | tf_op jit(solution)/shard_map/ppermute | solution.py:32
  49.9 9.8 %collective-permute-start.18 = (bf16[48,16,128]{2,1,0:T(8,128)(2,1)S(1)}, bf16[48,16,128]{2,1,0:T(8,128)(2,1)S(1)}, u32[]{:S(2)}, u32[]{:S(2)}) collective-permute-start(bf16[48,16,128]{2,1,0:T(8,128)(2,1)S(1)} %shard_map.122), channel_id=1, source_target_pairs={{0,8},{8,0},{16,24},{24,16},{1,9},{9,1},{17,25},{25,17},{2,10},{10... | collective-permute-start | bytes 589832 | tf_op jit(solution)/shard_map/ppermute | solution.py:32
  58.8 5.5 %collective-permute-start.13 = (bf16[4,8,3072]{2,1,0:T(8,128)(2,1)S(1)}, bf16[4,8,3072]{2,1,0:T(8,128)(2,1)S(1)}, u32[]{:S(2)}, u32[]{:S(2)}) collective-permute-start(bf16[4,8,3072]{2,1,0:T(8,128)(2,1)S(1)} %get-tuple-element.54), channel_id=1, source_target_pairs={{0,1},{1,0},{2,3},{3,2},{4,5},{5,4},{6,7},{7,6},{8,9},{9,8},{10,11... | collective-permute-start | bytes 589832 | tf_op jit(solution)/shard_map/ppermute | solution.py:32
  64.2 1.5 %collective-permute-start.21 = (bf16[4,8,3072]{2,1,0:T(8,128)(2,1)S(1)}, bf16[4,8,3072]{2,1,0:T(8,128)(2,1)S(1)}, u32[]{:S(2)}, u32[]{:S(2)}) collective-permute-start(bf16[4,8,3072]{2,1,0:T(8,128)(2,1)S(1)} %get-tuple-element.64), channel_id=1, source_target_pairs={{0,1},{1,0},{2,3},{3,2},{4,5},{5,4},{6,7},{7,6},{8,9},{9,8},{10,11... | collective-permute-start | bytes 589832 | tf_op jit(solution)/shard_map/ppermute | solution.py:32
  65.8 13.0 %collective-permute-start.22 = (bf16[2,8,3072]{2,1,0:T(8,128)(2,1)S(1)}, bf16[2,8,3072]{2,1,0:T(8,128)(2,1)S(1)}, u32[]{:S(2)}, u32[]{:S(2)}) collective-permute-start(bf16[2,8,3072]{2,1,0:T(8,128)(2,1)S(1)} %get-tuple-element.67), channel_id=1, source_target_pairs={{0,2},{1,3},{2,0},{3,1},{4,6},{5,7},{6,4},{7,5},{8,10},{9,11},{10,... | collective-permute-start | bytes 294920 | tf_op jit(solution)/shard_map/ppermute | solution.py:32
  66.8 12.1 %collective-permute-start.23 = (bf16[2,8,3072]{2,1,0:T(8,128)(2,1)S(1)}, bf16[2,8,3072]{2,1,0:T(8,128)(2,1)S(1)}, u32[]{:S(2)}, u32[]{:S(2)}) collective-permute-start(bf16[2,8,3072]{2,1,0:T(8,128)(2,1)S(1)} %get-tuple-element.68), channel_id=1, source_target_pairs={{0,4},{1,5},{2,6},{3,7},{4,0},{5,1},{6,2},{7,3},{8,12},{9,13},{10,... | collective-permute-start | bytes 294920 | tf_op jit(solution)/shard_map/ppermute | solution.py:32
  70.1 8.8 %collective-permute-start.24 = (bf16[2,8,3072]{2,1,0:T(8,128)(2,1)S(1)}, bf16[2,8,3072]{2,1,0:T(8,128)(2,1)S(1)}, u32[]{:S(2)}, u32[]{:S(2)}) collective-permute-start(bf16[2,8,3072]{2,1,0:T(8,128)(2,1)S(1)} %get-tuple-element.69), channel_id=1, source_target_pairs={{0,6},{1,7},{2,4},{3,5},{4,2},{5,3},{6,0},{7,1},{8,14},{9,15},{10,... | collective-permute-start | bytes 294920 | tf_op jit(solution)/shard_map/ppermute | solution.py:32

commit v5 on v4

--- a/solution.py
+++ b/solution.py
@@ -1,3 +1,4 @@
+import functools
 import math
 
 import jax
@@ -152,8 +153,9 @@
             total[col] += dot(source[row], blocks[near], 1, 0)
 
 
-def add_backward(layout, row_ref, col_ref, first, here, source, blocks, total):
+def add_backward(layout, row_ref, col_ref, first, here, source, blocks, total, turned=False):
     group = layout.group
+    side = 0 if turned else 1
     for near in range(here):
         if layout.even:
             width = 2 if group % 2 == 0 else 1
@@ -164,13 +166,13 @@
                 left = [source[col] for col in cols]
                 right = [blocks[place + more] for more in range(width)]
                 left = left[0] if width == 1 else jnp.concatenate(left, axis=1)
-                right = right[0] if width == 1 else jnp.concatenate(right, axis=1)
-                product = dot(left, right, 1, 1)
+                right = right[0] if width == 1 else jnp.concatenate(right, axis=side)
+                product = dot(left, right, 1, side)
                 result = product if result is None else result + product
             total[first + near] = result
         else:
             row, col = read_slot(layout, row_ref, col_ref, first + near, 0)
-            total[row] += dot(source[col], blocks[near], 1, 1)
+            total[row] += dot(source[col], blocks[near], 1, side)
 
 
 def block_products(layout, row_ref, col_ref, first, here, left, right, out):
@@ -260,6 +262,27 @@
     return call(body, [shape_of(array.shape, array.dtype)], specs, [array, *before], moved=4 * array.size)[0]
 
 
+def turn(blocks, after):
+    count = blocks.shape[0]
+
+    def body(from_ref, after_ref, to_ref, token):
+        token[...] = jnp.zeros_like(token)
+
+        def one(place, carry):
+            to_ref[place] = from_ref[place].T
+            return carry
+
+        lax.fori_loop(0, count, one, 0, unroll=math.gcd(count, 48))
+
+    return call(
+        body,
+        [pltpu.VMEM(blocks.shape, blocks.dtype), shape_of((8, BLK), F32)],
+        [VM, VM],
+        [pltpu.with_memory_space_constraint(blocks, pltpu.VMEM), after],
+        moved=2 * blocks.size,
+    )
+
+
 def model_to_hidden(layout, rows_cols, shards, which, blocks, forward, hidden_blocks, n_row, after=()):
     count = len(shards)
     _, part, width = shards[0].shape
@@ -332,7 +355,7 @@
                 other_full[model_blocks] = jnp.zeros((tokens, BLK), BF16)
                 other_ref = other_full
             copies = send_products(layout, row_ref, col_ref, full, other_ref, made, grad, done)
-        work = add_forward if forward else add_backward
+        work = add_forward if forward else functools.partial(add_backward, turned=True)
         work(layout, row_ref, col_ref, 0, layout.groups, full, weights, total)
         me = lax.axis_index("col")
         for entry in range(half):
@@ -457,14 +480,14 @@
     return call(body, outs, [VM] * (2 + len(parts)), [own, bias, *parts], moved=own.size * 20)
 
 
-def scale_by_slope(own, parts, slope):
-    def body(own_ref, slope_ref, *refs):
+def scale_by_slope(own, parts, slope, after):
+    def body(own_ref, slope_ref, after_ref, *refs):
         parts, (out_ref, token) = refs[:-2], refs[-2:]
         out_ref[...] = (add_up(own_ref, parts) * slope_ref[...]).astype(BF16)
         token[...] = jnp.zeros_like(token)
 
     outs = [shape_of(own.shape, BF16), shape_of((8, BLK), F32)]
-    return call(body, outs, [VM] * (2 + len(parts)), [own, slope, *parts], moved=own.size * 16)
+    return call(body, outs, [VM] * (3 + len(parts)), [own, slope, after, *parts], moved=own.size * 16)
 
 
 def pair_sums(*pairs):
@@ -542,7 +565,8 @@
 
     activated, slope = activate(hidden_own, hidden_parts, bias_wide)
     activated_shares = gather_row(activated, n_row)
-    grad_hidden, grad_there = scale_by_slope(act_own, act_parts, slope)
+    first_turned, turned_there = turn(first_held, slope)
+    grad_hidden, grad_there = scale_by_slope(act_own, act_parts, slope, turned_there)
     met = swap(grad_there, "col", n_col, 1)
     grad_later = follow(grad_hidden, met)
     grad_shares = [grad_hidden]
@@ -554,7 +578,7 @@
     )
     out_came = swap(out_send, "col", n_col, 1)
     in_keep, in_send = hidden_to_model(
-        first, first_at, grad_shares, first_held, False, model_blocks, n_col, after=(out_done,)
+        first, first_at, grad_shares, first_turned, False, model_blocks, n_col, after=(out_done,)
     )
     in_came = swap(in_send, "col", n_col, 1)
     owns, sends = pair_sums((out_keep, out_came), (in_keep, in_came))

time: 79.9 us -> 78.5 us (0.982)
  waiting for transfers between devices: 11.6 us -> 5.12 us
  local copies, waits for them, and re-layouts: 0.01 us -> 3.75 us
  Pallas kernels: 40.5 us -> 41.8 us
    ppermute x25, waiting for transfers between devices: 11.6 us -> 5.12 us  [swap(): lax.ppermute(array, axis, [(place, place ^ mask) for place in range(size)])]
    unnamed x2 -> x6, local copies, waits for them, and re-layouts: 0.01 us -> 3.75 us
    pallas_call x17 -> x18, Pallas kernels: 40.5 us -> 41.8 us  [call(): pl.pallas_call(body, out_shape=outs, in_specs=in_specs, out_specs=[whole]...]
  transfers between devices with their start and end apart: 25 -> 25, of which waited for: 6 -> 6; matrix products, arithmetic and copies ran while one was open for 0% -> 0% of each run, Pallas kernels for 44% -> 47%
where the time goes in v5:
time: 78.5 us; the launch traced here: 78.2 us
  Pallas kernels  41.8 us (53%)
  starting transfers between devices  26.6 us (34%)
  waiting for transfers between devices  5.12 us (7%)
  local copies, waits for them, and re-layouts  3.75 us (5%)
  between operations  0.87 us (1%)
    pallas_call x18, Pallas kernels, call(): pl.pallas_call(body, out_shape=outs, in_specs=in_specs, out_specs=[whole]...  41.8 us
    ppermute x25, starting transfers between devices, swap(): lax.ppermute(array, axis, [(place, place ^ mask) for place in range(size)])  26.6 us
    ppermute x25, waiting for transfers between devices, swap(): lax.ppermute(array, axis, [(place, place ^ mask) for place in range(size)])  5.12 us
    unnamed x6, local copies, waits for them, and re-layouts  3.75 us
  transfers between devices with their start and end apart: 25, of which 6 were waited for; matrix products, arithmetic and copies ran while one was open for 0% of the time, Pallas kernels for 47%

profile of v5, /device:TPU:0, one launch (start us, length us, event | category | flops | bytes accessed | tf_op | source)
XLA Modules:
  0.0 78.2 jit_solution(4762908388122023489)
XLA Ops:
  0.6 0.8 %shard_map.111.refs_0_ = bf16[2,8,3072]{2,1,0:T(8,128)(2,1)S(1)} custom-call(bf16[8,3072]{1,0:T(8,128)(2,1)} %first_ref.1, bf16[8,3072]{1,0:T(8,128)(2,1)} %second_ref.1), custom_call_target="tpu_custom_call" | custom-call | bytes 196608 | tf_op jit(solution)/shard_map/pallas_call | solution.py:39
  1.5 3.1 %collective-permute-start.1 = (bf16[2,8,3072]{2,1,0:T(8,128)(2,1)S(1)}, bf16[2,8,3072]{2,1,0:T(8,128)(2,1)S(1)}, u32[]{:S(2)}, u32[]{:S(2)}) collective-permute-start(bf16[2,8,3072]{2,1,0:T(8,128)(2,1)S(1)} %shard_map.111.refs_0_), channel_id=1, source_target_pairs={{0,2},{1,3},{2,0},{3,1},{4,6},{5,7},{6,4},{7,5},{8,10},{9,11},{10,... | collective-permute-start | bytes 294920 | tf_op jit(solution)/shard_map/ppermute | solution.py:33
  4.5 2.6 %collective-permute-start.3 = (bf16[2,8,3072]{2,1,0:T(8,128)(2,1)S(1)}, bf16[2,8,3072]{2,1,0:T(8,128)(2,1)S(1)}, u32[]{:S(2)}, u32[]{:S(2)}) collective-permute-start(bf16[2,8,3072]{2,1,0:T(8,128)(2,1)S(1)} %shard_map.111.refs_0_), channel_id=1, source_target_pairs={{0,4},{1,5},{2,6},{3,7},{4,0},{5,1},{6,2},{7,3},{8,12},{9,13},{10,... | collective-permute-start | bytes 294920 | tf_op jit(solution)/shard_map/ppermute | solution.py:33
  7.1 0.0 collective-permute-start.5
  7.1 0.0 collective-permute-start
  7.1 3.7 %shard_map.112 = (bf16[288,128,128]{2,1,0:T(8,128)(2,1)S(1)}, f32[8,128]{1,0:T(8,128)S(1)}) custom-call(bf16[288,128,128]{2,1,0:T(8,128)(2,1)} %bitcast.9), custom_call_target="tpu_custom_call" | custom-call | bytes 18874368 | tf_op jit(solution)/shard_map/pallas_call | solution.py:39
  10.8 3.7 %shard_map.113 = (bf16[288,128,128]{2,1,0:T(8,128)(2,1)S(1)}, f32[8,128]{1,0:T(8,128)S(1)}) custom-call(bf16[288,128,128]{2,1,0:T(8,128)(2,1)} %bitcast.10), custom_call_target="tpu_custom_call" | custom-call | bytes 18874368 | tf_op jit(solution)/shard_map/pallas_call | solution.py:39
  14.5 0.0 collective-permute-done.1.array_ref
  14.6 0.6 collective-permute-start.2
  15.1 0.0 collective-permute-done.3.array_ref
  15.1 0.1 collective-permute-start.4
  15.2 0.0 collective-permute-done.5.array_ref
  15.2 0.5 collective-permute-start.6
  15.8 1.0 %shard_map.110 = (s32[24,128]{1,0:T(8,128)S(1)}, s32[48,128]{1,0:T(8,128)S(1)}) custom-call(s32[24,48]{1,0:T(8,128)} %refs_0_.1, s32[24,48]{1,0:T(8,128)} %bitcast.11), custom_call_target="tpu_custom_call" | custom-call | tf_op jit(solution)/shard_map/pallas_call | solution.py:39
  16.8 0.0 collective-permute-done.refs_1_
  16.8 0.0 collective-permute-done.2.refs_3_
  16.8 0.0 collective-permute-done.4.refs_5_
  16.9 0.0 collective-permute-done.6.refs_7_
  16.9 0.0 copy-start.2
  16.9 3.5 %shard_map.117 = (f32[48,16,128]{2,1,0:T(8,128)S(1)}, bf16[48,16,128]{2,1,0:T(8,128)(2,1)S(1)}, bf16[48,16,128]{2,1,0:T(8,128)(2,1)S(1)}, bf16[48,16,128]{2,1,0:T(8,128)(2,1)S(1)}, bf16[24,64,128]{2,1,0:T(8,128)(2,1)S(1)}) custom-call(s32[24,128]{1,0:T(8,128)S(1)} %get-tuple-element.43.row_ref.col_ref, s32[24,128]{1,0:T(8,128)S(1)} %get-tuple-element.43.row_ref.col_ref, ...), custom_call_target="tpu_custom_call" | custom-call | flops 603979776 | bytes 9437184 | tf_op jit(solution)/shard_map/pallas_call | solution.py:39
  20.4 1.8 %collective-permute-start.7 = (bf16[48,16,128]{2,1,0:T(8,128)(2,1)S(1)}, bf16[48,16,128]{2,1,0:T(8,128)(2,1)S(1)}, u32[]{:S(2)}, u32[]{:S(2)}) collective-permute-start(bf16[48,16,128]{2,1,0:T(8,128)(2,1)S(1)} %get-tuple-element.48), channel_id=1, source_target_pairs={{0,8},{8,0},{16,24},{24,16},{1,9},{9,1},{17,25},{25,17},{2,10},{10... | collective-permute-start | bytes 589832 | tf_op jit(solution)/shard_map/ppermute | solution.py:33
  22.2 1.5 %collective-permute-start.8 = (bf16[48,16,128]{2,1,0:T(8,128)(2,1)S(1)}, bf16[48,16,128]{2,1,0:T(8,128)(2,1)S(1)}, u32[]{:S(2)}, u32[]{:S(2)}) collective-permute-start(bf16[48,16,128]{2,1,0:T(8,128)(2,1)S(1)} %get-tuple-element.49), channel_id=1, source_target_pairs={{0,16},{8,24},{16,0},{24,8},{1,17},{9,25},{17,1},{25,9},{2,18},{10... | collective-permute-start | bytes 589832 | tf_op jit(solution)/shard_map/ppermute | solution.py:33
  23.7 0.3 collective-permute-start.9
  24.0 4.8 %shard_map.119 = (f32[48,16,128]{2,1,0:T(8,128)S(1)}, bf16[48,16,128]{2,1,0:T(8,128)(2,1)S(1)}, bf16[48,16,128]{2,1,0:T(8,128)(2,1)S(1)}, bf16[48,16,128]{2,1,0:T(8,128)(2,1)S(1)}, bf16[24,64,128]{2,1,0:T(8,128)(2,1)S(1)}) custom-call(s32[48,128]{1,0:T(8,128)S(1)} %get-tuple-element.42.row_ref.col_ref, s32[48,128]{1,0:T(8,128)S(1)} %get-tuple-element.42.row_ref.col_ref, ...), custom_call_target="tpu_custom_call" | custom-call | flops 603979776 | bytes 9437184 | tf_op jit(solution)/shard_map/pallas_call | solution.py:39
  28.8 1.8 %collective-permute-start.14 = (bf16[48,16,128]{2,1,0:T(8,128)(2,1)S(1)}, bf16[48,16,128]{2,1,0:T(8,128)(2,1)S(1)}, u32[]{:S(2)}, u32[]{:S(2)}) collective-permute-start(bf16[48,16,128]{2,1,0:T(8,128)(2,1)S(1)} %get-tuple-element.60), channel_id=1, source_target_pairs={{0,8},{8,0},{16,24},{24,16},{1,9},{9,1},{17,25},{25,17},{2,10},{10... | collective-permute-start | bytes 589832 | tf_op jit(solution)/shard_map/ppermute | solution.py:33
  30.6 1.6 %collective-permute-start.15 = (bf16[48,16,128]{2,1,0:T(8,128)(2,1)S(1)}, bf16[48,16,128]{2,1,0:T(8,128)(2,1)S(1)}, u32[]{:S(2)}, u32[]{:S(2)}) collective-permute-start(bf16[48,16,128]{2,1,0:T(8,128)(2,1)S(1)} %get-tuple-element.61), channel_id=1, source_target_pairs={{0,16},{8,24},{16,0},{24,8},{1,17},{9,25},{17,1},{25,9},{2,18},{10... | collective-permute-start | bytes 589832 | tf_op jit(solution)/shard_map/ppermute | solution.py:33
  32.1 0.0 collective-permute-done.7.refs_0_
  32.1 0.2 collective-permute-start.16
  32.4 0.5 collective-permute-done.8.refs_1_
  32.9 0.8 collective-permute-done.9.refs_2_
  33.6 0.4 shard_map.118
  34.0 1.5 %collective-permute-start.12 = (bf16[48,16,128]{2,1,0:T(8,128)(2,1)S(1)}, bf16[48,16,128]{2,1,0:T(8,128)(2,1)S(1)}, u32[]{:S(2)}, u32[]{:S(2)}) collective-permute-start(bf16[48,16,128]{2,1,0:T(8,128)(2,1)S(1)} %get-tuple-element.51.refs_0_), channel_id=1, source_target_pairs={{0,24},{8,16},{16,8},{24,0},{1,25},{9,17},{17,9},{25,1},{2,26},{10... | collective-permute-start | bytes 589832 | tf_op jit(solution)/shard_map/ppermute | solution.py:33
  35.6 1.4 %collective-permute-start.11 = (bf16[48,16,128]{2,1,0:T(8,128)(2,1)S(1)}, bf16[48,16,128]{2,1,0:T(8,128)(2,1)S(1)}, u32[]{:S(2)}, u32[]{:S(2)}) collective-permute-start(bf16[48,16,128]{2,1,0:T(8,128)(2,1)S(1)} %get-tuple-element.51.refs_0_), channel_id=1, source_target_pairs={{0,16},{8,24},{16,0},{24,8},{1,17},{9,25},{17,1},{25,9},{2,18},{10... | collective-permute-start | bytes 589832 | tf_op jit(solution)/shard_map/ppermute | solution.py:33
  37.0 0.0 collective-permute-done.14.refs_0_
  37.0 1.4 %collective-permute-start.10 = (bf16[48,16,128]{2,1,0:T(8,128)(2,1)S(1)}, bf16[48,16,128]{2,1,0:T(8,128)(2,1)S(1)}, u32[]{:S(2)}, u32[]{:S(2)}) collective-permute-start(bf16[48,16,128]{2,1,0:T(8,128)(2,1)S(1)} %get-tuple-element.51.refs_0_), channel_id=1, source_target_pairs={{0,8},{8,0},{16,24},{24,16},{1,9},{9,1},{17,25},{25,17},{2,10},{10... | collective-permute-start | bytes 589832 | tf_op jit(solution)/shard_map/ppermute | solution.py:33
  38.4 2.8 %shard_map.121 = (bf16[288,128,128]{2,1,0:T(8,128)(2,1)S(1)}, f32[8,128]{1,0:T(8,128)S(1)}) custom-call(bf16[288,128,128]{2,1,0:T(8,128)(2,1)S(1)} %get-tuple-element.46.refs_8_.from_ref, f32[48,16,128]{2,1,0:T(8,128)S(1)} %get-tuple-element.58.after_ref.slope_ref), custom_call_target="tpu_custom_call" | custom-call | bytes 9437184 | tf_op jit(solution)/shard_map/pallas_call | solution.py:39
  41.1 0.0 copy-start
  41.1 3.7 %copy-done = bf16[288,128,128]{2,1,0:T(8,128)(2,1)} copy-done((bf16[288,128,128]{2,1,0:T(8,128)(2,1)}, bf16[288,128,128]{2,1,0:T(8,128)(2,1)S(1)}, u32[]{:S(2)}) %copy-start) | copy-done | bytes 9437208
  44.9 1.7 %collective-permute-done.15.refs_1_ = bf16[48,16,128]{2,1,0:T(8,128)(2,1)S(1)} collective-permute-done((bf16[48,16,128]{2,1,0:T(8,128)(2,1)S(1)}, bf16[48,16,128]{2,1,0:T(8,128)(2,1)S(1)}, u32[]{:S(2)}, u32[]{:S(2)}) %collective-permute-start.15) | collective-permute-done | bytes 196640 | tf_op jit(solution)/shard_map/ppermute | solution.py:33
  46.6 0.0 collective-permute-done.16.refs_2_
  46.6 0.1 shard_map.122
  46.7 0.1 collective-permute-start.17
  46.8 1.6 %collective-permute-start.20 = (bf16[48,16,128]{2,1,0:T(8,128)(2,1)S(1)}, bf16[48,16,128]{2,1,0:T(8,128)(2,1)S(1)}, u32[]{:S(2)}, u32[]{:S(2)}) collective-permute-start(bf16[48,16,128]{2,1,0:T(8,128)(2,1)S(1)} %get-tuple-element.63.array_ref.refs_0_), channel_id=1, source_target_pairs={{0,24},{8,16},{16,8},{24,0},{1,25},{9,17},{17,9},{25,1},{2,26},{10... | collective-permute-start | bytes 589832 | tf_op jit(solution)/shard_map/ppermute | solution.py:33
  48.4 0.0 collective-permute-done.17.refs_0_
  48.4 1.5 %collective-permute-start.19 = (bf16[48,16,128]{2,1,0:T(8,128)(2,1)S(1)}, bf16[48,16,128]{2,1,0:T(8,128)(2,1)S(1)}, u32[]{:S(2)}, u32[]{:S(2)}) collective-permute-start(bf16[48,16,128]{2,1,0:T(8,128)(2,1)S(1)} %shard_map.123), channel_id=1, source_target_pairs={{0,16},{8,24},{16,0},{24,8},{1,17},{9,25},{17,1},{25,9},{2,18},{10... | collective-permute-start | bytes 589832 | tf_op jit(solution)/shard_map/ppermute | solution.py:33
  49.8 0.0 collective-permute-done.12.refs_3_
  49.8 0.6 collective-permute-start.18
  50.4 0.0 collective-permute-done.11.refs_2_
  50.4 8.4 %shard_map.120 = (f32[4,8,3072]{2,1,0:T(8,128)S(1)}, bf16[4,8,3072]{2,1,0:T(8,128)(2,1)S(1)}, f32[8,128]{1,0:T(8,128)S(1)}, f32[288,128,128]{2,1,0:T(8,128)}) custom-call(s32[48,128]{1,0:T(8,128)S(1)} %get-tuple-element.42.row_ref.col_ref, s32[48,128]{1,0:T(8,128)S(1)} %get-tuple-element.42.row_ref.col_ref, ...), custom_call_target="tpu_custom_call" | custom-call | flops 1207959552 | bytes 28311552 | tf_op jit(solution)/shard_map/pallas_call | solution.py:39
  58.8 0.1 collective-permute-start.13
  58.9 0.3 collective-permute-done.19.refs_2_
  59.2 0.4 collective-permute-done.18.refs_1_
  59.6 3.2 %shard_map.124 = (f32[4,8,3072]{2,1,0:T(8,128)S(1)}, bf16[4,8,3072]{2,1,0:T(8,128)(2,1)S(1)}) custom-call(s32[24,128]{1,0:T(8,128)S(1)} %get-tuple-element.43.row_ref.col_ref, s32[24,128]{1,0:T(8,128)S(1)} %get-tuple-element.43.row_ref.col_ref, bf16[48,16,128]{2,1,0:T(8,128)(2,1)S(1)} %get-tuple-element.63.array_ref.refs_0_, ...), custom_call_target="tpu_custom_call" | custom-call | flops 603979776 | bytes 9437184 | tf_op jit(solution)/shard_map/pallas_call | solution.py:39
  62.9 0.1 collective-permute-start.21
  62.9 0.0 collective-permute-done.13.refs_1_
  62.9 1.4 %collective-permute-done.21.refs_3_ = bf16[4,8,3072]{2,1,0:T(8,128)(2,1)S(1)} collective-permute-done((bf16[4,8,3072]{2,1,0:T(8,128)(2,1)S(1)}, bf16[4,8,3072]{2,1,0:T(8,128)(2,1)S(1)}, u32[]{:S(2)}, u32[]{:S(2)}) %collective-permute-start.21) | collective-permute-done | bytes 196640 | tf_op jit(solution)/shard_map/ppermute | solution.py:33
  64.4 0.1 shard_map.125
  64.4 0.9 %collective-permute-start.22 = (bf16[2,8,3072]{2,1,0:T(8,128)(2,1)S(1)}, bf16[2,8,3072]{2,1,0:T(8,128)(2,1)S(1)}, u32[]{:S(2)}, u32[]{:S(2)}) collective-permute-start(bf16[2,8,3072]{2,1,0:T(8,128)(2,1)S(1)} %get-tuple-element.71), channel_id=1, source_target_pairs={{0,2},{1,3},{2,0},{3,1},{4,6},{5,7},{6,4},{7,5},{8,10},{9,11},{10,... | collective-permute-start | bytes 294920 | tf_op jit(solution)/shard_map/ppermute | solution.py:33
  65.4 3.3 %collective-permute-start.23 = (bf16[2,8,3072]{2,1,0:T(8,128)(2,1)S(1)}, bf16[2,8,3072]{2,1,0:T(8,128)(2,1)S(1)}, u32[]{:S(2)}, u32[]{:S(2)}) collective-permute-start(bf16[2,8,3072]{2,1,0:T(8,128)(2,1)S(1)} %get-tuple-element.72), channel_id=1, source_target_pairs={{0,4},{1,5},{2,6},{3,7},{4,0},{5,1},{6,2},{7,3},{8,12},{9,13},{10,... | collective-permute-start | bytes 294920 | tf_op jit(solution)/shard_map/ppermute | solution.py:33
  68.7 0.2 collective-permute-start.24
  68.9 8.6 %shard_map.127 = (f32[288,128,128]{2,1,0:T(8,128)}, f32[48,128]{1,0:T(8,128)}) custom-call(s32[24,128]{1,0:T(8,128)S(1)} %get-tuple-element.43.row_ref.col_ref, s32[24,128]{1,0:T(8,128)S(1)} %get-tuple-element.43.row_ref.col_ref, bf16[24,64,128]{2,1,0:T(8,128)(2,1)S(1)} %get-tuple-element.52.refs_8_.left_ref, ...), custom_call_target="tpu_custom_call" | custom-call | flops 603979776 | bytes 18874368 | tf_op jit(solution)/shard_map/pallas_call | solution.py:39
  77.5 0.0 collective-permute-done.22.refs_2_
  77.5 0.0 collective-permute-done.24.refs_4_
  77.5 0.7 shard_map.126
  (11 shorter events, 0.1 us)
Async XLA Ops:
  1.5 13.1 %collective-permute-start.1 = (bf16[2,8,3072]{2,1,0:T(8,128)(2,1)S(1)}, bf16[2,8,3072]{2,1,0:T(8,128)(2,1)S(1)}, u32[]{:S(2)}, u32[]{:S(2)}) collective-permute-start(bf16[2,8,3072]{2,1,0:T(8,128)(2,1)S(1)} %shard_map.111.refs_0_), channel_id=1, source_target_pairs={{0,2},{1,3},{2,0},{3,1},{4,6},{5,7},{6,4},{7,5},{8,10},{9,11},{10,... | collective-permute-start | bytes 294920 | tf_op jit(solution)/shard_map/ppermute | solution.py:33
  4.5 10.6 %collective-permute-start.3 = (bf16[2,8,3072]{2,1,0:T(8,128)(2,1)S(1)}, bf16[2,8,3072]{2,1,0:T(8,128)(2,1)S(1)}, u32[]{:S(2)}, u32[]{:S(2)}) collective-permute-start(bf16[2,8,3072]{2,1,0:T(8,128)(2,1)S(1)} %shard_map.111.refs_0_), channel_id=1, source_target_pairs={{0,4},{1,5},{2,6},{3,7},{4,0},{5,1},{6,2},{7,3},{8,12},{9,13},{10,... | collective-permute-start | bytes 294920 | tf_op jit(solution)/shard_map/ppermute | solution.py:33
  7.1 8.1 %collective-permute-start.5 = (bf16[2,8,3072]{2,1,0:T(8,128)(2,1)S(1)}, bf16[2,8,3072]{2,1,0:T(8,128)(2,1)S(1)}, u32[]{:S(2)}, u32[]{:S(2)}) collective-permute-start(bf16[2,8,3072]{2,1,0:T(8,128)(2,1)S(1)} %shard_map.111.refs_0_), channel_id=1, source_target_pairs={{0,6},{1,7},{2,4},{3,5},{4,2},{5,3},{6,0},{7,1},{8,14},{9,15},{10,... | collective-permute-start | bytes 294920 | tf_op jit(solution)/shard_map/ppermute | solution.py:33
  7.1 9.7 %collective-permute-start = (bf16[2,8,3072]{2,1,0:T(8,128)(2,1)S(1)}, bf16[2,8,3072]{2,1,0:T(8,128)(2,1)S(1)}, u32[]{:S(2)}, u32[]{:S(2)}) collective-permute-start(bf16[2,8,3072]{2,1,0:T(8,128)(2,1)S(1)} %shard_map.111.refs_0_), channel_id=1, source_target_pairs={{0,1},{1,0},{2,3},{3,2},{4,5},{5,4},{6,7},{7,6},{8,9},{9,8},{10,11... | collective-permute-start | bytes 294920 | tf_op jit(solution)/shard_map/ppermute | solution.py:33
  14.6 2.3 %collective-permute-start.2 = (bf16[2,8,3072]{2,1,0:T(8,128)(2,1)S(1)}, bf16[2,8,3072]{2,1,0:T(8,128)(2,1)S(1)}, u32[]{:S(2)}, u32[]{:S(2)}) collective-permute-start(bf16[2,8,3072]{2,1,0:T(8,128)(2,1)S(1)} %shard_map.114.refs_2_), channel_id=1, source_target_pairs={{0,1},{1,0},{2,3},{3,2},{4,5},{5,4},{6,7},{7,6},{8,9},{9,8},{10,11... | collective-permute-start | bytes 294920 | tf_op jit(solution)/shard_map/ppermute | solution.py:33
  15.1 1.7 %collective-permute-start.4 = (bf16[2,8,3072]{2,1,0:T(8,128)(2,1)S(1)}, bf16[2,8,3072]{2,1,0:T(8,128)(2,1)S(1)}, u32[]{:S(2)}, u32[]{:S(2)}) collective-permute-start(bf16[2,8,3072]{2,1,0:T(8,128)(2,1)S(1)} %shard_map.115.refs_4_), channel_id=1, source_target_pairs={{0,1},{1,0},{2,3},{3,2},{4,5},{5,4},{6,7},{7,6},{8,9},{9,8},{10,11... | collective-permute-start | bytes 294920 | tf_op jit(solution)/shard_map/ppermute | solution.py:33
  15.2 1.6 %collective-permute-start.6 = (bf16[2,8,3072]{2,1,0:T(8,128)(2,1)S(1)}, bf16[2,8,3072]{2,1,0:T(8,128)(2,1)S(1)}, u32[]{:S(2)}, u32[]{:S(2)}) collective-permute-start(bf16[2,8,3072]{2,1,0:T(8,128)(2,1)S(1)} %shard_map.116.refs_6_), channel_id=1, source_target_pairs={{0,1},{1,0},{2,3},{3,2},{4,5},{5,4},{6,7},{7,6},{8,9},{9,8},{10,11... | collective-permute-start | bytes 294920 | tf_op jit(solution)/shard_map/ppermute | solution.py:33
  16.9 15.5 %copy-start.2 = (bf16[6144]{0:T(1024)(128)(2,1)S(1)}, bf16[6144]{0:T(1024)(128)(2,1)}, u32[]{:S(2)}) copy-start(bf16[6144]{0:T(1024)(128)(2,1)} %param.11) | copy-start | bytes 36868
  20.4 11.7 %collective-permute-start.7 = (bf16[48,16,128]{2,1,0:T(8,128)(2,1)S(1)}, bf16[48,16,128]{2,1,0:T(8,128)(2,1)S(1)}, u32[]{:S(2)}, u32[]{:S(2)}) collective-permute-start(bf16[48,16,128]{2,1,0:T(8,128)(2,1)S(1)} %get-tuple-element.48), channel_id=1, source_target_pairs={{0,8},{8,0},{16,24},{24,16},{1,9},{9,1},{17,25},{25,17},{2,10},{10... | collective-permute-start | bytes 589832 | tf_op jit(solution)/shard_map/ppermute | solution.py:33
  22.2 10.7 %collective-permute-start.8 = (bf16[48,16,128]{2,1,0:T(8,128)(2,1)S(1)}, bf16[48,16,128]{2,1,0:T(8,128)(2,1)S(1)}, u32[]{:S(2)}, u32[]{:S(2)}) collective-permute-start(bf16[48,16,128]{2,1,0:T(8,128)(2,1)S(1)} %get-tuple-element.49), channel_id=1, source_target_pairs={{0,16},{8,24},{16,0},{24,8},{1,17},{9,25},{17,1},{25,9},{2,18},{10... | collective-permute-start | bytes 589832 | tf_op jit(solution)/shard_map/ppermute | solution.py:33
  23.7 9.9 %collective-permute-start.9 = (bf16[48,16,128]{2,1,0:T(8,128)(2,1)S(1)}, bf16[48,16,128]{2,1,0:T(8,128)(2,1)S(1)}, u32[]{:S(2)}, u32[]{:S(2)}) collective-permute-start(bf16[48,16,128]{2,1,0:T(8,128)(2,1)S(1)} %get-tuple-element.50), channel_id=1, source_target_pairs={{0,24},{8,16},{16,8},{24,0},{1,25},{9,17},{17,9},{25,1},{2,26},{10... | collective-permute-start | bytes 589832 | tf_op jit(solution)/shard_map/ppermute | solution.py:33
  28.8 8.2 %collective-permute-start.14 = (bf16[48,16,128]{2,1,0:T(8,128)(2,1)S(1)}, bf16[48,16,128]{2,1,0:T(8,128)(2,1)S(1)}, u32[]{:S(2)}, u32[]{:S(2)}) collective-permute-start(bf16[48,16,128]{2,1,0:T(8,128)(2,1)S(1)} %get-tuple-element.60), channel_id=1, source_target_pairs={{0,8},{8,0},{16,24},{24,16},{1,9},{9,1},{17,25},{25,17},{2,10},{10... | collective-permute-start | bytes 589832 | tf_op jit(solution)/shard_map/ppermute | solution.py:33
  30.6 16.0 %collective-permute-start.15 = (bf16[48,16,128]{2,1,0:T(8,128)(2,1)S(1)}, bf16[48,16,128]{2,1,0:T(8,128)(2,1)S(1)}, u32[]{:S(2)}, u32[]{:S(2)}) collective-permute-start(bf16[48,16,128]{2,1,0:T(8,128)(2,1)S(1)} %get-tuple-element.61), channel_id=1, source_target_pairs={{0,16},{8,24},{16,0},{24,8},{1,17},{9,25},{17,1},{25,9},{2,18},{10... | collective-permute-start | bytes 589832 | tf_op jit(solution)/shard_map/ppermute | solution.py:33
  32.1 14.4 %collective-permute-start.16 = (bf16[48,16,128]{2,1,0:T(8,128)(2,1)S(1)}, bf16[48,16,128]{2,1,0:T(8,128)(2,1)S(1)}, u32[]{:S(2)}, u32[]{:S(2)}) collective-permute-start(bf16[48,16,128]{2,1,0:T(8,128)(2,1)S(1)} %get-tuple-element.62), channel_id=1, source_target_pairs={{0,24},{8,16},{16,8},{24,0},{1,25},{9,17},{17,9},{25,1},{2,26},{10... | collective-permute-start | bytes 589832 | tf_op jit(solution)/shard_map/ppermute | solution.py:33
  34.0 15.8 %collective-permute-start.12 = (bf16[48,16,128]{2,1,0:T(8,128)(2,1)S(1)}, bf16[48,16,128]{2,1,0:T(8,128)(2,1)S(1)}, u32[]{:S(2)}, u32[]{:S(2)}) collective-permute-start(bf16[48,16,128]{2,1,0:T(8,128)(2,1)S(1)} %get-tuple-element.51.refs_0_), channel_id=1, source_target_pairs={{0,24},{8,16},{16,8},{24,0},{1,25},{9,17},{17,9},{25,1},{2,26},{10... | collective-permute-start | bytes 589832 | tf_op jit(solution)/shard_map/ppermute | solution.py:33
  35.6 14.9 %collective-permute-start.11 = (bf16[48,16,128]{2,1,0:T(8,128)(2,1)S(1)}, bf16[48,16,128]{2,1,0:T(8,128)(2,1)S(1)}, u32[]{:S(2)}, u32[]{:S(2)}) collective-permute-start(bf16[48,16,128]{2,1,0:T(8,128)(2,1)S(1)} %get-tuple-element.51.refs_0_), channel_id=1, source_target_pairs={{0,16},{8,24},{16,0},{24,8},{1,17},{9,25},{17,1},{25,9},{2,18},{10... | collective-permute-start | bytes 589832 | tf_op jit(solution)/shard_map/ppermute | solution.py:33
  37.0 13.4 %collective-permute-start.10 = (bf16[48,16,128]{2,1,0:T(8,128)(2,1)S(1)}, bf16[48,16,128]{2,1,0:T(8,128)(2,1)S(1)}, u32[]{:S(2)}, u32[]{:S(2)}) collective-permute-start(bf16[48,16,128]{2,1,0:T(8,128)(2,1)S(1)} %get-tuple-element.51.refs_0_), channel_id=1, source_target_pairs={{0,8},{8,0},{16,24},{24,16},{1,9},{9,1},{17,25},{25,17},{2,10},{10... | collective-permute-start | bytes 589832 | tf_op jit(solution)/shard_map/ppermute | solution.py:33
  41.1 3.7 %copy-start = (bf16[288,128,128]{2,1,0:T(8,128)(2,1)}, bf16[288,128,128]{2,1,0:T(8,128)(2,1)S(1)}, u32[]{:S(2)}) copy-start(bf16[288,128,128]{2,1,0:T(8,128)(2,1)S(1)} %get-tuple-element.66.refs_5_) | copy-start | bytes 28311556
  46.6 13.0 %copy-start.1 = (bf16[288,128,128]{2,1,0:T(8,128)(2,1)S(1)}, bf16[288,128,128]{2,1,0:T(8,128)(2,1)}, u32[]{:S(2)}) copy-start(bf16[288,128,128]{2,1,0:T(8,128)(2,1)} %copy-done) | copy-start | bytes 28311556
  46.7 1.7 %collective-permute-start.17 = (f32[8,128]{1,0:T(8,128)S(1)}, f32[8,128]{1,0:T(8,128)S(1)}, u32[]{:S(2)}, u32[]{:S(2)}) collective-permute-start(f32[8,128]{1,0:T(8,128)S(1)} %get-tuple-element.64), channel_id=1, source_target_pairs={{0,1},{1,0},{2,3},{3,2},{4,5},{5,4},{6,7},{7,6},{8,9},{9,8},{10,11... | collective-permute-start | bytes 12296 | tf_op jit(solution)/shard_map/ppermute | solution.py:33
  46.8 12.1 %collective-permute-start.20 = (bf16[48,16,128]{2,1,0:T(8,128)(2,1)S(1)}, bf16[48,16,128]{2,1,0:T(8,128)(2,1)S(1)}, u32[]{:S(2)}, u32[]{:S(2)}) collective-permute-start(bf16[48,16,128]{2,1,0:T(8,128)(2,1)S(1)} %get-tuple-element.63.array_ref.refs_0_), channel_id=1, source_target_pairs={{0,24},{8,16},{16,8},{24,0},{1,25},{9,17},{17,9},{25,1},{2,26},{10... | collective-permute-start | bytes 589832 | tf_op jit(solution)/shard_map/ppermute | solution.py:33
  48.4 10.8 %collective-permute-start.19 = (bf16[48,16,128]{2,1,0:T(8,128)(2,1)S(1)}, bf16[48,16,128]{2,1,0:T(8,128)(2,1)S(1)}, u32[]{:S(2)}, u32[]{:S(2)}) collective-permute-start(bf16[48,16,128]{2,1,0:T(8,128)(2,1)S(1)} %shard_map.123), channel_id=1, source_target_pairs={{0,16},{8,24},{16,0},{24,8},{1,17},{9,25},{17,1},{25,9},{2,18},{10... | collective-permute-start | bytes 589832 | tf_op jit(solution)/shard_map/ppermute | solution.py:33
  49.8 9.8 %collective-permute-start.18 = (bf16[48,16,128]{2,1,0:T(8,128)(2,1)S(1)}, bf16[48,16,128]{2,1,0:T(8,128)(2,1)S(1)}, u32[]{:S(2)}, u32[]{:S(2)}) collective-permute-start(bf16[48,16,128]{2,1,0:T(8,128)(2,1)S(1)} %shard_map.123), channel_id=1, source_target_pairs={{0,8},{8,0},{16,24},{24,16},{1,9},{9,1},{17,25},{25,17},{2,10},{10... | collective-permute-start | bytes 589832 | tf_op jit(solution)/shard_map/ppermute | solution.py:33
  58.8 4.1 %collective-permute-start.13 = (bf16[4,8,3072]{2,1,0:T(8,128)(2,1)S(1)}, bf16[4,8,3072]{2,1,0:T(8,128)(2,1)S(1)}, u32[]{:S(2)}, u32[]{:S(2)}) collective-permute-start(bf16[4,8,3072]{2,1,0:T(8,128)(2,1)S(1)} %get-tuple-element.56), channel_id=1, source_target_pairs={{0,1},{1,0},{2,3},{3,2},{4,5},{5,4},{6,7},{7,6},{8,9},{9,8},{10,11... | collective-permute-start | bytes 589832 | tf_op jit(solution)/shard_map/ppermute | solution.py:33
  62.9 1.5 %collective-permute-start.21 = (bf16[4,8,3072]{2,1,0:T(8,128)(2,1)S(1)}, bf16[4,8,3072]{2,1,0:T(8,128)(2,1)S(1)}, u32[]{:S(2)}, u32[]{:S(2)}) collective-permute-start(bf16[4,8,3072]{2,1,0:T(8,128)(2,1)S(1)} %get-tuple-element.68), channel_id=1, source_target_pairs={{0,1},{1,0},{2,3},{3,2},{4,5},{5,4},{6,7},{7,6},{8,9},{9,8},{10,11... | collective-permute-start | bytes 589832 | tf_op jit(solution)/shard_map/ppermute | solution.py:33
  64.4 13.0 %collective-permute-start.22 = (bf16[2,8,3072]{2,1,0:T(8,128)(2,1)S(1)}, bf16[2,8,3072]{2,1,0:T(8,128)(2,1)S(1)}, u32[]{:S(2)}, u32[]{:S(2)}) collective-permute-start(bf16[2,8,3072]{2,1,0:T(8,128)(2,1)S(1)} %get-tuple-element.71), channel_id=1, source_target_pairs={{0,2},{1,3},{2,0},{3,1},{4,6},{5,7},{6,4},{7,5},{8,10},{9,11},{10,... | collective-permute-start | bytes 294920 | tf_op jit(solution)/shard_map/ppermute | solution.py:33
  65.4 12.1 %collective-permute-start.23 = (bf16[2,8,3072]{2,1,0:T(8,128)(2,1)S(1)}, bf16[2,8,3072]{2,1,0:T(8,128)(2,1)S(1)}, u32[]{:S(2)}, u32[]{:S(2)}) collective-permute-start(bf16[2,8,3072]{2,1,0:T(8,128)(2,1)S(1)} %get-tuple-element.72), channel_id=1, source_target_pairs={{0,4},{1,5},{2,6},{3,7},{4,0},{5,1},{6,2},{7,3},{8,12},{9,13},{10,... | collective-permute-start | bytes 294920 | tf_op jit(solution)/shard_map/ppermute | solution.py:33
  68.7 8.8 %collective-permute-start.24 = (bf16[2,8,3072]{2,1,0:T(8,128)(2,1)S(1)}, bf16[2,8,3072]{2,1,0:T(8,128)(2,1)S(1)}, u32[]{:S(2)}, u32[]{:S(2)}) collective-permute-start(bf16[2,8,3072]{2,1,0:T(8,128)(2,1)S(1)} %get-tuple-element.73), channel_id=1, source_target_pairs={{0,6},{1,7},{2,4},{3,5},{4,2},{5,3},{6,0},{7,1},{8,14},{9,15},{10,... | collective-permute-start | bytes 294920 | tf_op jit(solution)/shard_map/ppermute | solution.py:33

commit v6 on v5

--- a/solution.py
+++ b/solution.py
@@ -14,7 +14,7 @@
 VMEM_LIMIT = 12 * 1024 * 1024
 VMEM_GRAD = 28 * 1024 * 1024
 RING = 24
-GRAD_PARTS = (24, 16, 12, 8, 6, 4, 3, 2, 1)
+GRAD_PARTS = (12, 16, 8, 6, 4, 3, 2, 1)
 
 slope_const = math.sqrt(2.0 / math.pi)
 
@@ -293,7 +293,7 @@
 
     def body(row_ref, col_ref, *refs):
         shard_refs = refs[:count]
-        weights, own, *sends, whole, stage, full, total = refs[count + len(after) :]
+        weights, own, *sends, full, stage, total = refs[count + len(after) :]
         gather_model(lax.axis_index("col"), shard_refs, which, stage, full)
         if spare:
             full[model_blocks] = jnp.zeros((tokens, BLK), BF16)
@@ -305,11 +305,10 @@
         for mask, out in enumerate([own] + sends):
             start = pl.multiple_of((me ^ mask) * piece, piece)
             out[...] = total[pl.ds(0, hidden_blocks), pl.ds(start, piece), :].astype(out.dtype)
-        whole[...] = full[pl.ds(0, model_blocks)]
 
     share = (hidden_blocks, piece, BLK)
     outs = [shape_of(share, F32)] + [shape_of(share, BF16)] * (n_row - 1)
-    outs += [shape_of((model_blocks, tokens, BLK), BF16)]
+    outs += [shape_of((model_blocks + spare, tokens, BLK), BF16)]
     flops, moved = apply_cost(layout, tokens)
     args = [*rows_cols, *shards, *after, pltpu.with_memory_space_constraint(blocks, pltpu.VMEM)]
     own, *sends, whole = call(
@@ -319,7 +318,6 @@
         args,
         scratch=[
             pltpu.VMEM((tokens, width), F32),
-            pltpu.VMEM((model_blocks + spare, tokens, BLK), BF16),
             pltpu.VMEM((hidden_blocks + spare, tokens, BLK), F32),
         ],
         flops=flops,
@@ -340,7 +338,7 @@
     def body(row_ref, col_ref, *refs):
         share_refs, refs = refs[:count], refs[count + len(after) :]
         if grads:
-            other_ref, weights, keep, send, token, grad, full, total, other_full, made, done = refs
+            other_ref, weights, keep, send, token, grad, full, total, made, done = refs
             token[...] = jnp.zeros_like(token)
         else:
             weights, keep, send, full, total = refs
@@ -350,10 +348,6 @@
         if forward or spare:
             total[...] = jnp.zeros_like(total)
         if grads:
-            if spare:
-                other_full[pl.ds(0, model_blocks)] = other_ref[...]
-                other_full[model_blocks] = jnp.zeros((tokens, BLK), BF16)
-                other_ref = other_full
             copies = send_products(layout, row_ref, col_ref, full, other_ref, made, grad, done)
         work = add_forward if forward else functools.partial(add_backward, turned=True)
         work(layout, row_ref, col_ref, 0, layout.groups, full, weights, total)
@@ -371,22 +365,19 @@
 
     pair = (half, piece, model_blocks * BLK)
     outs = [shape_of(pair, F32), shape_of(pair, BF16)]
-    out_specs = [VM] * (4 if grads else 2)
+    whole = shape_of((hidden_blocks + spare, tokens, BLK), BF16)
+    out_specs = [VM] * (4 if grads else 3)
     args = [*rows_cols, *shares, *after]
-    scratch = [
-        pltpu.VMEM((hidden_blocks + spare, tokens, BLK), BF16),
-        pltpu.VMEM((model_blocks + spare, tokens, BLK), F32),
-    ]
+    scratch = [pltpu.VMEM((model_blocks + spare, tokens, BLK), F32)]
     flops, moved = apply_cost(layout, tokens)
     if grads:
         outs += [shape_of((8, BLK), F32), shape_of((layout.capacity, BLK, BLK), F32)]
         out_specs[3] = pl.BlockSpec(memory_space=pltpu.HBM)
         args += [other]
-        scratch += [
-            pltpu.VMEM((model_blocks + spare, tokens, BLK), BF16),
-            *ring_scratch(layout),
-        ]
+        scratch = [pltpu.VMEM(whole.shape, BF16), *scratch, *ring_scratch(layout)]
         flops, moved = 2 * flops, 3 * moved
+    else:
+        outs += [whole]
     args += [pltpu.with_memory_space_constraint(blocks, pltpu.VMEM)]
     return call(
         body,
@@ -422,38 +413,21 @@
     return copies[-slots:]
 
 
-def weight_grad(layout, rows_cols, left, shares):
-    spare = layout.spare
-    count = len(shares)
-    left_blocks, tokens, _ = left.shape
-    hidden_blocks = shares[0].shape[0]
-
-    def body(row_ref, col_ref, left_ref, *refs):
-        share_refs, (grad, sum_ref, made, done, full, *wide) = refs[:count], refs[count:]
-        gather_hidden(lax.axis_index("row"), share_refs, full)
-        if spare:
-            full[hidden_blocks] = jnp.zeros((tokens, BLK), BF16)
-            wide[0][pl.ds(0, left_blocks)] = left_ref[...]
-            wide[0][left_blocks] = jnp.zeros((tokens, BLK), BF16)
-            left_ref = wide[0]
-        copies = send_products(layout, row_ref, col_ref, left_ref, full, made, grad, done)
+def weight_grad(layout, rows_cols, left, right, hidden_blocks):
+    def body(row_ref, col_ref, left_ref, right_ref, grad, sum_ref, made, done):
+        copies = send_products(layout, row_ref, col_ref, left_ref, right_ref, made, grad, done)
         for block in range(hidden_blocks):
-            sum_ref[pl.ds(block, 1), :] = jnp.sum(full[block].astype(F32), axis=0, keepdims=True)
+            sum_ref[pl.ds(block, 1), :] = jnp.sum(right_ref[block].astype(F32), axis=0, keepdims=True)
         for copy in copies:
             copy.wait()
 
-    flops, moved = apply_cost(layout, tokens)
-    out = shape_of((layout.capacity, BLK, BLK), F32)
-    scratch = ring_scratch(layout)
-    scratch += [pltpu.VMEM((hidden_blocks + spare, tokens, BLK), BF16)]
-    if spare:
-        scratch += [pltpu.VMEM((left_blocks + 1, tokens, BLK), BF16)]
+    flops, moved = apply_cost(layout, left.shape[1])
     return call(
         body,
-        [out, shape_of((hidden_blocks, BLK), F32)],
-        [SM, SM, VM] + [VM] * count,
-        [*rows_cols, left, *shares],
-        scratch=scratch,
+        [shape_of((layout.capacity, BLK, BLK), F32), shape_of((hidden_blocks, BLK), F32)],
+        [SM, SM, VM, VM],
+        [*rows_cols, left, right],
+        scratch=ring_scratch(layout),
         out_specs=[pl.BlockSpec(memory_space=pltpu.HBM), VM],
         flops=flops,
         moved=2 * moved,
@@ -577,13 +551,13 @@
         second, second_at, activated_shares, second_held, True, model_blocks, n_col, other=full_cotangent
     )
     out_came = swap(out_send, "col", n_col, 1)
-    in_keep, in_send = hidden_to_model(
+    in_keep, in_send, full_grad = hidden_to_model(
         first, first_at, grad_shares, first_turned, False, model_blocks, n_col, after=(out_done,)
     )
     in_came = swap(in_send, "col", n_col, 1)
     owns, sends = pair_sums((out_keep, out_came), (in_keep, in_came))
-    parts = [swap(send, "col", n_col, 2 * entry) for entry, send in enumerate(sends, 1)]
-    w1_grad, bias_sum = weight_grad(first, first_at, full_tokens, grad_shares)
+    parts = [swap(send, "col", n_col, 2 * entry) for entry, send in sorted(enumerate(sends, 1), key=lambda e: e[0] == 1)]
+    w1_grad, bias_sum = weight_grad(first, first_at, full_tokens, full_grad, hidden_blocks)
     out, tokens_grad = final_sums(owns, parts)
     return (
         out,

time: 78.5 us -> 78.1 us (level)
  no operation moved by 1% of the time
where the time goes in v6:
time: 78.1 us; the launch traced here: 77.8 us
  Pallas kernels  41.6 us (53%)
  starting transfers between devices  26.4 us (34%)
  waiting for transfers between devices  5.08 us (7%)
  local copies, waits for them, and re-layouts  3.75 us (5%)
  between operations  0.87 us (1%)
    pallas_call x18, Pallas kernels, call(): pl.pallas_call(body, out_shape=outs, in_specs=in_specs, out_specs=[whole]...  41.6 us
    ppermute x25, starting transfers between devices, swap(): lax.ppermute(array, axis, [(place, place ^ mask) for place in range(size)])  26.4 us
    ppermute x25, waiting for transfers between devices, swap(): lax.ppermute(array, axis, [(place, place ^ mask) for place in range(size)])  5.08 us
    unnamed x6, local copies, waits for them, and re-layouts  3.75 us
  transfers between devices with their start and end apart: 25, of which 6 were waited for; matrix products, arithmetic and copies ran while one was open for 0% of the time, Pallas kernels for 47%

profile of v6, /device:TPU:0, one launch (start us, length us, event | category | flops | bytes accessed | tf_op | source)
XLA Modules:
  0.0 77.8 jit_solution(4644386128341201778)
XLA Ops:
  0.6 0.8 %shard_map.111.refs_0_ = bf16[2,8,3072]{2,1,0:T(8,128)(2,1)S(1)} custom-call(bf16[8,3072]{1,0:T(8,128)(2,1)} %first_ref.1, bf16[8,3072]{1,0:T(8,128)(2,1)} %second_ref.1), custom_call_target="tpu_custom_call" | custom-call | bytes 196608 | tf_op jit(solution)/shard_map/pallas_call | solution.py:39
  1.5 3.1 %collective-permute-start.1 = (bf16[2,8,3072]{2,1,0:T(8,128)(2,1)S(1)}, bf16[2,8,3072]{2,1,0:T(8,128)(2,1)S(1)}, u32[]{:S(2)}, u32[]{:S(2)}) collective-permute-start(bf16[2,8,3072]{2,1,0:T(8,128)(2,1)S(1)} %shard_map.111.refs_0_), channel_id=1, source_target_pairs={{0,2},{1,3},{2,0},{3,1},{4,6},{5,7},{6,4},{7,5},{8,10},{9,11},{10,... | collective-permute-start | bytes 294920 | tf_op jit(solution)/shard_map/ppermute | solution.py:33
  4.5 2.6 %collective-permute-start.3 = (bf16[2,8,3072]{2,1,0:T(8,128)(2,1)S(1)}, bf16[2,8,3072]{2,1,0:T(8,128)(2,1)S(1)}, u32[]{:S(2)}, u32[]{:S(2)}) collective-permute-start(bf16[2,8,3072]{2,1,0:T(8,128)(2,1)S(1)} %shard_map.111.refs_0_), channel_id=1, source_target_pairs={{0,4},{1,5},{2,6},{3,7},{4,0},{5,1},{6,2},{7,3},{8,12},{9,13},{10,... | collective-permute-start | bytes 294920 | tf_op jit(solution)/shard_map/ppermute | solution.py:33
  7.1 0.0 collective-permute-start.5
  7.1 0.0 collective-permute-start
  7.1 3.7 %shard_map.112 = (bf16[288,128,128]{2,1,0:T(8,128)(2,1)S(1)}, f32[8,128]{1,0:T(8,128)S(1)}) custom-call(bf16[288,128,128]{2,1,0:T(8,128)(2,1)} %bitcast.9), custom_call_target="tpu_custom_call" | custom-call | bytes 18874368 | tf_op jit(solution)/shard_map/pallas_call | solution.py:39
  10.8 3.7 %shard_map.113 = (bf16[288,128,128]{2,1,0:T(8,128)(2,1)S(1)}, f32[8,128]{1,0:T(8,128)S(1)}) custom-call(bf16[288,128,128]{2,1,0:T(8,128)(2,1)} %bitcast.10), custom_call_target="tpu_custom_call" | custom-call | bytes 18874368 | tf_op jit(solution)/shard_map/pallas_call | solution.py:39
  14.5 0.0 collective-permute-done.1.array_ref
  14.6 0.6 collective-permute-start.2
  15.1 0.0 collective-permute-done.3.array_ref
  15.1 0.1 collective-permute-start.4
  15.2 0.0 collective-permute-done.5.array_ref
  15.2 0.5 collective-permute-start.6
  15.8 1.0 %shard_map.110 = (s32[24,128]{1,0:T(8,128)S(1)}, s32[48,128]{1,0:T(8,128)S(1)}) custom-call(s32[24,48]{1,0:T(8,128)} %refs_0_.1, s32[24,48]{1,0:T(8,128)} %bitcast.11), custom_call_target="tpu_custom_call" | custom-call | tf_op jit(solution)/shard_map/pallas_call | solution.py:39
  16.8 0.0 collective-permute-done.refs_1_
  16.8 0.0 collective-permute-done.2.refs_3_
  16.8 0.0 collective-permute-done.4.refs_5_
  16.9 0.0 collective-permute-done.6.refs_7_
  16.9 0.0 copy-start.2
  16.9 3.5 %shard_map.117 = (f32[48,16,128]{2,1,0:T(8,128)S(1)}, bf16[48,16,128]{2,1,0:T(8,128)(2,1)S(1)}, bf16[48,16,128]{2,1,0:T(8,128)(2,1)S(1)}, bf16[48,16,128]{2,1,0:T(8,128)(2,1)S(1)}, bf16[24,64,128]{2,1,0:T(8,128)(2,1)S(1)}) custom-call(s32[24,128]{1,0:T(8,128)S(1)} %get-tuple-element.44.row_ref.col_ref, s32[24,128]{1,0:T(8,128)S(1)} %get-tuple-element.44.row_ref.col_ref, ...), custom_call_target="tpu_custom_call" | custom-call | flops 603979776 | bytes 9437184 | tf_op jit(solution)/shard_map/pallas_call | solution.py:39
  20.3 1.8 %collective-permute-start.7 = (bf16[48,16,128]{2,1,0:T(8,128)(2,1)S(1)}, bf16[48,16,128]{2,1,0:T(8,128)(2,1)S(1)}, u32[]{:S(2)}, u32[]{:S(2)}) collective-permute-start(bf16[48,16,128]{2,1,0:T(8,128)(2,1)S(1)} %get-tuple-element.49), channel_id=1, source_target_pairs={{0,8},{8,0},{16,24},{24,16},{1,9},{9,1},{17,25},{25,17},{2,10},{10... | collective-permute-start | bytes 589832 | tf_op jit(solution)/shard_map/ppermute | solution.py:33
  22.1 1.5 %collective-permute-start.8 = (bf16[48,16,128]{2,1,0:T(8,128)(2,1)S(1)}, bf16[48,16,128]{2,1,0:T(8,128)(2,1)S(1)}, u32[]{:S(2)}, u32[]{:S(2)}) collective-permute-start(bf16[48,16,128]{2,1,0:T(8,128)(2,1)S(1)} %get-tuple-element.50), channel_id=1, source_target_pairs={{0,16},{8,24},{16,0},{24,8},{1,17},{9,25},{17,1},{25,9},{2,18},{10... | collective-permute-start | bytes 589832 | tf_op jit(solution)/shard_map/ppermute | solution.py:33
  23.6 0.3 collective-permute-start.9
  23.9 4.8 %shard_map.119 = (f32[48,16,128]{2,1,0:T(8,128)S(1)}, bf16[48,16,128]{2,1,0:T(8,128)(2,1)S(1)}, bf16[48,16,128]{2,1,0:T(8,128)(2,1)S(1)}, bf16[48,16,128]{2,1,0:T(8,128)(2,1)S(1)}, bf16[24,64,128]{2,1,0:T(8,128)(2,1)S(1)}) custom-call(s32[48,128]{1,0:T(8,128)S(1)} %get-tuple-element.43.row_ref.col_ref, s32[48,128]{1,0:T(8,128)S(1)} %get-tuple-element.43.row_ref.col_ref, ...), custom_call_target="tpu_custom_call" | custom-call | flops 603979776 | bytes 9437184 | tf_op jit(solution)/shard_map/pallas_call | solution.py:39
  28.7 1.8 %collective-permute-start.14 = (bf16[48,16,128]{2,1,0:T(8,128)(2,1)S(1)}, bf16[48,16,128]{2,1,0:T(8,128)(2,1)S(1)}, u32[]{:S(2)}, u32[]{:S(2)}) collective-permute-start(bf16[48,16,128]{2,1,0:T(8,128)(2,1)S(1)} %get-tuple-element.61), channel_id=1, source_target_pairs={{0,8},{8,0},{16,24},{24,16},{1,9},{9,1},{17,25},{25,17},{2,10},{10... | collective-permute-start | bytes 589832 | tf_op jit(solution)/shard_map/ppermute | solution.py:33
  30.5 1.5 %collective-permute-start.15 = (bf16[48,16,128]{2,1,0:T(8,128)(2,1)S(1)}, bf16[48,16,128]{2,1,0:T(8,128)(2,1)S(1)}, u32[]{:S(2)}, u32[]{:S(2)}) collective-permute-start(bf16[48,16,128]{2,1,0:T(8,128)(2,1)S(1)} %get-tuple-element.62), channel_id=1, source_target_pairs={{0,16},{8,24},{16,0},{24,8},{1,17},{9,25},{17,1},{25,9},{2,18},{10... | collective-permute-start | bytes 589832 | tf_op jit(solution)/shard_map/ppermute | solution.py:33
  32.1 0.0 collective-permute-done.7.refs_0_
  32.1 0.2 collective-permute-start.16
  32.3 0.6 collective-permute-done.8.refs_1_
  32.8 0.7 collective-permute-done.9.refs_2_
  33.6 0.4 shard_map.118
  34.0 1.5 %collective-permute-start.12 = (bf16[48,16,128]{2,1,0:T(8,128)(2,1)S(1)}, bf16[48,16,128]{2,1,0:T(8,128)(2,1)S(1)}, u32[]{:S(2)}, u32[]{:S(2)}) collective-permute-start(bf16[48,16,128]{2,1,0:T(8,128)(2,1)S(1)} %get-tuple-element.52.refs_0_), channel_id=1, source_target_pairs={{0,24},{8,16},{16,8},{24,0},{1,25},{9,17},{17,9},{25,1},{2,26},{10... | collective-permute-start | bytes 589832 | tf_op jit(solution)/shard_map/ppermute | solution.py:33
  35.5 1.5 %collective-permute-start.11 = (bf16[48,16,128]{2,1,0:T(8,128)(2,1)S(1)}, bf16[48,16,128]{2,1,0:T(8,128)(2,1)S(1)}, u32[]{:S(2)}, u32[]{:S(2)}) collective-permute-start(bf16[48,16,128]{2,1,0:T(8,128)(2,1)S(1)} %get-tuple-element.52.refs_0_), channel_id=1, source_target_pairs={{0,16},{8,24},{16,0},{24,8},{1,17},{9,25},{17,1},{25,9},{2,18},{10... | collective-permute-start | bytes 589832 | tf_op jit(solution)/shard_map/ppermute | solution.py:33
  36.9 0.0 collective-permute-done.14.refs_0_
  36.9 1.4 %collective-permute-start.10 = (bf16[48,16,128]{2,1,0:T(8,128)(2,1)S(1)}, bf16[48,16,128]{2,1,0:T(8,128)(2,1)S(1)}, u32[]{:S(2)}, u32[]{:S(2)}) collective-permute-start(bf16[48,16,128]{2,1,0:T(8,128)(2,1)S(1)} %get-tuple-element.52.refs_0_), channel_id=1, source_target_pairs={{0,8},{8,0},{16,24},{24,16},{1,9},{9,1},{17,25},{25,17},{2,10},{10... | collective-permute-start | bytes 589832 | tf_op jit(solution)/shard_map/ppermute | solution.py:33
  38.3 2.8 %shard_map.121 = (bf16[288,128,128]{2,1,0:T(8,128)(2,1)S(1)}, f32[8,128]{1,0:T(8,128)S(1)}) custom-call(bf16[288,128,128]{2,1,0:T(8,128)(2,1)S(1)} %get-tuple-element.47.refs_8_.from_ref, f32[48,16,128]{2,1,0:T(8,128)S(1)} %get-tuple-element.59.after_ref.slope_ref), custom_call_target="tpu_custom_call" | custom-call | bytes 9437184 | tf_op jit(solution)/shard_map/pallas_call | solution.py:39
  41.1 0.0 copy-start
  41.1 3.7 %copy-done = bf16[288,128,128]{2,1,0:T(8,128)(2,1)} copy-done((bf16[288,128,128]{2,1,0:T(8,128)(2,1)}, bf16[288,128,128]{2,1,0:T(8,128)(2,1)S(1)}, u32[]{:S(2)}) %copy-start) | copy-done | bytes 9437208
  44.8 1.7 %collective-permute-done.15.refs_1_ = bf16[48,16,128]{2,1,0:T(8,128)(2,1)S(1)} collective-permute-done((bf16[48,16,128]{2,1,0:T(8,128)(2,1)S(1)}, bf16[48,16,128]{2,1,0:T(8,128)(2,1)S(1)}, u32[]{:S(2)}, u32[]{:S(2)}) %collective-permute-start.15) | collective-permute-done | bytes 196640 | tf_op jit(solution)/shard_map/ppermute | solution.py:33
  46.5 0.0 collective-permute-done.16.refs_2_
  46.5 0.1 shard_map.122
  46.6 0.1 collective-permute-start.17
  46.7 1.6 %collective-permute-start.20 = (bf16[48,16,128]{2,1,0:T(8,128)(2,1)S(1)}, bf16[48,16,128]{2,1,0:T(8,128)(2,1)S(1)}, u32[]{:S(2)}, u32[]{:S(2)}) collective-permute-start(bf16[48,16,128]{2,1,0:T(8,128)(2,1)S(1)} %get-tuple-element.64.array_ref.refs_0_), channel_id=1, source_target_pairs={{0,24},{8,16},{16,8},{24,0},{1,25},{9,17},{17,9},{25,1},{2,26},{10... | collective-permute-start | bytes 589832 | tf_op jit(solution)/shard_map/ppermute | solution.py:33
  48.3 0.0 collective-permute-done.17.refs_0_
  48.3 1.4 %collective-permute-start.19 = (bf16[48,16,128]{2,1,0:T(8,128)(2,1)S(1)}, bf16[48,16,128]{2,1,0:T(8,128)(2,1)S(1)}, u32[]{:S(2)}, u32[]{:S(2)}) collective-permute-start(bf16[48,16,128]{2,1,0:T(8,128)(2,1)S(1)} %shard_map.123), channel_id=1, source_target_pairs={{0,16},{8,24},{16,0},{24,8},{1,17},{9,25},{17,1},{25,9},{2,18},{10... | collective-permute-start | bytes 589832 | tf_op jit(solution)/shard_map/ppermute | solution.py:33
  49.7 0.0 collective-permute-done.12.refs_3_
  49.7 0.6 collective-permute-start.18
  50.4 0.0 collective-permute-done.11.refs_2_
  50.4 8.4 %shard_map.120 = (f32[4,8,3072]{2,1,0:T(8,128)S(1)}, bf16[4,8,3072]{2,1,0:T(8,128)(2,1)S(1)}, f32[8,128]{1,0:T(8,128)S(1)}, f32[288,128,128]{2,1,0:T(8,128)}) custom-call(s32[48,128]{1,0:T(8,128)S(1)} %get-tuple-element.43.row_ref.col_ref, s32[48,128]{1,0:T(8,128)S(1)} %get-tuple-element.43.row_ref.col_ref, ...), custom_call_target="tpu_custom_call" | custom-call | flops 1207959552 | bytes 28311552 | tf_op jit(solution)/shard_map/pallas_call | solution.py:39
  58.8 0.1 collective-permute-start.13
  58.9 0.3 collective-permute-done.19.refs_2_
  59.1 0.4 collective-permute-done.18.refs_1_
  59.5 3.2 %shard_map.124 = (f32[4,8,3072]{2,1,0:T(8,128)S(1)}, bf16[4,8,3072]{2,1,0:T(8,128)(2,1)S(1)}, bf16[48,64,128]{2,1,0:T(8,128)(2,1)S(1)}) custom-call(s32[24,128]{1,0:T(8,128)S(1)} %get-tuple-element.44.row_ref.col_ref, s32[24,128]{1,0:T(8,128)S(1)} %get-tuple-element.44.row_ref.col_ref, bf16[48,16,128]{2,1,0:T(8,128)(2,1)S(1)} %get-tuple-element.64.array_ref.refs_0_, ...), custom_call_target="tpu_custom_call" | custom-call | flops 603979776 | bytes 9437184 | tf_op jit(solution)/shard_map/pallas_call | solution.py:39
  62.7 0.1 collective-permute-start.21
  62.8 0.0 collective-permute-done.13.refs_1_
  62.8 1.4 %collective-permute-done.21.refs_3_ = bf16[4,8,3072]{2,1,0:T(8,128)(2,1)S(1)} collective-permute-done((bf16[4,8,3072]{2,1,0:T(8,128)(2,1)S(1)}, bf16[4,8,3072]{2,1,0:T(8,128)(2,1)S(1)}, u32[]{:S(2)}, u32[]{:S(2)}) %collective-permute-start.21) | collective-permute-done | bytes 196640 | tf_op jit(solution)/shard_map/ppermute | solution.py:33
  64.2 0.1 shard_map.125
  64.3 1.9 %collective-permute-start.22 = (bf16[2,8,3072]{2,1,0:T(8,128)(2,1)S(1)}, bf16[2,8,3072]{2,1,0:T(8,128)(2,1)S(1)}, u32[]{:S(2)}, u32[]{:S(2)}) collective-permute-start(bf16[2,8,3072]{2,1,0:T(8,128)(2,1)S(1)} %get-tuple-element.72), channel_id=1, source_target_pairs={{0,4},{1,5},{2,6},{3,7},{4,0},{5,1},{6,2},{7,3},{8,12},{9,13},{10,... | collective-permute-start | bytes 294920 | tf_op jit(solution)/shard_map/ppermute | solution.py:33
  66.2 1.8 %collective-permute-start.23 = (bf16[2,8,3072]{2,1,0:T(8,128)(2,1)S(1)}, bf16[2,8,3072]{2,1,0:T(8,128)(2,1)S(1)}, u32[]{:S(2)}, u32[]{:S(2)}) collective-permute-start(bf16[2,8,3072]{2,1,0:T(8,128)(2,1)S(1)} %get-tuple-element.73), channel_id=1, source_target_pairs={{0,6},{1,7},{2,4},{3,5},{4,2},{5,3},{6,0},{7,1},{8,14},{9,15},{10,... | collective-permute-start | bytes 294920 | tf_op jit(solution)/shard_map/ppermute | solution.py:33
  68.1 0.5 collective-permute-start.24
  68.5 8.5 %shard_map.127 = (f32[288,128,128]{2,1,0:T(8,128)}, f32[48,128]{1,0:T(8,128)}) custom-call(s32[24,128]{1,0:T(8,128)S(1)} %get-tuple-element.44.row_ref.col_ref, s32[24,128]{1,0:T(8,128)S(1)} %get-tuple-element.44.row_ref.col_ref, bf16[24,64,128]{2,1,0:T(8,128)(2,1)S(1)} %get-tuple-element.53.refs_8_.left_ref, ...), custom_call_target="tpu_custom_call" | custom-call | flops 603979776 | bytes 18874368 | tf_op jit(solution)/shard_map/pallas_call | solution.py:39
  77.1 0.0 collective-permute-done.23.refs_3_
  77.1 0.0 collective-permute-done.24.refs_4_
  77.1 0.7 shard_map.126
  (11 shorter events, 0.1 us)
Async XLA Ops:
  1.5 13.1 %collective-permute-start.1 = (bf16[2,8,3072]{2,1,0:T(8,128)(2,1)S(1)}, bf16[2,8,3072]{2,1,0:T(8,128)(2,1)S(1)}, u32[]{:S(2)}, u32[]{:S(2)}) collective-permute-start(bf16[2,8,3072]{2,1,0:T(8,128)(2,1)S(1)} %shard_map.111.refs_0_), channel_id=1, source_target_pairs={{0,2},{1,3},{2,0},{3,1},{4,6},{5,7},{6,4},{7,5},{8,10},{9,11},{10,... | collective-permute-start | bytes 294920 | tf_op jit(solution)/shard_map/ppermute | solution.py:33
  4.5 10.6 %collective-permute-start.3 = (bf16[2,8,3072]{2,1,0:T(8,128)(2,1)S(1)}, bf16[2,8,3072]{2,1,0:T(8,128)(2,1)S(1)}, u32[]{:S(2)}, u32[]{:S(2)}) collective-permute-start(bf16[2,8,3072]{2,1,0:T(8,128)(2,1)S(1)} %shard_map.111.refs_0_), channel_id=1, source_target_pairs={{0,4},{1,5},{2,6},{3,7},{4,0},{5,1},{6,2},{7,3},{8,12},{9,13},{10,... | collective-permute-start | bytes 294920 | tf_op jit(solution)/shard_map/ppermute | solution.py:33
  7.1 8.1 %collective-permute-start.5 = (bf16[2,8,3072]{2,1,0:T(8,128)(2,1)S(1)}, bf16[2,8,3072]{2,1,0:T(8,128)(2,1)S(1)}, u32[]{:S(2)}, u32[]{:S(2)}) collective-permute-start(bf16[2,8,3072]{2,1,0:T(8,128)(2,1)S(1)} %shard_map.111.refs_0_), channel_id=1, source_target_pairs={{0,6},{1,7},{2,4},{3,5},{4,2},{5,3},{6,0},{7,1},{8,14},{9,15},{10,... | collective-permute-start | bytes 294920 | tf_op jit(solution)/shard_map/ppermute | solution.py:33
  7.1 9.7 %collective-permute-start = (bf16[2,8,3072]{2,1,0:T(8,128)(2,1)S(1)}, bf16[2,8,3072]{2,1,0:T(8,128)(2,1)S(1)}, u32[]{:S(2)}, u32[]{:S(2)}) collective-permute-start(bf16[2,8,3072]{2,1,0:T(8,128)(2,1)S(1)} %shard_map.111.refs_0_), channel_id=1, source_target_pairs={{0,1},{1,0},{2,3},{3,2},{4,5},{5,4},{6,7},{7,6},{8,9},{9,8},{10,11... | collective-permute-start | bytes 294920 | tf_op jit(solution)/shard_map/ppermute | solution.py:33
  14.6 2.3 %collective-permute-start.2 = (bf16[2,8,3072]{2,1,0:T(8,128)(2,1)S(1)}, bf16[2,8,3072]{2,1,0:T(8,128)(2,1)S(1)}, u32[]{:S(2)}, u32[]{:S(2)}) collective-permute-start(bf16[2,8,3072]{2,1,0:T(8,128)(2,1)S(1)} %shard_map.114.refs_2_), channel_id=1, source_target_pairs={{0,1},{1,0},{2,3},{3,2},{4,5},{5,4},{6,7},{7,6},{8,9},{9,8},{10,11... | collective-permute-start | bytes 294920 | tf_op jit(solution)/shard_map/ppermute | solution.py:33
  15.1 1.7 %collective-permute-start.4 = (bf16[2,8,3072]{2,1,0:T(8,128)(2,1)S(1)}, bf16[2,8,3072]{2,1,0:T(8,128)(2,1)S(1)}, u32[]{:S(2)}, u32[]{:S(2)}) collective-permute-start(bf16[2,8,3072]{2,1,0:T(8,128)(2,1)S(1)} %shard_map.115.refs_4_), channel_id=1, source_target_pairs={{0,1},{1,0},{2,3},{3,2},{4,5},{5,4},{6,7},{7,6},{8,9},{9,8},{10,11... | collective-permute-start | bytes 294920 | tf_op jit(solution)/shard_map/ppermute | solution.py:33
  15.2 1.6 %collective-permute-start.6 = (bf16[2,8,3072]{2,1,0:T(8,128)(2,1)S(1)}, bf16[2,8,3072]{2,1,0:T(8,128)(2,1)S(1)}, u32[]{:S(2)}, u32[]{:S(2)}) collective-permute-start(bf16[2,8,3072]{2,1,0:T(8,128)(2,1)S(1)} %shard_map.116.refs_6_), channel_id=1, source_target_pairs={{0,1},{1,0},{2,3},{3,2},{4,5},{5,4},{6,7},{7,6},{8,9},{9,8},{10,11... | collective-permute-start | bytes 294920 | tf_op jit(solution)/shard_map/ppermute | solution.py:33
  16.9 15.4 %copy-start.2 = (bf16[6144]{0:T(1024)(128)(2,1)S(1)}, bf16[6144]{0:T(1024)(128)(2,1)}, u32[]{:S(2)}) copy-start(bf16[6144]{0:T(1024)(128)(2,1)} %param.11) | copy-start | bytes 36868
  20.3 11.7 %collective-permute-start.7 = (bf16[48,16,128]{2,1,0:T(8,128)(2,1)S(1)}, bf16[48,16,128]{2,1,0:T(8,128)(2,1)S(1)}, u32[]{:S(2)}, u32[]{:S(2)}) collective-permute-start(bf16[48,16,128]{2,1,0:T(8,128)(2,1)S(1)} %get-tuple-element.49), channel_id=1, source_target_pairs={{0,8},{8,0},{16,24},{24,16},{1,9},{9,1},{17,25},{25,17},{2,10},{10... | collective-permute-start | bytes 589832 | tf_op jit(solution)/shard_map/ppermute | solution.py:33
  22.1 10.7 %collective-permute-start.8 = (bf16[48,16,128]{2,1,0:T(8,128)(2,1)S(1)}, bf16[48,16,128]{2,1,0:T(8,128)(2,1)S(1)}, u32[]{:S(2)}, u32[]{:S(2)}) collective-permute-start(bf16[48,16,128]{2,1,0:T(8,128)(2,1)S(1)} %get-tuple-element.50), channel_id=1, source_target_pairs={{0,16},{8,24},{16,0},{24,8},{1,17},{9,25},{17,1},{25,9},{2,18},{10... | collective-permute-start | bytes 589832 | tf_op jit(solution)/shard_map/ppermute | solution.py:33
  23.6 9.9 %collective-permute-start.9 = (bf16[48,16,128]{2,1,0:T(8,128)(2,1)S(1)}, bf16[48,16,128]{2,1,0:T(8,128)(2,1)S(1)}, u32[]{:S(2)}, u32[]{:S(2)}) collective-permute-start(bf16[48,16,128]{2,1,0:T(8,128)(2,1)S(1)} %get-tuple-element.51), channel_id=1, source_target_pairs={{0,24},{8,16},{16,8},{24,0},{1,25},{9,17},{17,9},{25,1},{2,26},{10... | collective-permute-start | bytes 589832 | tf_op jit(solution)/shard_map/ppermute | solution.py:33
  28.7 8.2 %collective-permute-start.14 = (bf16[48,16,128]{2,1,0:T(8,128)(2,1)S(1)}, bf16[48,16,128]{2,1,0:T(8,128)(2,1)S(1)}, u32[]{:S(2)}, u32[]{:S(2)}) collective-permute-start(bf16[48,16,128]{2,1,0:T(8,128)(2,1)S(1)} %get-tuple-element.61), channel_id=1, source_target_pairs={{0,8},{8,0},{16,24},{24,16},{1,9},{9,1},{17,25},{25,17},{2,10},{10... | collective-permute-start | bytes 589832 | tf_op jit(solution)/shard_map/ppermute | solution.py:33
  30.5 16.0 %collective-permute-start.15 = (bf16[48,16,128]{2,1,0:T(8,128)(2,1)S(1)}, bf16[48,16,128]{2,1,0:T(8,128)(2,1)S(1)}, u32[]{:S(2)}, u32[]{:S(2)}) collective-permute-start(bf16[48,16,128]{2,1,0:T(8,128)(2,1)S(1)} %get-tuple-element.62), channel_id=1, source_target_pairs={{0,16},{8,24},{16,0},{24,8},{1,17},{9,25},{17,1},{25,9},{2,18},{10... | collective-permute-start | bytes 589832 | tf_op jit(solution)/shard_map/ppermute | solution.py:33
  32.1 14.5 %collective-permute-start.16 = (bf16[48,16,128]{2,1,0:T(8,128)(2,1)S(1)}, bf16[48,16,128]{2,1,0:T(8,128)(2,1)S(1)}, u32[]{:S(2)}, u32[]{:S(2)}) collective-permute-start(bf16[48,16,128]{2,1,0:T(8,128)(2,1)S(1)} %get-tuple-element.63), channel_id=1, source_target_pairs={{0,24},{8,16},{16,8},{24,0},{1,25},{9,17},{17,9},{25,1},{2,26},{10... | collective-permute-start | bytes 589832 | tf_op jit(solution)/shard_map/ppermute | solution.py:33
  34.0 15.8 %collective-permute-start.12 = (bf16[48,16,128]{2,1,0:T(8,128)(2,1)S(1)}, bf16[48,16,128]{2,1,0:T(8,128)(2,1)S(1)}, u32[]{:S(2)}, u32[]{:S(2)}) collective-permute-start(bf16[48,16,128]{2,1,0:T(8,128)(2,1)S(1)} %get-tuple-element.52.refs_0_), channel_id=1, source_target_pairs={{0,24},{8,16},{16,8},{24,0},{1,25},{9,17},{17,9},{25,1},{2,26},{10... | collective-permute-start | bytes 589832 | tf_op jit(solution)/shard_map/ppermute | solution.py:33
  35.5 14.9 %collective-permute-start.11 = (bf16[48,16,128]{2,1,0:T(8,128)(2,1)S(1)}, bf16[48,16,128]{2,1,0:T(8,128)(2,1)S(1)}, u32[]{:S(2)}, u32[]{:S(2)}) collective-permute-start(bf16[48,16,128]{2,1,0:T(8,128)(2,1)S(1)} %get-tuple-element.52.refs_0_), channel_id=1, source_target_pairs={{0,16},{8,24},{16,0},{24,8},{1,17},{9,25},{17,1},{25,9},{2,18},{10... | collective-permute-start | bytes 589832 | tf_op jit(solution)/shard_map/ppermute | solution.py:33
  36.9 13.4 %collective-permute-start.10 = (bf16[48,16,128]{2,1,0:T(8,128)(2,1)S(1)}, bf16[48,16,128]{2,1,0:T(8,128)(2,1)S(1)}, u32[]{:S(2)}, u32[]{:S(2)}) collective-permute-start(bf16[48,16,128]{2,1,0:T(8,128)(2,1)S(1)} %get-tuple-element.52.refs_0_), channel_id=1, source_target_pairs={{0,8},{8,0},{16,24},{24,16},{1,9},{9,1},{17,25},{25,17},{2,10},{10... | collective-permute-start | bytes 589832 | tf_op jit(solution)/shard_map/ppermute | solution.py:33
  41.1 3.7 %copy-start = (bf16[288,128,128]{2,1,0:T(8,128)(2,1)}, bf16[288,128,128]{2,1,0:T(8,128)(2,1)S(1)}, u32[]{:S(2)}) copy-start(bf16[288,128,128]{2,1,0:T(8,128)(2,1)S(1)} %get-tuple-element.67.refs_5_) | copy-start | bytes 28311556
  46.5 13.0 %copy-start.1 = (bf16[288,128,128]{2,1,0:T(8,128)(2,1)S(1)}, bf16[288,128,128]{2,1,0:T(8,128)(2,1)}, u32[]{:S(2)}) copy-start(bf16[288,128,128]{2,1,0:T(8,128)(2,1)} %copy-done) | copy-start | bytes 28311556
  46.6 1.7 %collective-permute-start.17 = (f32[8,128]{1,0:T(8,128)S(1)}, f32[8,128]{1,0:T(8,128)S(1)}, u32[]{:S(2)}, u32[]{:S(2)}) collective-permute-start(f32[8,128]{1,0:T(8,128)S(1)} %get-tuple-element.65), channel_id=1, source_target_pairs={{0,1},{1,0},{2,3},{3,2},{4,5},{5,4},{6,7},{7,6},{8,9},{9,8},{10,11... | collective-permute-start | bytes 12296 | tf_op jit(solution)/shard_map/ppermute | solution.py:33
  46.7 12.2 %collective-permute-start.20 = (bf16[48,16,128]{2,1,0:T(8,128)(2,1)S(1)}, bf16[48,16,128]{2,1,0:T(8,128)(2,1)S(1)}, u32[]{:S(2)}, u32[]{:S(2)}) collective-permute-start(bf16[48,16,128]{2,1,0:T(8,128)(2,1)S(1)} %get-tuple-element.64.array_ref.refs_0_), channel_id=1, source_target_pairs={{0,24},{8,16},{16,8},{24,0},{1,25},{9,17},{17,9},{25,1},{2,26},{10... | collective-permute-start | bytes 589832 | tf_op jit(solution)/shard_map/ppermute | solution.py:33
  48.3 10.8 %collective-permute-start.19 = (bf16[48,16,128]{2,1,0:T(8,128)(2,1)S(1)}, bf16[48,16,128]{2,1,0:T(8,128)(2,1)S(1)}, u32[]{:S(2)}, u32[]{:S(2)}) collective-permute-start(bf16[48,16,128]{2,1,0:T(8,128)(2,1)S(1)} %shard_map.123), channel_id=1, source_target_pairs={{0,16},{8,24},{16,0},{24,8},{1,17},{9,25},{17,1},{25,9},{2,18},{10... | collective-permute-start | bytes 589832 | tf_op jit(solution)/shard_map/ppermute | solution.py:33
  49.7 9.8 %collective-permute-start.18 = (bf16[48,16,128]{2,1,0:T(8,128)(2,1)S(1)}, bf16[48,16,128]{2,1,0:T(8,128)(2,1)S(1)}, u32[]{:S(2)}, u32[]{:S(2)}) collective-permute-start(bf16[48,16,128]{2,1,0:T(8,128)(2,1)S(1)} %shard_map.123), channel_id=1, source_target_pairs={{0,8},{8,0},{16,24},{24,16},{1,9},{9,1},{17,25},{25,17},{2,10},{10... | collective-permute-start | bytes 589832 | tf_op jit(solution)/shard_map/ppermute | solution.py:33
  58.8 4.0 %collective-permute-start.13 = (bf16[4,8,3072]{2,1,0:T(8,128)(2,1)S(1)}, bf16[4,8,3072]{2,1,0:T(8,128)(2,1)S(1)}, u32[]{:S(2)}, u32[]{:S(2)}) collective-permute-start(bf16[4,8,3072]{2,1,0:T(8,128)(2,1)S(1)} %get-tuple-element.57), channel_id=1, source_target_pairs={{0,1},{1,0},{2,3},{3,2},{4,5},{5,4},{6,7},{7,6},{8,9},{9,8},{10,11... | collective-permute-start | bytes 589832 | tf_op jit(solution)/shard_map/ppermute | solution.py:33
  62.7 1.5 %collective-permute-start.21 = (bf16[4,8,3072]{2,1,0:T(8,128)(2,1)S(1)}, bf16[4,8,3072]{2,1,0:T(8,128)(2,1)S(1)}, u32[]{:S(2)}, u32[]{:S(2)}) collective-permute-start(bf16[4,8,3072]{2,1,0:T(8,128)(2,1)S(1)} %get-tuple-element.69), channel_id=1, source_target_pairs={{0,1},{1,0},{2,3},{3,2},{4,5},{5,4},{6,7},{7,6},{8,9},{9,8},{10,11... | collective-permute-start | bytes 589832 | tf_op jit(solution)/shard_map/ppermute | solution.py:33
  64.3 12.7 %collective-permute-start.22 = (bf16[2,8,3072]{2,1,0:T(8,128)(2,1)S(1)}, bf16[2,8,3072]{2,1,0:T(8,128)(2,1)S(1)}, u32[]{:S(2)}, u32[]{:S(2)}) collective-permute-start(bf16[2,8,3072]{2,1,0:T(8,128)(2,1)S(1)} %get-tuple-element.72), channel_id=1, source_target_pairs={{0,4},{1,5},{2,6},{3,7},{4,0},{5,1},{6,2},{7,3},{8,12},{9,13},{10,... | collective-permute-start | bytes 294920 | tf_op jit(solution)/shard_map/ppermute | solution.py:33
  66.2 10.8 %collective-permute-start.23 = (bf16[2,8,3072]{2,1,0:T(8,128)(2,1)S(1)}, bf16[2,8,3072]{2,1,0:T(8,128)(2,1)S(1)}, u32[]{:S(2)}, u32[]{:S(2)}) collective-permute-start(bf16[2,8,3072]{2,1,0:T(8,128)(2,1)S(1)} %get-tuple-element.73), channel_id=1, source_target_pairs={{0,6},{1,7},{2,4},{3,5},{4,2},{5,3},{6,0},{7,1},{8,14},{9,15},{10,... | collective-permute-start | bytes 294920 | tf_op jit(solution)/shard_map/ppermute | solution.py:33
  68.1 9.0 %collective-permute-start.24 = (bf16[2,8,3072]{2,1,0:T(8,128)(2,1)S(1)}, bf16[2,8,3072]{2,1,0:T(8,128)(2,1)S(1)}, u32[]{:S(2)}, u32[]{:S(2)}) collective-permute-start(bf16[2,8,3072]{2,1,0:T(8,128)(2,1)S(1)} %get-tuple-element.74), channel_id=1, source_target_pairs={{0,2},{1,3},{2,0},{3,1},{4,6},{5,7},{6,4},{7,5},{8,10},{9,11},{10,... | collective-permute-start | bytes 294920 | tf_op jit(solution)/shard_map/ppermute | solution.py:33
